TPU v7x, 32 devices: a whole 2x2x4 slice. The times are simulated.
32 devices in a mesh: space: 8 (over y, x, core), chan: 4 (over z).
Axes of the slice: x: 2, y: 2, z: 4, core: 2. Of those that a mesh axis runs over, the one named last changes fastest.
Arguments:
- inputs: bfloat16 [128, 32, 32, 128], P('chan', 'space'), may hold values from -6 to 6
- filters: bfloat16 [27, 128, 128], P(None, 'chan'), may hold values from -0.109375 to 0.109375
- cotangent: bfloat16 [128, 32, 32, 128], P('chan', 'space'), may hold values from -6 to 6
Outputs:
- grad_inputs: bfloat16 [128, 32, 32, 128], P('chan', 'space')
- grad_filters: float32 [27, 128, 128], P(None, 'chan')
All inputs are finite; a program needn't handle non-finite values.
Results may differ from a plain program's by a relative error of at most 0.0049.
Values may be sent and summed in bfloat16 or wider, within the bound.
No kernel may reach another device: no remote copies, remote signals or barrier semaphores. Data moves between devices by JAX's collectives and lax.ppermute only.
A program may use at most 128 MiB of HBM per device.

v0:
```python
import math

import jax
import jax.numpy as jnp
from jax import lax
from jax.sharding import PartitionSpec as P


def with_halo(block, sides, width):
    for axis, dim in sides:
        count = lax.axis_size(axis)
        forward = [(i, i + 1) for i in range(count - 1)]
        backward = [(target, source) for source, target in forward]
        low = lax.ppermute(
            lax.slice_in_dim(block, block.shape[dim] - width, None, axis=dim), axis, forward
        )
        high = lax.ppermute(lax.slice_in_dim(block, 0, width, axis=dim), axis, backward)
        block = jnp.concatenate([low, block, high], axis=dim)
    return block


def shifted(padded, depth_off, row_off, column_off, plane_count, row_count, column_count):
    return padded[
        :,
        depth_off : depth_off + plane_count,
        row_off : row_off + row_count,
        column_off : column_off + column_count,
    ]


def forward_part(padded, weights, plane_count, row_count, column_count):
    total = None
    for depth_off in range(3):
        stacked = jnp.concatenate(
            [
                shifted(
                    padded, depth_off, inner // 3, inner % 3, plane_count, row_count, column_count
                )
                for inner in range(9)
            ],
            axis=0,
        )
        block = weights[9 * depth_off : 9 * depth_off + 9].reshape(
            9 * weights.shape[1], weights.shape[2]
        )
        term = jnp.einsum("io,idhw->odhw", block, stacked, preferred_element_type=jnp.float32)
        total = term if total is None else total + term
    return total


def body(inputs, filters, cotangent):
    plane_count = inputs.shape[1]
    row_count = inputs.shape[2]
    column_count = inputs.shape[3]
    in_rim = with_halo(inputs, (("space", 1),), 1)
    in_pad = jnp.pad(in_rim, ((0, 0), (0, 0), (1, 1), (1, 1)))
    partial_sum = forward_part(in_pad, filters, plane_count, row_count, column_count)
    pre_act = lax.psum_scatter(partial_sum, "chan", scatter_dimension=0, tiled=True)
    sigma = jax.nn.sigmoid(pre_act)
    grad_out = (cotangent.astype(jnp.float32) * sigma * (1.0 + pre_act * (1.0 - sigma))).astype(
        jnp.bfloat16
    )
    grad_all = lax.all_gather(grad_out, "chan", axis=0, tiled=True)
    grad_rim = with_halo(grad_all, (("space", 1),), 1)
    grad_pad = jnp.pad(grad_rim, ((0, 0), (0, 0), (1, 1), (1, 1)))
    grad_in = None
    for offset in range(27):
        depth_off = offset // 9
        row_off = offset // 3 % 3
        column_off = offset % 3
        window = shifted(
            grad_pad,
            2 - depth_off,
            2 - row_off,
            2 - column_off,
            plane_count,
            row_count,
            column_count,
        )
        term = jnp.einsum(
            "io,odhw->idhw", filters[offset], window, preferred_element_type=jnp.float32
        )
        grad_in = term if grad_in is None else grad_in + term
    stacked_in = jnp.stack(
        [
            shifted(
                in_pad,
                offset // 9,
                offset // 3 % 3,
                offset % 3,
                plane_count,
                row_count,
                column_count,
            )
            for offset in range(27)
        ]
    )
    grad_w = jnp.einsum("kidhw,odhw->kio", stacked_in, grad_all, preferred_element_type=jnp.float32)
    grad_w = lax.psum(grad_w, "space")
    cell_total = plane_count * lax.axis_size("space") * row_count * column_count
    return (grad_in.astype(jnp.bfloat16), grad_w * (1.0 / math.sqrt(cell_total)))


def solution(mesh):
    placed = (P("chan", "space", None, None), P(None, "chan", None), P("chan", "space", None, None))
    return jax.shard_map(
        body,
        mesh=mesh,
        in_specs=placed,
        out_specs=(P("chan", "space", None, None), P(None, "chan", None)),
        check_vma=False,
    )
```

profile of v0, /device:TPU:0, one launch (start us, length us, event | category | flops | bytes accessed | tf_op | source)
XLA Modules:
  0.0 501.5 jit_solution(2108430833571555232)
XLA Ops:
  7.2 1.9 copy.42
  10.5 3.0 collective-permute-start
  14.7 2.1 select_maximum_fusion.2
  27.7 3.6 copy-done.7
  31.3 2.9 copy-done.8
  34.1 9.1 %fusion.136 = f32[4,32,128,128]{3,2,1,0:T(8,128)S(1)} fusion(bf16[288,4,32,128]{3,0,2,1:T(8,128)(2,1)} %copy-done.8, bf16[288,128,1,1]{1,0,3,2:T(8,128)(2,1)S(1)} %bitcast.324), kind=kOutput, calls=%fused_computation.213 | convolution fusion | flops 1207959552 | bytes 17899520 | tf_op jit(solution)/shard_map/io,idhw->odhw/dot_general | solution.py:46
  43.3 10.6 %fusion.137 = f32[4,32,128,128]{3,2,1,0:T(8,128)} fusion(bf16[288,4,32,128]{3,0,2,1:T(8,128)(2,1)} %copy-done.7, bf16[288,128,1,1]{1,0,3,2:T(8,128)(2,1)S(1)} %bitcast.323), kind=kOutput, calls=%fused_computation.214 | convolution fusion | flops 1207959552 | bytes 17899520 | tf_op jit(solution)/shard_map/io,idhw->odhw/dot_general | solution.py:46
  53.9 13.5 %add_bitcast_fusion = f32[128,4,32,128]{0,3,2,1:T(8,128)} fusion(f32[4,32,128,128]{3,2,1,0:T(8,128)S(1)} %fusion.136, f32[4,32,128,128]{3,2,1,0:T(8,128)} %fusion.137, bf16[288,4,32,128]{3,0,2,1:T(8,128)(2,1)} %copy-done.6, bf16[288,128,1,1]{1,0,3,2:T(8,128)(2,1)S(1)} %bitcast.322), kind=kOutput, calls=%fused_computation.16 | convolution fusion | flops 1212153856 | bytes 34676736 | tf_op jit(solution)/shard_map/io,idhw->odhw/dot_general | solution.py:46
  67.4 10.3 %copy.48 = f32[128,4,32,128]{3,2,1,0:T(8,128)} copy(f32[128,4,32,128]{0,3,2,1:T(8,128)} %add_bitcast_fusion) | data formatting | bytes 16777216 | tf_op jit(solution)/shard_map/add | solution.py:47
  81.7 148.3 %reduce-scatter.2.cloned.1.call-done = f32[32,4,32,128]{3,2,1,0:T(8,128)} async-done(((f32[128,4,32,128]{3,2,1,0:T(8,128)}), f32[32,4,32,128]{3,2,1,0:T(8,128)}) %reduce-scatter.2.cloned.1.call-update) | async-done | bytes 2097168 | tf_op jit(solution)/shard_map/reduce_scatter | solution.py:58
  230.0 3.7 multiply_convert_fusion
  235.2 2.3 bitcast_dynamic-update-slice_fusion.22
  248.1 1.7 bitcast_dynamic-update-slice_fusion.13
  266.9 48.5 %all-gather.2.cloned.1.call-done = bf16[128,4,32,128]{3,2,1,0:T(8,128)(2,1)} async-done(((bf16[32,4,32,128]{3,2,1,0:T(8,128)(2,1)}), bf16[128,4,32,128]{3,2,1,0:T(8,128)(2,1)}) %all-gather.2.cloned.1.call-update) | async-done | bytes 4194320 | tf_op jit(solution)/shard_map/all_gather | solution.py:63
  315.3 5.0 %copy.49 = bf16[128,4,32,128]{3,0,2,1:T(8,128)(2,1)S(1)} copy(bf16[128,4,32,128]{3,2,1,0:T(8,128)(2,1)} %all-gather.2.cloned.1.call-done) | data formatting | bytes 8388608 | tf_op jit(solution)/shard_map/all_gather | solution.py:63
  320.4 2.0 copy-done.1
  325.1 4.4 collective-permute-start.2
  329.5 13.8 %fusion.70 = f32[27,32,128]{2,1,0:T(8,128)} fusion(bf16[27,32,4,32,128]{4,1,3,2,0:T(8,128)(2,1)} %bitcast_dynamic-update-slice_fusion, bf16[128,4,32,128,1]{3,2,1,0,4:T(8,128)(2,1)S(1)} %bitcast.321), kind=kOutput, calls=%fused_computation.94 | convolution fusion | flops 3623878656 | bytes 32948224 | tf_op jit(solution)/shard_map/kidhw,odhw->kio/dot_general | solution.py:98
  343.4 4.8 fusion.88
  348.2 48.0 %all-reduce.4.cloned.1.call-done = f32[27,32,128]{2,1,0:T(8,128)} async-done(((f32[27,32,128]{2,1,0:T(8,128)}), f32[27,32,128]{2,1,0:T(8,128)}) %all-reduce.4.cloned.1.call-update) | async-done | bytes 442384 | tf_op jit(solution)/shard_map/psum | solution.py:99
  396.2 1.8 broadcast_multiply_fusion
  398.0 10.0 %select_maximum_fusion = bf16[128,6,34,130]{3,0,2,1:T(8,128)(2,1)S(1)} fusion(bf16[128,1,32,128]{3,0,2,1:T(8,128)(2,1)S(1)} %collective-permute-done.3, bf16[128,4,32,128]{3,0,2,1:T(8,128)(2,1)} %copy-done.1, bf16[128,1,32,128]{3,0,2,1:T(8,128)(2,1)} %collective-permute-done.2), kind=kLoop, calls=%fused_computation.7 | loop fusion | flops 64496640 | bytes 13080576 | tf_op jit(solution)/shard_map/concatenate | solution.py:18
  408.1 3.4 fusion.11
  411.5 2.9 fusion.13
  414.3 2.0 fusion.15
  416.3 2.9 fusion.19
  419.2 2.0 fusion.21
  421.3 2.9 fusion.23
  424.2 2.9 fusion.25
  427.1 2.1 fusion.27
  429.2 2.9 fusion.29
  432.1 3.1 fusion.31
  435.1 2.0 fusion.33
  437.1 2.9 fusion.35
  440.0 2.0 fusion.37
  442.0 2.9 fusion.39
  444.9 2.9 fusion.41
  447.7 2.0 fusion.43
  449.7 2.8 fusion.45
  452.5 2.8 fusion.47
  455.4 2.0 fusion.49
  457.4 2.9 fusion.53
  460.3 2.2 fusion.55
  462.5 2.9 fusion.59
  465.4 2.9 fusion.57
  468.3 3.2 fusion.17
  471.5 2.0 fusion.51
  473.5 19.6 %fusion.67 = bf16[32,4,32,128]{3,0,2,1:T(8,128)(2,1)S(1)} fusion(f32[4,32,128,32]{2,3,1,0:T(8,128)} %fusion.11, f32[4,32,128,32]{2,3,1,0:T(8,128)} %fusion.13, f32[4,32,128,32]{2,3,1,0:T(8,128)} %fusion.15, f32[4,32,128,32]{2,3,1,0:T(8,128)} %fusion.17, f32[4,32,128,32]{2,3,1,0:T(8,128)} %fusion.19, f32[4,32,128,32]{2,3,1,0:T(8,128)} %fusion.21, ...), kind=kOutput, calls=%fused_computation.83 | convolution fusion | flops 148373504 | bytes 59777024 | tf_op jit(solution)/shard_map/io,odhw->idhw/dot_general | solution.py:80
  (77 shorter events, 50.6 us)
Async XLA Ops:
  7.2 222.9 %reduce-scatter.2.cloned.1.call-start = ((), (), s32[]{:S(2)}) async-start(), calls=%async_computation.1 | async-start | bytes 10485760 | tf_op jit(solution)/shard_map/reduce_scatter | solution.py:58
  9.1 12.0 %copy-start.3 = (bf16[32,4,32,128]{3,0,2,1:T(8,128)(2,1)}, bf16[32,4,32,128]{3,0,2,1:T(8,128)(2,1)S(1)}, u32[]{:S(2)}) copy-start(bf16[32,4,32,128]{3,0,2,1:T(8,128)(2,1)S(1)} %copy.42) | copy-start | bytes 3145732
  9.2 5.3 %collective-permute-start.1 = (bf16[32,1,32,128]{3,0,2,1:T(8,128)(2,1)S(1)}, bf16[32,1,32,128]{3,0,2,1:T(8,128)(2,1)S(1)}, u32[]{:S(2)}, u32[]{:S(2)}) collective-permute-start(bf16[32,1,32,128]{3,0,2,1:T(8,128)(2,1)S(1)} %get-tuple-element.35), channel_id=1, source_target_pairs={{4,0},{8,4},{12,8},{16,12},{20,16},{24,20},{28,24},{5,1},{9,5},{13... | collective-permute-start | bytes 786440 | tf_op jit(solution)/shard_map/ppermute | solution.py:17
  10.5 4.2 collective-permute-start
  14.5 6.6 %copy-start.11 = (bf16[32,1,32,128]{3,0,2,1:T(8,128)(2,1)}, bf16[32,1,32,128]{3,0,2,1:T(8,128)(2,1)S(1)}, u32[]{:S(2)}) copy-start(bf16[32,1,32,128]{3,0,2,1:T(8,128)(2,1)S(1)} %collective-permute-done.1) | copy-start | bytes 786436
  14.7 6.5 %copy-start.13 = (bf16[32,1,32,128]{3,0,2,1:T(8,128)(2,1)}, bf16[32,1,32,128]{3,0,2,1:T(8,128)(2,1)S(1)}, u32[]{:S(2)}) copy-start(bf16[32,1,32,128]{3,0,2,1:T(8,128)(2,1)S(1)} %collective-permute-done) | copy-start | bytes 786436
  18.8 2.3 copy-start.9
  27.6 3.6 copy-start.7
  27.7 6.5 %copy-start.8 = (bf16[288,4,32,128]{3,0,2,1:T(8,128)(2,1)}, bf16[288,4,32,128]{3,0,2,1:T(8,128)(2,1)S(1)}, u32[]{:S(2)}) copy-start(bf16[288,4,32,128]{3,0,2,1:T(8,128)(2,1)S(1)} %get-tuple-element.10) | copy-start | bytes 28311556
  27.7 15.6 %copy-start.6 = (bf16[288,4,32,128]{3,0,2,1:T(8,128)(2,1)}, bf16[288,4,32,128]{3,0,2,1:T(8,128)(2,1)S(1)}, u32[]{:S(2)}) copy-start(bf16[288,4,32,128]{3,0,2,1:T(8,128)(2,1)S(1)} %get-tuple-element.8) | copy-start | bytes 28311556
  77.7 237.6 %all-gather.2.cloned.1.call-start = ((), (), s32[]{:S(2)}) async-start(), calls=%async_computation.2 | async-start | bytes 5242880 | tf_op jit(solution)/shard_map/all_gather | solution.py:63
  233.7 162.5 %all-reduce.4.cloned.1.call-start = ((), (), s32[]{:S(2)}) async-start(), calls=%async_computation.3 | async-start | bytes 884736 | tf_op jit(solution)/shard_map/psum | solution.py:99
  240.0 8.1 %copy-start.10 = (bf16[32,4,32,128]{3,2,1,0:T(8,128)(2,1)S(1)}, bf16[32,4,32,128]{3,2,1,0:T(8,128)(2,1)}, u32[]{:S(2)}) copy-start(bf16[32,4,32,128]{3,2,1,0:T(8,128)(2,1)} %param.3) | copy-start | bytes 3145732
  252.4 8.0 %copy-start.4 = (bf16[32,4,32,128]{3,0,2,1:T(8,128)(2,1)S(1)}, bf16[32,4,32,128]{3,0,2,1:T(8,128)(2,1)}, u32[]{:S(2)}) copy-start(bf16[32,4,32,128]{3,0,2,1:T(8,128)(2,1)} %copy-done.3) | copy-start | bytes 3145732
  252.4 8.0 %copy-start.12 = (bf16[32,1,32,128]{3,0,2,1:T(8,128)(2,1)S(1)}, bf16[32,1,32,128]{3,0,2,1:T(8,128)(2,1)}, u32[]{:S(2)}) copy-start(bf16[32,1,32,128]{3,0,2,1:T(8,128)(2,1)} %copy-done.11) | copy-start | bytes 786436
  315.3 14.2 %copy-start.5 = (bf16[128,4,32,128]{3,2,1,0:T(8,128)(2,1)S(1)}, bf16[128,4,32,128]{3,2,1,0:T(8,128)(2,1)}, u32[]{:S(2)}) copy-start(bf16[128,4,32,128]{3,2,1,0:T(8,128)(2,1)} %all-gather.2.cloned.1.call-done) | copy-start | bytes 12582916
  320.4 2.0 copy-start.1
  323.8 74.2 %collective-permute-start.3 = (bf16[128,1,32,128]{3,0,2,1:T(8,128)(2,1)}, bf16[128,1,32,128]{3,0,2,1:T(8,128)(2,1)S(1)}, u32[]{:S(2)}, u32[]{:S(2)}) collective-permute-start(bf16[128,1,32,128]{3,0,2,1:T(8,128)(2,1)} %get-tuple-element.7), channel_id=1, source_target_pairs={{4,0},{8,4},{12,8},{16,12},{20,16},{24,20},{28,24},{5,1},{9,5},{13... | collective-permute-start | bytes 3145736 | tf_op jit(solution)/shard_map/ppermute | solution.py:17
  325.1 72.9 %collective-permute-start.2 = (bf16[128,1,32,128]{3,0,2,1:T(8,128)(2,1)}, bf16[128,1,32,128]{3,0,2,1:T(8,128)(2,1)}, u32[]{:S(2)}, u32[]{:S(2)}) collective-permute-start(bf16[128,1,32,128]{3,0,2,1:T(8,128)(2,1)} %get-tuple-element.6), channel_id=1, source_target_pairs={{0,4},{4,8},{8,12},{12,16},{16,20},{20,24},{24,28},{1,5},{5,9},{9,... | collective-permute-start | bytes 3145736 | tf_op jit(solution)/shard_map/ppermute | solution.py:14
  398.0 10.0 %copy-start.14 = (bf16[27,32,128]{2,1,0:T(8,128)(2,1)S(1)}, bf16[27,32,128]{2,1,0:T(8,128)(2,1)}, u32[]{:S(2)}) copy-start(bf16[27,32,128]{2,1,0:T(8,128)(2,1)} %param.4) | copy-start | bytes 663556
  408.1 57.3 %copy-start = (bf16[128,6,34,130]{3,0,2,1:T(8,128)(2,1)}, bf16[128,6,34,130]{3,0,2,1:T(8,128)(2,1)S(1)}, u32[]{:S(2)}) copy-start(bf16[128,6,34,130]{3,0,2,1:T(8,128)(2,1)S(1)} %select_maximum_fusion) | copy-start | bytes 20367364
  462.5 5.8 %copy-start.2 = (bf16[128,4,32,128]{3,0,2,1:T(8,128)(2,1)S(1)}, bf16[128,4,32,128]{3,0,2,1:T(8,128)(2,1)}, u32[]{:S(2)}) copy-start(bf16[128,4,32,128]{3,0,2,1:T(8,128)(2,1)} %copy-done.1) | copy-start | bytes 12582916
Sparse Core Ops, SparseCore 0:
  77.8 152.1 reduce-scatter.1
  233.8 81.4 all-gather.1
  343.5 52.6 all-reduce.3
where the time goes:
time: 511 us; the launch traced here: 501 us
  waiting for transfers between devices  245 us (48%)
  matrix products  137 us (27%)
  local copies, waits for them, and re-layouts  72.6 us (14%)
  other arithmetic  22.2 us (4%)
  between operations  14.5 us (3%)
  starting transfers between devices  10.4 us (2%)
    reduce_scatter x1, waiting for transfers between devices, body(): lax.psum_scatter(partial_sum, 'chan', scatter_dimension=0, tiled=True)  148 us
    dot_general x27, matrix products, body(): jnp.einsum('io,odhw->idhw', filters[offset], window, preferred_element_ty...  89.9 us
    unnamed x63, local copies, waits for them, and re-layouts  51.9 us
    all_gather x1, waiting for transfers between devices, body(): grad_all = lax.all_gather(grad_out, 'chan', axis=0, tiled=True)  48.5 us
    psum x1, waiting for transfers between devices, body(): grad_w = lax.psum(grad_w, 'space')  48 us
    dot_general x3, matrix products, forward_part(): jnp.einsum('io,idhw->odhw', block, stacked, preferred_element_type=jnp.fl...  33.2 us
    dot_general x1, matrix products, body(): jnp.einsum('kidhw,odhw->kio', stacked_in, grad_all, preferred_element_typ...  13.8 us
    concatenate x2, other arithmetic, with_halo(): block = jnp.concatenate([low, block, high], axis=dim)  12.1 us
  transfers between devices with their start and end apart: 7, of which 4 were waited for; matrix products, arithmetic and copies ran while one was open for 12% of the time, Pallas kernels for 0%

commit v1 on v0

v1 whole, which is shorter than its diff:
```python
import functools
import math

import jax
import jax.numpy as jnp
from jax import lax
from jax.experimental import pallas as pl
from jax.experimental.pallas import tpu as pltpu
from jax.sharding import PartitionSpec as P

BF16 = jnp.bfloat16
F32 = jnp.float32
VMEM_BYTES = 56 * 1024 * 1024


def ring(count, step):
    return [(i, (i + step) % count) for i in range(count)]


def shift_sum(parts, groups, cells, up_first):
    first, mid, last = (p.reshape(groups, cells, -1) for p in parts)
    if up_first:
        first, last = last, first
    col = lax.broadcasted_iota(jnp.int32, mid.shape, 1)
    before = jnp.where(col == 0, 0.0, pltpu.roll(first, 1, 1))
    after = jnp.where(col == cells - 1, 0.0, pltpu.roll(last, cells - 1, 1))
    return mid + before + after


def forward_kernel(chan_count, z_ref, *refs):
    pieces = refs[:chan_count]
    low_ref, high_ref, weights_ref, slope_ref, first_ref, last_ref = refs[chan_count:]
    rows, planes, group, cells = pieces[0].shape
    channels = group * chan_count
    z = z_ref[0]
    offsets = [
        pl.multiple_of(lax.rem(z - j + chan_count, chan_count) * group, group)
        for j in range(chan_count)
    ]

    @pl.loop(0, rows)
    def _(r):
        for j in range(chan_count):
            for p in range(planes):
                first_ref[r, p + 1, pl.ds(offsets[j], group), :] = pieces[j][r, p]
            first_ref[r, 0, pl.ds(offsets[j], group), :] = low_ref[
                r, 0, j * group : (j + 1) * group, :
            ]
            first_ref[r, planes + 1, pl.ds(offsets[j], group), :] = high_ref[
                r, 0, j * group : (j + 1) * group, :
            ]
        for p in range(planes + 2):
            last_ref[r, p] = first_ref[r, p].T

    @pl.loop(0, rows - 2)
    def _(r):
        lhs = jnp.concatenate(
            [
                last_ref[r + b, a : a + planes].reshape(planes * cells, channels)
                for a in range(3)
                for b in range(3)
            ],
            axis=1,
        )
        out = jnp.dot(lhs, weights_ref[...], preferred_element_type=F32)
        pre = shift_sum(
            [out[:, c * channels : (c + 1) * channels] for c in range(3)], planes, cells, False
        )
        sigma = 1.0 / (1.0 + jnp.exp(-pre))
        slope_ref[r] = sigma * (1.0 + pre * (1.0 - sigma))


def grad_out_kernel(chan_count, z_ref, *refs):
    pieces = refs[:chan_count]
    slope_ref, grad_ref, low_ref, high_ref, hold_ref = refs[chan_count:]
    rows, planes, group, cells = pieces[0].shape
    z = z_ref[0]
    offsets = [
        pl.multiple_of(lax.rem(z - j + chan_count, chan_count) * group, group)
        for j in range(chan_count)
    ]

    @pl.loop(0, rows)
    def _(r):
        for p in range(planes):
            for j in range(chan_count):
                hold_ref[p, pl.ds(offsets[j], group), :] = pieces[j][r, p]
        for p in range(planes):
            cot = hold_ref[p].T.astype(F32)
            grad = (cot * slope_ref[r, p]).astype(BF16)
            grad_ref[r, p] = grad
            if p == 0:
                low_ref[r] = grad
            if p == planes - 1:
                high_ref[r] = grad


def filter_kernel(chan_count, space_count, shard, core_ref, x_ref, grad_ref, keep_ref, send_ref, acc_ref, pack_ref):
    rows = grad_ref.shape[0] - 2
    planes, cells, channels = grad_ref.shape[1:]
    group = channels // chan_count
    acc_ref[...] = jnp.zeros_like(acc_ref)

    @pl.loop(0, rows)
    def _(h):
        lhs = jnp.concatenate(
            [
                jnp.concatenate([x_ref[h + 1 + b, d + a] for d in range(planes)], axis=1)
                for a in range(3)
                for b in range(3)
            ],
            axis=0,
        )
        grad = grad_ref[h + 1].astype(F32)
        col = lax.broadcasted_iota(jnp.int32, grad.shape, 1)
        after = jnp.where(col == cells - 1, 0.0, pltpu.roll(grad, cells - 1, 1))
        before = jnp.where(col == 0, 0.0, pltpu.roll(grad, 1, 1))
        rhs = jnp.concatenate(
            [v.astype(BF16).reshape(planes * cells, channels) for v in (after, grad, before)],
            axis=1,
        )
        acc_ref[...] += jnp.dot(lhs, rhs, preferred_element_type=F32)

    used = 27 * group
    for z in range(chan_count):
        for offset in range(27):
            row = (offset // 3) * channels + z * group
            col = (offset % 3) * channels
            pack_ref[z, offset * group : (offset + 1) * group, :] = acc_ref[
                row : row + group, col : col + channels
            ]
        pack_ref[z, used:, :] = jnp.zeros((space_count * shard - used, channels), F32)
    core = core_ref[0]
    for chip in range(space_count // 2):
        mine = pl.multiple_of((2 * chip + core) * shard, 8)
        other = pl.multiple_of((2 * chip + 1 - core) * shard, 8)
        for z in range(chan_count):
            keep_ref[chip, z] = pack_ref[z, pl.ds(mine, shard), :]
            send_ref[chip, z] = pack_ref[z, pl.ds(other, shard), :]


def input_kernel(chan_count, z_ref, grad_ref, low_ref, high_ref, weights_ref, *refs):
    outs = refs[:chan_count]
    hold_ref = refs[chan_count]
    rows = grad_ref.shape[0] - 2
    planes, cells, channels = grad_ref.shape[1:]
    group = channels // chan_count
    z = z_ref[0]
    offsets = [
        pl.multiple_of(lax.rem(z + j, chan_count) * group, group) for j in range(chan_count)
    ]

    @pl.loop(0, rows)
    def _(h):
        columns = []
        for a in range(3):
            for b in range(3):
                r = h + 2 - b
                if a == 1:
                    columns.append(grad_ref[r].reshape(planes * cells, channels))
                elif a == 0:
                    body = grad_ref[r, 1:planes].reshape((planes - 1) * cells, channels)
                    columns.append(jnp.concatenate([body, high_ref[r]], axis=0))
                else:
                    body = grad_ref[r, 0 : planes - 1].reshape((planes - 1) * cells, channels)
                    columns.append(jnp.concatenate([low_ref[r], body], axis=0))
        out = jnp.dot(
            jnp.concatenate(columns, axis=1), weights_ref[...], preferred_element_type=F32
        )
        total = shift_sum(
            [out[:, c * channels : (c + 1) * channels] for c in range(3)], planes, cells, True
        ).astype(BF16)
        for p in range(planes):
            hold_ref[p] = total[p].T
        for j in range(chan_count):
            for p in range(planes):
                outs[j][h, p] = hold_ref[p, pl.ds(offsets[j], group), :]


def call(kernel, outs, scratch, flops, args, scalar):
    nbytes = sum(math.prod(a.shape) * a.dtype.itemsize for a in list(args) + list(outs))
    return pl.pallas_call(
        kernel,
        out_shape=outs,
        in_specs=[pl.BlockSpec(memory_space=pltpu.SMEM)]
        + [pl.BlockSpec(memory_space=pltpu.VMEM)] * len(args),
        out_specs=[pl.BlockSpec(memory_space=pltpu.VMEM)] * len(outs),
        scratch_shapes=scratch,
        compiler_params=pltpu.CompilerParams(vmem_limit_bytes=VMEM_BYTES),
        cost_estimate=pl.CostEstimate(flops=flops, bytes_accessed=nbytes, transcendentals=0),
    )(scalar, *args)


def row_blocks(array, halo, z, chan_count):
    turned = jnp.pad(array.transpose(2, 1, 0, 3), ((halo, halo), (0, 0), (0, 0), (0, 0)))
    rows = array.shape[2] // chan_count
    return [
        lax.dynamic_slice_in_dim(turned, lax.rem(z + j, chan_count) * rows, rows + 2 * halo, axis=0)
        for j in range(chan_count)
    ]


def exchange(blocks, axis):
    count = len(blocks)
    return [blocks[0]] + [
        lax.ppermute(blocks[j], axis, ring(count, j)) for j in range(1, count)
    ]


def body(inputs, filters, cotangent):
    chan_count = lax.axis_size("chan")
    space_count = lax.axis_size("space")
    group, planes, height, cells = inputs.shape
    channels = group * chan_count
    rows = height // chan_count
    z = lax.axis_index("chan").astype(jnp.int32)
    s = lax.axis_index("space").astype(jnp.int32)
    upward = [(i, i + 1) for i in range(space_count - 1)]
    downward = [(i + 1, i) for i in range(space_count - 1)]
    shape = jax.ShapeDtypeStruct
    z_arg = z.reshape(1)

    x_pieces = exchange(row_blocks(inputs, 2, z, chan_count), "chan")
    filter_all = lax.all_gather(filters, "chan", axis=1, tiled=True)
    by_offset = filter_all.reshape(9, 3, channels, channels)
    weights_f = by_offset.transpose(0, 2, 1, 3).reshape(9 * channels, 3 * channels)
    weights_b = by_offset.transpose(0, 3, 1, 2).reshape(9 * channels, 3 * channels)

    x_top = jnp.concatenate([p[:, planes - 1 :] for p in x_pieces], axis=2)
    x_bottom = jnp.concatenate([p[:, :1] for p in x_pieces], axis=2)
    x_low = lax.ppermute(x_top, "space", upward)
    x_high = lax.ppermute(x_bottom, "space", downward)
    c_pieces = exchange(row_blocks(cotangent, 1, z, chan_count), "chan")

    macs = 27 * channels * channels * rows * planes * cells
    padded = (rows + 4, planes + 2, channels, cells)
    slope, x_first = call(
        functools.partial(forward_kernel, chan_count),
        [shape((rows + 2, planes, cells, channels), F32), shape(padded, BF16)],
        [pltpu.VMEM((rows + 4, planes + 2, cells, channels), BF16)],
        2 * macs * (rows + 2) // rows,
        [*x_pieces, x_low, x_high, weights_f],
        z_arg,
    )
    grad, g_bottom, g_top = call(
        functools.partial(grad_out_kernel, chan_count),
        [shape((rows + 2, planes, cells, channels), BF16)]
        + [shape((rows + 2, cells, channels), BF16)] * 2,
        [pltpu.VMEM((planes, channels, cells), BF16)],
        10 * rows * planes * cells * channels,
        [*c_pieces, slope],
        z_arg,
    )
    g_low = lax.ppermute(g_top, "space", upward)
    g_high = lax.ppermute(g_bottom, "space", downward)

    chips = space_count // 2
    shard = -(-27 * group // (16 * space_count)) * 16
    half = shape((chips, chan_count, shard, channels), F32)
    keep, send = call(
        functools.partial(filter_kernel, chan_count, space_count, shard),
        [half, half],
        [
            pltpu.VMEM((9 * channels, 3 * channels), F32),
            pltpu.VMEM((chan_count, space_count * shard, channels), F32),
        ],
        2 * macs,
        [x_first, grad],
        lax.rem(s, 2).reshape(1),
    )
    from_core = lax.ppermute(send, "space", [(i, i ^ 1) for i in range(space_count)])

    back = call(
        functools.partial(input_kernel, chan_count),
        [shape((rows, planes, group, cells), BF16)] * chan_count,
        [pltpu.VMEM((planes, channels, cells), BF16)],
        2 * macs,
        [grad, g_low, g_high, weights_b],
        z_arg,
    )
    returned = exchange(back, "chan")

    pair_sum = keep + from_core
    chip = s // 2
    own = lax.dynamic_index_in_dim(pair_sum, chip, 0, keepdims=False)
    rounded = pair_sum.astype(BF16)
    chip_sum = own
    for k in range(1, chips):
        block = lax.dynamic_index_in_dim(rounded, chip ^ k, 0, keepdims=False)
        got = lax.ppermute(block, "space", [(i, i ^ (2 * k)) for i in range(space_count)])
        chip_sum = chip_sum + got.astype(F32)
    parts = [
        lax.dynamic_index_in_dim(chip_sum, lax.rem(z + j, chan_count), 0, keepdims=False)
        for j in range(chan_count)
    ]
    shard_sum = sum(exchange(parts, "chan"))
    cell_total = planes * space_count * height * cells
    shard_sum = shard_sum * (1.0 / math.sqrt(cell_total))
    whole = lax.all_gather(shard_sum, "space", axis=0, tiled=True)
    grad_w = whole[: 27 * group].reshape(27, group, channels)

    reverse = returned[::-1]
    doubled = jnp.concatenate(reverse + reverse, axis=0)
    start = lax.rem(chan_count - 1 - z + chan_count, chan_count) * rows
    ordered = lax.dynamic_slice_in_dim(doubled, start, height, axis=0)
    return ordered.transpose(2, 1, 0, 3), grad_w


def solution(mesh):
    placed = (P("chan", "space", None, None), P(None, "chan", None), P("chan", "space", None, None))
    return jax.shard_map(
        body,
        mesh=mesh,
        in_specs=placed,
        out_specs=(P("chan", "space", None, None), P(None, "chan", None)),
        check_vma=False,
    )
```

time: 511 us -> 194 us (0.38); the launches traced: 501 us -> 193 us
  waiting for transfers between devices: 245 us -> 41 us
  matrix products: 137 us -> 0 us
  local copies, waits for them, and re-layouts: 72.6 us -> 17 us
  blocking collectives: 0 us -> 51.9 us
  Pallas kernels: 0 us -> 37.8 us
  starting transfers between devices: 10.4 us -> 44.3 us
  other arithmetic: 22.2 us -> 0.27 us
  between operations: 14.5 us -> 0.99 us
    reduce_scatter x1 -> x0, waiting for transfers between devices: 148 us -> none  [body(): lax.psum_scatter(partial_sum, 'chan', scatter_dimension=0, tiled=True)]
    dot_general x31 -> x0, matrix products: 137 us -> none  [the longest x27 89.9 us: body(): jnp.einsum('io,odhw->idhw', filters[offset], window, preferred_element_ty...]
    all_gather x0 -> x2, blocking collectives: none -> 51.9 us  [the longest x1 43.4 us: body(): filter_all = lax.all_gather(filters, 'chan', axis=1, tiled=True)]
    all_gather x1 -> x0, waiting for transfers between devices: 48.5 us -> none  [body(): grad_all = lax.all_gather(grad_out, 'chan', axis=0, tiled=True)]
    psum x1 -> x0, waiting for transfers between devices: 48 us -> none  [body(): grad_w = lax.psum(grad_w, 'space')]
    unnamed x63 -> x36, local copies, waits for them, and re-layouts: 51.9 us -> 9.24 us
    ppermute x4 -> x20, waiting for transfers between devices: 0.14 us -> 41 us  [the longest x12 33.1 us: exchange(): lax.ppermute(blocks[j], axis, ring(count, j))]
    pallas_call x0 -> x4, Pallas kernels: none -> 37.8 us  [call(): pl.pallas_call(kernel, out_shape=outs, in_specs=[pl.BlockSpec(memory_spac...]
  transfers between devices with their start and end apart: 7 -> 20, of which waited for: 4 -> 7; matrix products, arithmetic and copies ran while one was open for 12% -> 5% of each run, Pallas kernels for 0% -> 12%
where the time goes in v1:
time: 194 us; the launch traced here: 193 us
  blocking collectives  51.9 us (27%)
  starting transfers between devices  44.3 us (23%)
  waiting for transfers between devices  41 us (21%)
  Pallas kernels  37.8 us (19%)
  local copies, waits for them, and re-layouts  17 us (9%)
    all_gather x1, blocking collectives, body(): filter_all = lax.all_gather(filters, 'chan', axis=1, tiled=True)  43.4 us
    pallas_call x4, Pallas kernels, call(): pl.pallas_call(kernel, out_shape=outs, in_specs=[pl.BlockSpec(memory_spac...  37.8 us
    ppermute x12, waiting for transfers between devices, exchange(): lax.ppermute(blocks[j], axis, ring(count, j))  33.1 us
    ppermute x12, starting transfers between devices, exchange(): lax.ppermute(blocks[j], axis, ring(count, j))  27 us
    unnamed x36, local copies, waits for them, and re-layouts  9.24 us
    all_gather x1, blocking collectives, body(): whole = lax.all_gather(shard_sum, 'space', axis=0, tiled=True)  8.5 us
    ppermute x3, waiting for transfers between devices, body(): lax.ppermute(block, 'space', [(i, i ^ 2 * k) for i in range(space_count)])  6.21 us
    ppermute x1, starting transfers between devices, body(): lax.ppermute(send, 'space', [(i, i ^ 1) for i in range(space_count)])  5.43 us
  transfers between devices with their start and end apart: 20, of which 7 were waited for; matrix products, arithmetic and copies ran while one was open for 5% of the time, Pallas kernels for 12%

profile of v1, /device:TPU:0, one launch (start us, length us, event | category | flops | bytes accessed | tf_op | source)
XLA Modules:
  0.0 193.3 jit_solution(13359456898143160480)
XLA Ops:
  0.7 2.0 %copy.21 = bf16[32,4,32,128]{3,0,1,2:T(8,128)(2,1)S(1)} copy(bf16[32,4,32,128]{3,2,1,0:T(8,128)(2,1)} %param.3) | data formatting | bytes 2097152 | tf_op args[0]
  2.7 1.2 pad_dynamic-slice_fusion.6
  3.9 3.0 %collective-permute-start.3 = (bf16[12,4,32,128]{3,2,1,0:T(8,128)(2,1)S(1)}, bf16[12,4,32,128]{3,2,1,0:T(8,128)(2,1)}, u32[]{:S(2)}, u32[]{:S(2)}) collective-permute-start(bf16[12,4,32,128]{3,2,1,0:T(8,128)(2,1)S(1)} %get-tuple-element.33), channel_id=1, source_target_pairs={{0,1},{1,2},{2,3},{3,0},{4,5},{5,6},{6,7},{7,4},{8,9},{9,10},{10,1... | collective-permute-start | bytes 1179656 | tf_op jit(solution)/shard_map/ppermute | solution.py:206
  6.9 2.6 %collective-permute-start.4 = (bf16[12,4,32,128]{3,2,1,0:T(8,128)(2,1)S(1)}, bf16[12,4,32,128]{3,2,1,0:T(8,128)(2,1)}, u32[]{:S(2)}, u32[]{:S(2)}) collective-permute-start(bf16[12,4,32,128]{3,2,1,0:T(8,128)(2,1)S(1)} %get-tuple-element.34), channel_id=1, source_target_pairs={{0,2},{1,3},{2,0},{3,1},{4,6},{5,7},{6,4},{7,5},{8,10},{9,11},{10,... | collective-permute-start | bytes 1179656 | tf_op jit(solution)/shard_map/ppermute | solution.py:206
  9.5 1.3 collective-permute-start.5
  10.9 0.7 copy.22
  11.6 7.5 %collective-permute-done.3.refs_1_ = bf16[12,4,32,128]{3,2,1,0:T(8,128)(2,1)} collective-permute-done((bf16[12,4,32,128]{3,2,1,0:T(8,128)(2,1)S(1)}, bf16[12,4,32,128]{3,2,1,0:T(8,128)(2,1)}, u32[]{:S(2)}, u32[]{:S(2)}) %collective-permute-start.3) | collective-permute-done | bytes 393248 | tf_op jit(solution)/shard_map/ppermute | solution.py:206
  19.2 1.0 fusion.6
  20.1 15.1 %collective-permute-done.4.refs_2_ = bf16[12,4,32,128]{3,2,1,0:T(8,128)(2,1)} collective-permute-done((bf16[12,4,32,128]{3,2,1,0:T(8,128)(2,1)S(1)}, bf16[12,4,32,128]{3,2,1,0:T(8,128)(2,1)}, u32[]{:S(2)}, u32[]{:S(2)}) %collective-permute-start.4) | collective-permute-done | bytes 393248 | tf_op jit(solution)/shard_map/ppermute | solution.py:206
  35.2 1.0 fusion.7
  36.2 1.0 fusion.8
  37.2 1.3 collective-permute-start.7
  38.5 3.1 %collective-permute-start.6 = (bf16[12,1,128,128]{3,2,1,0:T(8,128)(2,1)S(1)}, bf16[12,1,128,128]{3,2,1,0:T(8,128)(2,1)S(1)}, u32[]{:S(2)}, u32[]{:S(2)}) collective-permute-start(bf16[12,1,128,128]{3,2,1,0:T(8,128)(2,1)S(1)} %pad_maximum_fusion), channel_id=1, source_target_pairs={{0,4},{4,8},{8,12},{12,16},{16,20},{20,24},{24,28},{1,5},{5,9},{9,... | collective-permute-start | bytes 1179656 | tf_op jit(solution)/shard_map/ppermute | solution.py:231
  41.6 1.0 pad_dynamic-slice_fusion
  42.6 7.9 %collective-permute-start = (bf16[10,4,32,128]{3,2,1,0:T(8,128)(2,1)S(1)}, bf16[10,4,32,128]{3,2,1,0:T(8,128)(2,1)S(1)}, u32[]{:S(2)}, u32[]{:S(2)}) collective-permute-start(bf16[10,4,32,128]{3,2,1,0:T(8,128)(2,1)S(1)} %get-tuple-element.37), channel_id=1, source_target_pairs={{0,1},{1,2},{2,3},{3,0},{4,5},{5,6},{6,7},{7,4},{8,9},{9,10},{10,1... | collective-permute-start | bytes 983048 | tf_op jit(solution)/shard_map/ppermute | solution.py:206
  50.5 2.6 %collective-permute-start.1 = (bf16[10,4,32,128]{3,2,1,0:T(8,128)(2,1)S(1)}, bf16[10,4,32,128]{3,2,1,0:T(8,128)(2,1)S(1)}, u32[]{:S(2)}, u32[]{:S(2)}) collective-permute-start(bf16[10,4,32,128]{3,2,1,0:T(8,128)(2,1)S(1)} %get-tuple-element.38), channel_id=1, source_target_pairs={{0,2},{1,3},{2,0},{3,1},{4,6},{5,7},{6,4},{7,5},{8,10},{9,11},{10,... | collective-permute-start | bytes 983048 | tf_op jit(solution)/shard_map/ppermute | solution.py:206
  53.1 43.4 %all_gather.6 = bf16[27,128,128]{2,1,0:T(8,128)(2,1)S(1)} all-gather(bf16[27,32,128]{2,1,0:T(8,128)(2,1)S(1)} %copy-done.6), channel_id=1, replica_groups=mesh['space'=8,'chan'=4] {'chan'}, dimensions={1}, use_global_device_ids=true | all-gather | bytes 1105920 | tf_op jit(solution)/shard_map/all_gather | solution.py:224
  96.5 0.8 copy.12
  97.3 1.1 copy.24
  98.3 0.7 copy-done.7
  99.1 0.1 copy-done.8
  99.2 13.6 %shard_map.50 = (f32[10,4,128,128]{3,2,1,0:T(8,128)}, bf16[12,6,128,128]{3,2,1,0:T(8,128)(2,1)}) custom-call(s32[1]{0:T(128)} %bitcast.z_ref, bf16[12,4,32,128]{3,2,1,0:T(8,128)(2,1)} %get-tuple-element.35.refs_0_, bf16[12,4,32,128]{3,2,1,0:T(8,128)(2,1)} %collective-permute-done.3.refs_1_, bf16[12,4,32,128]{3,2,1,0:T(8,128)(2,1)} %collective-permute-done.4.refs_2_, ...), custom_call_target="tpu_custom_call" | custom-call | flops 4529848320 | bytes 8224768 | tf_op jit(solution)/shard_map/pallas_call | solution.py:182
  112.9 0.7 copy-done.3
  113.8 4.5 %shard_map.51 = (bf16[10,4,128,128]{3,2,1,0:T(8,128)(2,1)}, bf16[10,128,128]{2,1,0:T(8,128)(2,1)}, bf16[10,128,128]{2,1,0:T(8,128)(2,1)}) custom-call(s32[1]{0:T(128)} %bitcast.z_ref, bf16[10,4,32,128]{3,2,1,0:T(8,128)(2,1)} %get-tuple-element.39.refs_0_, bf16[10,4,32,128]{3,2,1,0:T(8,128)(2,1)} %copy-done.3, bf16[10,4,32,128]{3,2,1,0:T(8,128)(2,1)} %copy-done.4, ...), custom_call_target="tpu_custom_call" | custom-call | flops 5242880 | bytes 5898240 | tf_op jit(solution)/shard_map/pallas_call | solution.py:182
  118.3 1.8 collective-permute-start.8
  120.0 1.3 collective-permute-start.9
  121.3 0.8 copy.13
  122.2 1.1 copy.23
  123.3 1.7 collective-permute-done.9.high_ref
  124.9 0.7 copy-done.10
  125.6 9.8 %shard_map.52 = (bf16[8,4,32,128]{3,2,1,0:T(8,128)(2,1)}, bf16[8,4,32,128]{3,2,1,0:T(8,128)(2,1)}, bf16[8,4,32,128]{3,2,1,0:T(8,128)(2,1)}, bf16[8,4,32,128]{3,2,1,0:T(8,128)(2,1)}) custom-call(s32[1]{0:T(128)} %bitcast.z_ref, bf16[10,4,128,128]{3,2,1,0:T(8,128)(2,1)} %get-tuple-element.14.grad_ref, bf16[10,128,128]{2,1,0:T(8,128)(2,1)} %copy-done.9, ...), custom_call_target="tpu_custom_call" | custom-call | flops 3623878656 | bytes 3899392 | tf_op jit(solution)/shard_map/pallas_call | solution.py:182
  135.4 3.3 %collective-permute-start.10 = (bf16[8,4,32,128]{3,2,1,0:T(8,128)(2,1)}, bf16[8,4,32,128]{3,2,1,0:T(8,128)(2,1)S(1)}, u32[]{:S(2)}, u32[]{:S(2)}) collective-permute-start(bf16[8,4,32,128]{3,2,1,0:T(8,128)(2,1)} %get-tuple-element.17), channel_id=1, source_target_pairs={{0,3},{1,0},{2,1},{3,2},{4,7},{5,4},{6,5},{7,6},{8,11},{9,8},{10,9... | collective-permute-start | bytes 786440 | tf_op jit(solution)/shard_map/ppermute | solution.py:206
  138.7 9.9 %shard_map.53 = (f32[4,4,112,128]{3,2,1,0:T(8,128)}, f32[4,4,112,128]{3,2,1,0:T(8,128)}) custom-call(s32[1]{0:T(128)} %bitcast.7.core_ref, bf16[12,6,128,128]{3,2,1,0:T(8,128)(2,1)} %get-tuple-element.21.x_ref, bf16[10,4,128,128]{3,2,1,0:T(8,128)(2,1)} %get-tuple-element.14.grad_ref), custom_call_target="tpu_custom_call" | custom-call | flops 3623878656 | bytes 5505024 | tf_op jit(solution)/shard_map/pallas_call | solution.py:182
  148.6 5.4 %collective-permute-start.13 = (f32[4,4,112,128]{3,2,1,0:T(8,128)}, f32[4,4,112,128]{3,2,1,0:T(8,128)S(1)}, u32[]{:S(2)}, u32[]{:S(2)}) collective-permute-start(f32[4,4,112,128]{3,2,1,0:T(8,128)} %get-tuple-element.23), channel_id=1, source_target_pairs={{0,4},{4,0},{8,12},{12,8},{16,20},{20,16},{24,28},{28,24},{1,5},{5... | collective-permute-start | bytes 2752520 | tf_op jit(solution)/shard_map/ppermute | solution.py:271
  154.1 0.6 collective-permute-start.12
  154.7 9.4 %collective-permute-done.12 = bf16[8,4,32,128]{3,2,1,0:T(8,128)(2,1)S(1)} collective-permute-done((bf16[8,4,32,128]{3,2,1,0:T(8,128)(2,1)S(1)}, bf16[8,4,32,128]{3,2,1,0:T(8,128)(2,1)S(1)}, u32[]{:S(2)}, u32[]{:S(2)}) %collective-permute-start.12) | collective-permute-done | bytes 262176 | tf_op jit(solution)/shard_map/ppermute | solution.py:206
  164.6 2.9 %collective-permute-start.14 = (bf16[4,112,128]{2,1,0:T(8,128)(2,1)S(1)}, bf16[4,112,128]{2,1,0:T(8,128)(2,1)S(1)}, u32[]{:S(2)}, u32[]{:S(2)}) collective-permute-start(bf16[4,112,128]{2,1,0:T(8,128)(2,1)S(1)} %get-tuple-element.40), channel_id=1, source_target_pairs={{0,8},{4,12},{8,0},{12,4},{16,24},{20,28},{24,16},{28,20},{1,9},{5... | collective-permute-start | bytes 344072 | tf_op jit(solution)/shard_map/ppermute | solution.py:290
  167.5 0.2 collective-permute-start.15
  167.7 1.4 collective-permute-start.16
  169.2 2.3 %collective-permute-done.14 = bf16[4,112,128]{2,1,0:T(8,128)(2,1)S(1)} collective-permute-done((bf16[4,112,128]{2,1,0:T(8,128)(2,1)S(1)}, bf16[4,112,128]{2,1,0:T(8,128)(2,1)S(1)}, u32[]{:S(2)}, u32[]{:S(2)}) %collective-permute-start.14) | collective-permute-done | bytes 114720 | tf_op jit(solution)/shard_map/ppermute | solution.py:290
  171.5 3.9 %collective-permute-done.15 = bf16[4,112,128]{2,1,0:T(8,128)(2,1)S(1)} collective-permute-done((bf16[4,112,128]{2,1,0:T(8,128)(2,1)S(1)}, bf16[4,112,128]{2,1,0:T(8,128)(2,1)S(1)}, u32[]{:S(2)}, u32[]{:S(2)}) %collective-permute-start.15) | collective-permute-done | bytes 114720 | tf_op jit(solution)/shard_map/ppermute | solution.py:290
  175.5 1.1 collective-permute-start.17
  176.6 2.5 %collective-permute-start.18 = (f32[112,128]{1,0:T(8,128)S(1)}, f32[112,128]{1,0:T(8,128)S(1)}, u32[]{:S(2)}, u32[]{:S(2)}) collective-permute-start(f32[112,128]{1,0:T(8,128)S(1)} %get-tuple-element.51), channel_id=1, source_target_pairs={{0,2},{1,3},{2,0},{3,1},{4,6},{5,7},{6,4},{7,5},{8,10},{9,11},{10,... | collective-permute-start | bytes 172040 | tf_op jit(solution)/shard_map/ppermute | solution.py:206
  179.1 2.1 %collective-permute-start.19 = (f32[112,128]{1,0:T(8,128)S(1)}, f32[112,128]{1,0:T(8,128)S(1)}, u32[]{:S(2)}, u32[]{:S(2)}) collective-permute-start(f32[112,128]{1,0:T(8,128)S(1)} %get-tuple-element.50), channel_id=1, source_target_pairs={{0,3},{1,0},{2,1},{3,2},{4,7},{5,4},{6,5},{7,6},{8,11},{9,8},{10,9... | collective-permute-start | bytes 172040 | tf_op jit(solution)/shard_map/ppermute | solution.py:206
  181.2 1.6 copy.14
  182.9 1.1 collective-permute-done.18
  184.0 8.5 %all_gather.7 = f32[896,128]{1,0:T(8,128)S(1)} all-gather(f32[112,128]{1,0:T(8,128)S(1)} %fusion.4), channel_id=1, replica_groups=mesh['space'=8,'chan'=4] {'space'}, dimensions={0}, use_global_device_ids=true | all-gather | bytes 516096 | tf_op jit(solution)/shard_map/all_gather | solution.py:299
  192.5 0.8 slice.42
  (52 shorter events, 1.0 us)
Async XLA Ops:
  0.7 10.2 %copy-start = (bf16[32,4,32,128]{3,2,1,0:T(8,128)(2,1)S(1)}, bf16[32,4,32,128]{3,2,1,0:T(8,128)(2,1)}, u32[]{:S(2)}) copy-start(bf16[32,4,32,128]{3,2,1,0:T(8,128)(2,1)} %param.5) | copy-start | bytes 3145732
  3.9 15.2 %collective-permute-start.3 = (bf16[12,4,32,128]{3,2,1,0:T(8,128)(2,1)S(1)}, bf16[12,4,32,128]{3,2,1,0:T(8,128)(2,1)}, u32[]{:S(2)}, u32[]{:S(2)}) collective-permute-start(bf16[12,4,32,128]{3,2,1,0:T(8,128)(2,1)S(1)} %get-tuple-element.33), channel_id=1, source_target_pairs={{0,1},{1,2},{2,3},{3,0},{4,5},{5,6},{6,7},{7,4},{8,9},{9,10},{10,1... | collective-permute-start | bytes 1179656 | tf_op jit(solution)/shard_map/ppermute | solution.py:206
  6.9 28.2 %collective-permute-start.4 = (bf16[12,4,32,128]{3,2,1,0:T(8,128)(2,1)S(1)}, bf16[12,4,32,128]{3,2,1,0:T(8,128)(2,1)}, u32[]{:S(2)}, u32[]{:S(2)}) collective-permute-start(bf16[12,4,32,128]{3,2,1,0:T(8,128)(2,1)S(1)} %get-tuple-element.34), channel_id=1, source_target_pairs={{0,2},{1,3},{2,0},{3,1},{4,6},{5,7},{6,4},{7,5},{8,10},{9,11},{10,... | collective-permute-start | bytes 1179656 | tf_op jit(solution)/shard_map/ppermute | solution.py:206
  9.5 26.6 %collective-permute-start.5 = (bf16[12,4,32,128]{3,2,1,0:T(8,128)(2,1)S(1)}, bf16[12,4,32,128]{3,2,1,0:T(8,128)(2,1)}, u32[]{:S(2)}, u32[]{:S(2)}) collective-permute-start(bf16[12,4,32,128]{3,2,1,0:T(8,128)(2,1)S(1)} %get-tuple-element.32), channel_id=1, source_target_pairs={{0,3},{1,0},{2,1},{3,2},{4,7},{5,4},{6,5},{7,6},{8,11},{9,8},{10,9... | collective-permute-start | bytes 1179656 | tf_op jit(solution)/shard_map/ppermute | solution.py:206
  36.1 17.0 %copy-start.6 = (bf16[27,32,128]{2,1,0:T(8,128)(2,1)S(1)}, bf16[27,32,128]{2,1,0:T(8,128)(2,1)}, u32[]{:S(2)}) copy-start(bf16[27,32,128]{2,1,0:T(8,128)(2,1)} %param.4) | copy-start | bytes 663556
  37.2 61.1 %collective-permute-start.7 = (bf16[12,1,128,128]{3,2,1,0:T(8,128)(2,1)S(1)}, bf16[12,1,128,128]{3,2,1,0:T(8,128)(2,1)S(1)}, u32[]{:S(2)}, u32[]{:S(2)}) collective-permute-start(bf16[12,1,128,128]{3,2,1,0:T(8,128)(2,1)S(1)} %pad_maximum_fusion.1), channel_id=1, source_target_pairs={{4,0},{8,4},{12,8},{16,12},{20,16},{24,20},{28,24},{5,1},{9,5},{13... | collective-permute-start | bytes 1179656 | tf_op jit(solution)/shard_map/ppermute | solution.py:232
  38.5 59.8 %collective-permute-start.6 = (bf16[12,1,128,128]{3,2,1,0:T(8,128)(2,1)S(1)}, bf16[12,1,128,128]{3,2,1,0:T(8,128)(2,1)S(1)}, u32[]{:S(2)}, u32[]{:S(2)}) collective-permute-start(bf16[12,1,128,128]{3,2,1,0:T(8,128)(2,1)S(1)} %pad_maximum_fusion), channel_id=1, source_target_pairs={{0,4},{4,8},{8,12},{12,16},{16,20},{20,24},{24,28},{1,5},{5,9},{9,... | collective-permute-start | bytes 1179656 | tf_op jit(solution)/shard_map/ppermute | solution.py:231
  42.6 70.2 %collective-permute-start = (bf16[10,4,32,128]{3,2,1,0:T(8,128)(2,1)S(1)}, bf16[10,4,32,128]{3,2,1,0:T(8,128)(2,1)S(1)}, u32[]{:S(2)}, u32[]{:S(2)}) collective-permute-start(bf16[10,4,32,128]{3,2,1,0:T(8,128)(2,1)S(1)} %get-tuple-element.37), channel_id=1, source_target_pairs={{0,1},{1,2},{2,3},{3,0},{4,5},{5,6},{6,7},{7,4},{8,9},{9,10},{10,1... | collective-permute-start | bytes 983048 | tf_op jit(solution)/shard_map/ppermute | solution.py:206
  50.5 62.3 %collective-permute-start.1 = (bf16[10,4,32,128]{3,2,1,0:T(8,128)(2,1)S(1)}, bf16[10,4,32,128]{3,2,1,0:T(8,128)(2,1)S(1)}, u32[]{:S(2)}, u32[]{:S(2)}) collective-permute-start(bf16[10,4,32,128]{3,2,1,0:T(8,128)(2,1)S(1)} %get-tuple-element.38), channel_id=1, source_target_pairs={{0,2},{1,3},{2,0},{3,1},{4,6},{5,7},{6,4},{7,5},{8,10},{9,11},{10,... | collective-permute-start | bytes 983048 | tf_op jit(solution)/shard_map/ppermute | solution.py:206
  53.1 59.7 %collective-permute-start.2 = (bf16[10,4,32,128]{3,2,1,0:T(8,128)(2,1)S(1)}, bf16[10,4,32,128]{3,2,1,0:T(8,128)(2,1)S(1)}, u32[]{:S(2)}, u32[]{:S(2)}) collective-permute-start(bf16[10,4,32,128]{3,2,1,0:T(8,128)(2,1)S(1)} %get-tuple-element.36), channel_id=1, source_target_pairs={{0,3},{1,0},{2,1},{3,2},{4,7},{5,4},{6,5},{7,6},{8,11},{9,8},{10,9... | collective-permute-start | bytes 983048 | tf_op jit(solution)/shard_map/ppermute | solution.py:206
  98.3 0.8 copy-start.7
  98.3 0.9 copy-start.8
  112.8 0.7 copy-start.3
  112.8 0.8 copy-start.4
  112.8 0.9 copy-start.5
  118.3 5.0 %collective-permute-start.8 = (bf16[10,128,128]{2,1,0:T(8,128)(2,1)}, bf16[10,128,128]{2,1,0:T(8,128)(2,1)S(1)}, u32[]{:S(2)}, u32[]{:S(2)}) collective-permute-start(bf16[10,128,128]{2,1,0:T(8,128)(2,1)} %get-tuple-element.15), channel_id=1, source_target_pairs={{0,4},{4,8},{8,12},{12,16},{16,20},{20,24},{24,28},{1,5},{5,9},{9,... | collective-permute-start | bytes 983048 | tf_op jit(solution)/shard_map/ppermute | solution.py:254
  120.0 4.9 %collective-permute-start.9 = (bf16[10,128,128]{2,1,0:T(8,128)(2,1)}, bf16[10,128,128]{2,1,0:T(8,128)(2,1)S(1)}, u32[]{:S(2)}, u32[]{:S(2)}) collective-permute-start(bf16[10,128,128]{2,1,0:T(8,128)(2,1)} %get-tuple-element.16), channel_id=1, source_target_pairs={{4,0},{8,4},{12,8},{16,12},{20,16},{24,20},{28,24},{5,1},{9,5},{13... | collective-permute-start | bytes 983048 | tf_op jit(solution)/shard_map/ppermute | solution.py:255
  123.2 1.7 copy-start.9
  124.9 0.7 copy-start.10
  135.4 19.2 %collective-permute-start.10 = (bf16[8,4,32,128]{3,2,1,0:T(8,128)(2,1)}, bf16[8,4,32,128]{3,2,1,0:T(8,128)(2,1)S(1)}, u32[]{:S(2)}, u32[]{:S(2)}) collective-permute-start(bf16[8,4,32,128]{3,2,1,0:T(8,128)(2,1)} %get-tuple-element.17), channel_id=1, source_target_pairs={{0,3},{1,0},{2,1},{3,2},{4,7},{5,4},{6,5},{7,6},{8,11},{9,8},{10,9... | collective-permute-start | bytes 786440 | tf_op jit(solution)/shard_map/ppermute | solution.py:206
  138.7 16.0 %collective-permute-start.11 = (bf16[8,4,32,128]{3,2,1,0:T(8,128)(2,1)}, bf16[8,4,32,128]{3,2,1,0:T(8,128)(2,1)S(1)}, u32[]{:S(2)}, u32[]{:S(2)}) collective-permute-start(bf16[8,4,32,128]{3,2,1,0:T(8,128)(2,1)} %get-tuple-element.18), channel_id=1, source_target_pairs={{0,2},{1,3},{2,0},{3,1},{4,6},{5,7},{6,4},{7,5},{8,10},{9,11},{10,... | collective-permute-start | bytes 786440 | tf_op jit(solution)/shard_map/ppermute | solution.py:206
  138.7 15.4 %copy-start.11 = (bf16[8,4,32,128]{3,2,1,0:T(8,128)(2,1)S(1)}, bf16[8,4,32,128]{3,2,1,0:T(8,128)(2,1)}, u32[]{:S(2)}) copy-start(bf16[8,4,32,128]{3,2,1,0:T(8,128)(2,1)} %get-tuple-element.19) | copy-start | bytes 786436
  138.7 25.5 %copy-start.1 = (bf16[8,4,32,128]{3,2,1,0:T(8,128)(2,1)S(1)}, bf16[8,4,32,128]{3,2,1,0:T(8,128)(2,1)}, u32[]{:S(2)}) copy-start(bf16[8,4,32,128]{3,2,1,0:T(8,128)(2,1)} %get-tuple-element.20) | copy-start | bytes 786436
  148.6 15.8 %copy-start.2 = (f32[4,4,112,128]{3,2,1,0:T(8,128)S(1)}, f32[4,4,112,128]{3,2,1,0:T(8,128)}, u32[]{:S(2)}) copy-start(f32[4,4,112,128]{3,2,1,0:T(8,128)} %get-tuple-element.22) | copy-start | bytes 2752516
  148.6 15.7 %collective-permute-start.13 = (f32[4,4,112,128]{3,2,1,0:T(8,128)}, f32[4,4,112,128]{3,2,1,0:T(8,128)S(1)}, u32[]{:S(2)}, u32[]{:S(2)}) collective-permute-start(f32[4,4,112,128]{3,2,1,0:T(8,128)} %get-tuple-element.23), channel_id=1, source_target_pairs={{0,4},{4,0},{8,12},{12,8},{16,20},{20,16},{24,28},{28,24},{1,5},{5... | collective-permute-start | bytes 2752520 | tf_op jit(solution)/shard_map/ppermute | solution.py:271
  154.1 10.1 %collective-permute-start.12 = (bf16[8,4,32,128]{3,2,1,0:T(8,128)(2,1)S(1)}, bf16[8,4,32,128]{3,2,1,0:T(8,128)(2,1)S(1)}, u32[]{:S(2)}, u32[]{:S(2)}) collective-permute-start(bf16[8,4,32,128]{3,2,1,0:T(8,128)(2,1)S(1)} %copy-done.11), channel_id=1, source_target_pairs={{0,1},{1,2},{2,3},{3,0},{4,5},{5,6},{6,7},{7,4},{8,9},{9,10},{10,1... | collective-permute-start | bytes 786440 | tf_op jit(solution)/shard_map/ppermute | solution.py:206
  164.6 6.9 %collective-permute-start.14 = (bf16[4,112,128]{2,1,0:T(8,128)(2,1)S(1)}, bf16[4,112,128]{2,1,0:T(8,128)(2,1)S(1)}, u32[]{:S(2)}, u32[]{:S(2)}) collective-permute-start(bf16[4,112,128]{2,1,0:T(8,128)(2,1)S(1)} %get-tuple-element.40), channel_id=1, source_target_pairs={{0,8},{4,12},{8,0},{12,4},{16,24},{20,28},{24,16},{28,20},{1,9},{5... | collective-permute-start | bytes 344072 | tf_op jit(solution)/shard_map/ppermute | solution.py:290
  167.5 7.9 %collective-permute-start.15 = (bf16[4,112,128]{2,1,0:T(8,128)(2,1)S(1)}, bf16[4,112,128]{2,1,0:T(8,128)(2,1)S(1)}, u32[]{:S(2)}, u32[]{:S(2)}) collective-permute-start(bf16[4,112,128]{2,1,0:T(8,128)(2,1)S(1)} %get-tuple-element.42), channel_id=1, source_target_pairs={{0,16},{4,20},{8,24},{12,28},{16,0},{20,4},{24,8},{28,12},{1,17},{... | collective-permute-start | bytes 344072 | tf_op jit(solution)/shard_map/ppermute | solution.py:290
  167.7 7.6 %collective-permute-start.16 = (bf16[4,112,128]{2,1,0:T(8,128)(2,1)S(1)}, bf16[4,112,128]{2,1,0:T(8,128)(2,1)S(1)}, u32[]{:S(2)}, u32[]{:S(2)}) collective-permute-start(bf16[4,112,128]{2,1,0:T(8,128)(2,1)S(1)} %get-tuple-element.41), channel_id=1, source_target_pairs={{0,24},{4,28},{8,16},{12,20},{16,8},{20,12},{24,0},{28,4},{1,25},{... | collective-permute-start | bytes 344072 | tf_op jit(solution)/shard_map/ppermute | solution.py:290
  175.5 7.4 %collective-permute-start.17 = (f32[112,128]{1,0:T(8,128)S(1)}, f32[112,128]{1,0:T(8,128)S(1)}, u32[]{:S(2)}, u32[]{:S(2)}) collective-permute-start(f32[112,128]{1,0:T(8,128)S(1)} %get-tuple-element.49), channel_id=1, source_target_pairs={{0,1},{1,2},{2,3},{3,0},{4,5},{5,6},{6,7},{7,4},{8,9},{9,10},{10,1... | collective-permute-start | bytes 172040 | tf_op jit(solution)/shard_map/ppermute | solution.py:206
  176.6 7.3 %collective-permute-start.18 = (f32[112,128]{1,0:T(8,128)S(1)}, f32[112,128]{1,0:T(8,128)S(1)}, u32[]{:S(2)}, u32[]{:S(2)}) collective-permute-start(f32[112,128]{1,0:T(8,128)S(1)} %get-tuple-element.51), channel_id=1, source_target_pairs={{0,2},{1,3},{2,0},{3,1},{4,6},{5,7},{6,4},{7,5},{8,10},{9,11},{10,... | collective-permute-start | bytes 172040 | tf_op jit(solution)/shard_map/ppermute | solution.py:206
  179.1 4.9 %collective-permute-start.19 = (f32[112,128]{1,0:T(8,128)S(1)}, f32[112,128]{1,0:T(8,128)S(1)}, u32[]{:S(2)}, u32[]{:S(2)}) collective-permute-start(f32[112,128]{1,0:T(8,128)S(1)} %get-tuple-element.50), channel_id=1, source_target_pairs={{0,3},{1,0},{2,1},{3,2},{4,7},{5,4},{6,5},{7,6},{8,11},{9,8},{10,9... | collective-permute-start | bytes 172040 | tf_op jit(solution)/shard_map/ppermute | solution.py:206

commit v2 on v1

--- a/solution.py
+++ b/solution.py
@@ -25,6 +25,10 @@
     before = jnp.where(col == 0, 0.0, pltpu.roll(first, 1, 1))
     after = jnp.where(col == cells - 1, 0.0, pltpu.roll(last, cells - 1, 1))
     return mid + before + after
+
+
+def kept(flag, value):
+    return jnp.where(flag > 0, value, jnp.zeros_like(value))
 
 
 def forward_kernel(chan_count, z_ref, *refs):
@@ -43,12 +47,11 @@
         for j in range(chan_count):
             for p in range(planes):
                 first_ref[r, p + 1, pl.ds(offsets[j], group), :] = pieces[j][r, p]
-            first_ref[r, 0, pl.ds(offsets[j], group), :] = low_ref[
-                r, 0, j * group : (j + 1) * group, :
-            ]
-            first_ref[r, planes + 1, pl.ds(offsets[j], group), :] = high_ref[
-                r, 0, j * group : (j + 1) * group, :
-            ]
+            part = slice(j * group, (j + 1) * group)
+            first_ref[r, 0, pl.ds(offsets[j], group), :] = kept(z_ref[1], low_ref[r, 0, part, :])
+            first_ref[r, planes + 1, pl.ds(offsets[j], group), :] = kept(
+                z_ref[2], high_ref[r, 0, part, :]
+            )
         for p in range(planes + 2):
             last_ref[r, p] = first_ref[r, p].T
 
@@ -95,9 +98,10 @@
                 high_ref[r] = grad
 
 
-def filter_kernel(chan_count, space_count, shard, core_ref, x_ref, grad_ref, keep_ref, send_ref, acc_ref, pack_ref):
-    rows = grad_ref.shape[0] - 2
-    planes, cells, channels = grad_ref.shape[1:]
+def filter_kernel(
+    chan_count, space_count, shard, core_ref, x_ref, grad_ref, keep_ref, send_ref, acc_ref, pack_ref
+):
+    rows, planes, cells, channels = grad_ref.shape
     group = channels // chan_count
     acc_ref[...] = jnp.zeros_like(acc_ref)
 
@@ -105,13 +109,13 @@
     def _(h):
         lhs = jnp.concatenate(
             [
-                jnp.concatenate([x_ref[h + 1 + b, d + a] for d in range(planes)], axis=1)
+                jnp.concatenate([x_ref[h + b, d + a] for d in range(planes)], axis=1)
                 for a in range(3)
                 for b in range(3)
             ],
             axis=0,
         )
-        grad = grad_ref[h + 1].astype(F32)
+        grad = grad_ref[h].astype(F32)
         col = lax.broadcasted_iota(jnp.int32, grad.shape, 1)
         after = jnp.where(col == cells - 1, 0.0, pltpu.roll(grad, cells - 1, 1))
         before = jnp.where(col == 0, 0.0, pltpu.roll(grad, 1, 1))
@@ -139,42 +143,83 @@
             send_ref[chip, z] = pack_ref[z, pl.ds(other, shard), :]
 
 
-def input_kernel(chan_count, z_ref, grad_ref, low_ref, high_ref, weights_ref, *refs):
-    outs = refs[:chan_count]
-    hold_ref = refs[chan_count]
-    rows = grad_ref.shape[0] - 2
-    planes, cells, channels = grad_ref.shape[1:]
-    group = channels // chan_count
-    z = z_ref[0]
-    offsets = [
-        pl.multiple_of(lax.rem(z + j, chan_count) * group, group) for j in range(chan_count)
-    ]
-
-    @pl.loop(0, rows)
+def input_row(center, low, high, weights_ref, hold_ref, offsets):
+    columns = []
+    planes, cells, channels = center(1).shape
+    for a in range(3):
+        for b in range(3):
+            row = center(b)
+            if a == 1:
+                part = row.reshape(planes * cells, channels)
+            elif a == 0:
+                body = row[1:].reshape((planes - 1) * cells, channels)
+                part = jnp.concatenate([body, high(b)], axis=0)
+            else:
+                body = row[: planes - 1].reshape((planes - 1) * cells, channels)
+                part = jnp.concatenate([low(b), body], axis=0)
+            columns.append(part)
+    out = jnp.dot(jnp.concatenate(columns, axis=1), weights_ref[...], preferred_element_type=F32)
+    total = shift_sum(
+        [out[:, c * channels : (c + 1) * channels] for c in range(3)], planes, cells, True
+    ).astype(BF16)
+    for p in range(planes):
+        hold_ref[p] = total[p].T
+    group = channels // len(offsets)
+    return [
+        jnp.stack([hold_ref[p, pl.ds(offset, group), :] for p in range(planes)])
+        for offset in offsets
+    ]
+
+
+def group_offsets(z, chan_count, group):
+    return [pl.multiple_of(lax.rem(z + j, chan_count) * group, group) for j in range(chan_count)]
+
+
+def inner_kernel(chan_count, z_ref, grad_ref, low_ref, high_ref, weights_ref, *refs):
+    outs, hold_ref = refs[:chan_count], refs[chan_count]
+    rows, planes, cells, channels = grad_ref.shape
+    offsets = group_offsets(z_ref[0], chan_count, channels // chan_count)
+
+    @pl.loop(1, rows - 1)
     def _(h):
-        columns = []
-        for a in range(3):
-            for b in range(3):
-                r = h + 2 - b
-                if a == 1:
-                    columns.append(grad_ref[r].reshape(planes * cells, channels))
-                elif a == 0:
-                    body = grad_ref[r, 1:planes].reshape((planes - 1) * cells, channels)
-                    columns.append(jnp.concatenate([body, high_ref[r]], axis=0))
-                else:
-                    body = grad_ref[r, 0 : planes - 1].reshape((planes - 1) * cells, channels)
-                    columns.append(jnp.concatenate([low_ref[r], body], axis=0))
-        out = jnp.dot(
-            jnp.concatenate(columns, axis=1), weights_ref[...], preferred_element_type=F32
-        )
-        total = shift_sum(
-            [out[:, c * channels : (c + 1) * channels] for c in range(3)], planes, cells, True
-        ).astype(BF16)
-        for p in range(planes):
-            hold_ref[p] = total[p].T
-        for j in range(chan_count):
-            for p in range(planes):
-                outs[j][h, p] = hold_ref[p, pl.ds(offsets[j], group), :]
+        blocks = input_row(
+            lambda b: grad_ref[h + 1 - b],
+            lambda b: kept(z_ref[1], low_ref[h + 1 - b]),
+            lambda b: kept(z_ref[2], high_ref[h + 1 - b]),
+            weights_ref,
+            hold_ref,
+            offsets,
+        )
+        for out, block in zip(outs, blocks):
+            out[h - 1] = block
+
+
+def edge_kernel(chan_count, z_ref, grad_ref, low_ref, high_ref, up_ref, down_ref, weights_ref, *refs):
+    inner, outs, hold_ref = refs[:chan_count], refs[chan_count : 2 * chan_count], refs[-1]
+    rows, planes, cells, channels = grad_ref.shape
+    offsets = group_offsets(z_ref[0], chan_count, channels // chan_count)
+    for j in range(chan_count):
+        outs[j][1 : rows - 1] = inner[j][...]
+
+    def pick(h, b, beyond, inside):
+        row = h + 1 - b
+        if row < 0:
+            return kept(z_ref[3], beyond(up_ref))
+        if row >= rows:
+            return kept(z_ref[4], beyond(down_ref))
+        return inside(row)
+
+    for h in (0, rows - 1):
+        blocks = input_row(
+            lambda b: pick(h, b, lambda ref: ref[1 : planes + 1], lambda row: grad_ref[row]),
+            lambda b: pick(h, b, lambda ref: kept(z_ref[1], ref[0]), lambda row: kept(z_ref[1], low_ref[row])),
+            lambda b: pick(h, b, lambda ref: kept(z_ref[2], ref[planes + 1]), lambda row: kept(z_ref[2], high_ref[row])),
+            weights_ref,
+            hold_ref,
+            offsets,
+        )
+        for out, block in zip(outs, blocks):
+            out[h] = block
 
 
 def call(kernel, outs, scratch, flops, args, scalar):
@@ -187,7 +232,9 @@
         out_specs=[pl.BlockSpec(memory_space=pltpu.VMEM)] * len(outs),
         scratch_shapes=scratch,
         compiler_params=pltpu.CompilerParams(vmem_limit_bytes=VMEM_BYTES),
-        cost_estimate=pl.CostEstimate(flops=flops, bytes_accessed=nbytes, transcendentals=0),
+        cost_estimate=pl.CostEstimate(
+            flops=flops, bytes_accessed=nbytes if flops else 0, transcendentals=0
+        ),
     )(scalar, *args)
 
 
@@ -205,6 +252,25 @@
     return [blocks[0]] + [
         lax.ppermute(blocks[j], axis, ring(count, j)) for j in range(1, count)
     ]
+
+
+def after(value, *others):
+    return lax.optimization_barrier((value, *others))[0]
+
+
+def gather_filters(filters, z, s, chan_count, space_count):
+    offsets, group, channels = filters.shape
+    rows = offsets * group
+    shard = -(-rows // (16 * space_count)) * 16
+    flat = jnp.pad(filters.reshape(rows, channels), ((0, space_count * shard - rows), (0, 0)))
+    mine = lax.dynamic_slice_in_dim(flat, s * shard, shard, axis=0)
+    got = [mine] + [
+        lax.ppermute(mine, "chan", ring(chan_count, j)) for j in range(1, chan_count)
+    ]
+    doubled = jnp.stack(got[::-1] + got[::-1])
+    shares = lax.dynamic_slice_in_dim(doubled, chan_count - 1 - z, chan_count, axis=0)
+    whole = lax.all_gather(shares, "space", axis=1, tiled=True)
+    return whole[:, :rows].reshape(chan_count, offsets, group, channels)
 
 
 def body(inputs, filters, cotangent):
@@ -215,37 +281,48 @@
     rows = height // chan_count
     z = lax.axis_index("chan").astype(jnp.int32)
     s = lax.axis_index("space").astype(jnp.int32)
-    upward = [(i, i + 1) for i in range(space_count - 1)]
-    downward = [(i + 1, i) for i in range(space_count - 1)]
+    upward, downward = ring(space_count, 1), ring(space_count, -1)
     shape = jax.ShapeDtypeStruct
-    z_arg = z.reshape(1)
-
-    x_pieces = exchange(row_blocks(inputs, 2, z, chan_count), "chan")
-    filter_all = lax.all_gather(filters, "chan", axis=1, tiled=True)
-    by_offset = filter_all.reshape(9, 3, channels, channels)
-    weights_f = by_offset.transpose(0, 2, 1, 3).reshape(9 * channels, 3 * channels)
-    weights_b = by_offset.transpose(0, 3, 1, 2).reshape(9 * channels, 3 * channels)
+    z_arg = jnp.stack(
+        [z]
+        + [
+            flag.astype(jnp.int32)
+            for flag in (s > 0, s < space_count - 1, z > 0, z < chan_count - 1)
+        ]
+    )
+
+    x_pieces = exchange(row_blocks(inputs, 1, z, chan_count), "chan")
+    filter_all = gather_filters(filters, z, s, chan_count, space_count)
+    by_offset = filter_all.reshape(chan_count, 9, 3, group, channels)
+    weights_f = by_offset.transpose(1, 0, 3, 2, 4).reshape(9 * channels, 3 * channels)
+    weights_b = by_offset.transpose(1, 4, 2, 0, 3).reshape(9 * channels, 3 * channels)
+    first, second, *rest = x_pieces
+    second = after(second, weights_f)
+    x_pieces = [first, second, *rest]
 
     x_top = jnp.concatenate([p[:, planes - 1 :] for p in x_pieces], axis=2)
     x_bottom = jnp.concatenate([p[:, :1] for p in x_pieces], axis=2)
     x_low = lax.ppermute(x_top, "space", upward)
     x_high = lax.ppermute(x_bottom, "space", downward)
-    c_pieces = exchange(row_blocks(cotangent, 1, z, chan_count), "chan")
+    c_blocks = row_blocks(cotangent, 0, z, chan_count)
+    c_pieces = exchange(
+        c_blocks[:1] + [after(c, x) for c, x in zip(c_blocks[1:], x_pieces[1:])], "chan"
+    )
 
     macs = 27 * channels * channels * rows * planes * cells
-    padded = (rows + 4, planes + 2, channels, cells)
+    padded = (rows + 2, planes + 2, channels, cells)
+    plane = shape((rows, cells, channels), BF16)
     slope, x_first = call(
         functools.partial(forward_kernel, chan_count),
-        [shape((rows + 2, planes, cells, channels), F32), shape(padded, BF16)],
-        [pltpu.VMEM((rows + 4, planes + 2, cells, channels), BF16)],
-        2 * macs * (rows + 2) // rows,
+        [shape((rows, planes, cells, channels), F32), shape(padded, BF16)],
+        [pltpu.VMEM((rows + 2, planes + 2, cells, channels), BF16)],
+        0,
         [*x_pieces, x_low, x_high, weights_f],
         z_arg,
     )
     grad, g_bottom, g_top = call(
         functools.partial(grad_out_kernel, chan_count),
-        [shape((rows + 2, planes, cells, channels), BF16)]
-        + [shape((rows + 2, cells, channels), BF16)] * 2,
+        [shape((rows, planes, cells, channels), BF16), plane, plane],
         [pltpu.VMEM((planes, channels, cells), BF16)],
         10 * rows * planes * cells * channels,
         [*c_pieces, slope],
@@ -264,38 +341,59 @@
             pltpu.VMEM((9 * channels, 3 * channels), F32),
             pltpu.VMEM((chan_count, space_count * shard, channels), F32),
         ],
-        2 * macs,
+        6 * macs,
         [x_first, grad],
         lax.rem(s, 2).reshape(1),
     )
     from_core = lax.ppermute(send, "space", [(i, i ^ 1) for i in range(space_count)])
-
-    back = call(
-        functools.partial(input_kernel, chan_count),
-        [shape((rows, planes, group, cells), BF16)] * chan_count,
+    pair_sum = keep + from_core
+    edges = [
+        jnp.concatenate([g_low[r : r + 1], grad[r], g_high[r : r + 1]], axis=0)
+        for r in (rows - 1, 0)
+    ]
+    g_up = lax.ppermute(edges[0], "chan", ring(chan_count, 1))
+    g_down = lax.ppermute(edges[1], "chan", ring(chan_count, -1))
+    chip = s // 2
+    chip_sum = lax.dynamic_index_in_dim(pair_sum, chip, 0, keepdims=False)
+    rounded = pair_sum.astype(BF16)
+    from_chips = []
+    for k in range(1, chips):
+        block = lax.dynamic_index_in_dim(rounded, chip ^ k, 0, keepdims=False)
+        from_chips.append(
+            lax.ppermute(block, "space", [(i, i ^ (2 * k)) for i in range(space_count)])
+        )
+    g_low, g_high = after((g_low, g_high), rounded)
+    inner = call(
+        functools.partial(inner_kernel, chan_count),
+        [shape((rows - 2, planes, group, cells), BF16)] * chan_count,
         [pltpu.VMEM((planes, channels, cells), BF16)],
-        2 * macs,
+        5 * macs,
         [grad, g_low, g_high, weights_b],
         z_arg,
     )
-    returned = exchange(back, "chan")
-
-    pair_sum = keep + from_core
-    chip = s // 2
-    own = lax.dynamic_index_in_dim(pair_sum, chip, 0, keepdims=False)
-    rounded = pair_sum.astype(BF16)
-    chip_sum = own
-    for k in range(1, chips):
-        block = lax.dynamic_index_in_dim(rounded, chip ^ k, 0, keepdims=False)
-        got = lax.ppermute(block, "space", [(i, i ^ (2 * k)) for i in range(space_count)])
+    g_up, g_down, from_chips = after((g_up, g_down, from_chips), inner[0])
+    for got in from_chips:
         chip_sum = chip_sum + got.astype(F32)
     parts = [
         lax.dynamic_index_in_dim(chip_sum, lax.rem(z + j, chan_count), 0, keepdims=False)
         for j in range(chan_count)
     ]
-    shard_sum = sum(exchange(parts, "chan"))
+    g_up, g_down = after((g_up, g_down), parts)
+    back = call(
+        functools.partial(edge_kernel, chan_count),
+        [shape((rows, planes, group, cells), BF16)] * chan_count,
+        [pltpu.VMEM((planes, channels, cells), BF16)],
+        2 * macs,
+        [grad, g_low, g_high, g_up, g_down, weights_b, *inner],
+        z_arg,
+    )
+    returned = exchange(back, "chan")
+
+    summed = exchange(parts, "chan")
+    shard_sum = sum(after(summed, back[0]))
     cell_total = planes * space_count * height * cells
     shard_sum = shard_sum * (1.0 / math.sqrt(cell_total))
+    returned = after(returned, shard_sum)
     whole = lax.all_gather(shard_sum, "space", axis=0, tiled=True)
     grad_w = whole[: 27 * group].reshape(27, group, channels)
 

time: 194 us -> 141 us (0.73)
  the two profiles are of different devices: /device:TPU:0 before, /device:TPU:11 now
where the time goes in v2:
time: 141 us; the launch traced here: 140 us
  waiting for transfers between devices  37.7 us (27%)
  Pallas kernels  37.5 us (27%)
  starting transfers between devices  25.5 us (18%)
  blocking collectives  22.8 us (16%)
  local copies, waits for them, and re-layouts  14.5 us (10%)
    pallas_call x5, Pallas kernels, call(): pl.pallas_call(kernel, out_shape=outs, in_specs=[pl.BlockSpec(memory_spac...  37.5 us
    ppermute x12, waiting for transfers between devices, exchange(): lax.ppermute(blocks[j], axis, ring(count, j))  31.3 us
    all_gather x1, blocking collectives, gather_filters(): whole = lax.all_gather(shares, 'space', axis=1, tiled=True)  12.9 us
    ppermute x12, starting transfers between devices, exchange(): lax.ppermute(blocks[j], axis, ring(count, j))  11.8 us
    all_gather x1, blocking collectives, body(): whole = lax.all_gather(shard_sum, 'space', axis=0, tiled=True)  9.89 us
    unnamed x54, local copies, waits for them, and re-layouts  7.22 us
    ppermute x1, waiting for transfers between devices, body(): g_high = lax.ppermute(g_bottom, 'space', downward)  5.22 us
    ppermute x3, starting transfers between devices, gather_filters(): lax.ppermute(mine, 'chan', ring(chan_count, j))  4.67 us
  transfers between devices with their start and end apart: 25, of which 8 were waited for; matrix products, arithmetic and copies ran while one was open for 8% of the time, Pallas kernels for 24%

profile of v2, /device:TPU:11, one launch (start us, length us, event | category | flops | bytes accessed | tf_op | source)
XLA Modules:
  0.0 140.2 jit_solution(9748602112191693656)
XLA Ops:
  0.6 0.8 pad_dynamic-slice_fusion.6
  1.4 0.2 collective-permute-start.1
  1.6 2.3 %collective-permute-start.2 = (bf16[112,128]{1,0:T(8,128)(2,1)S(1)}, bf16[112,128]{1,0:T(8,128)(2,1)S(1)}, u32[]{:S(2)}, u32[]{:S(2)}) collective-permute-start(bf16[112,128]{1,0:T(8,128)(2,1)S(1)} %pad_dynamic-slice_fusion.6), channel_id=1, source_target_pairs={{0,2},{1,3},{2,0},{3,1},{4,6},{5,7},{6,4},{7,5},{8,10},{9,11},{10,... | collective-permute-start | bytes 86024 | tf_op jit(solution)/shard_map/ppermute | solution.py:268
  3.9 2.2 %collective-permute-start.3 = (bf16[112,128]{1,0:T(8,128)(2,1)S(1)}, bf16[112,128]{1,0:T(8,128)(2,1)S(1)}, u32[]{:S(2)}, u32[]{:S(2)}) collective-permute-start(bf16[112,128]{1,0:T(8,128)(2,1)S(1)} %pad_dynamic-slice_fusion.6), channel_id=1, source_target_pairs={{0,1},{1,2},{2,3},{3,0},{4,5},{5,6},{6,7},{7,4},{8,9},{9,10},{10,1... | collective-permute-start | bytes 86024 | tf_op jit(solution)/shard_map/ppermute | solution.py:268
  6.1 1.9 %copy.35 = bf16[32,4,32,128]{3,0,1,2:T(8,128)(2,1)S(1)} copy(bf16[32,4,32,128]{3,2,1,0:T(8,128)(2,1)} %param.3) | data formatting | bytes 2097152 | tf_op args[0]
  8.0 1.0 pad_dynamic-slice_fusion.2
  9.0 1.3 collective-permute-start.5
  10.4 1.1 collective-permute-start.7
  11.7 12.9 %all_gather.6 = bf16[4,896,128]{2,1,0:T(8,128)(2,1)S(1)} all-gather(bf16[4,112,128]{2,1,0:T(8,128)(2,1)S(1)} %constant_dynamic-slice_fusion.2), channel_id=1, replica_groups=mesh['space'=8,'chan'=4] {'space'}, dimensions={1}, use_global_device_ids=true | all-gather | bytes 1032192 | tf_op jit(solution)/shard_map/all_gather | solution.py:272
  24.6 0.6 copy.15
  25.3 1.1 copy.37
  26.3 9.5 %collective-permute-done.5.refs_2_ = bf16[10,4,32,128]{3,2,1,0:T(8,128)(2,1)S(1)} collective-permute-done((bf16[10,4,32,128]{3,2,1,0:T(8,128)(2,1)S(1)}, bf16[10,4,32,128]{3,2,1,0:T(8,128)(2,1)S(1)}, u32[]{:S(2)}, u32[]{:S(2)}) %collective-permute-start.5) | collective-permute-done | bytes 327712 | tf_op jit(solution)/shard_map/ppermute | solution.py:253
  35.9 3.8 %collective-permute-done.7.refs_3_ = bf16[10,4,32,128]{3,2,1,0:T(8,128)(2,1)S(1)} collective-permute-done((bf16[10,4,32,128]{3,2,1,0:T(8,128)(2,1)S(1)}, bf16[10,4,32,128]{3,2,1,0:T(8,128)(2,1)S(1)}, u32[]{:S(2)}, u32[]{:S(2)}) %collective-permute-start.7) | collective-permute-done | bytes 327712 | tf_op jit(solution)/shard_map/ppermute | solution.py:253
  39.7 0.5 collective-permute-start.10
  40.2 0.8 pad_maximum_fusion
  41.0 2.2 %collective-permute-start.9 = (bf16[10,1,128,128]{3,2,1,0:T(8,128)(2,1)}, bf16[10,1,128,128]{3,2,1,0:T(8,128)(2,1)S(1)}, u32[]{:S(2)}, u32[]{:S(2)}) collective-permute-start(bf16[10,1,128,128]{3,2,1,0:T(8,128)(2,1)} %pad_maximum_fusion), channel_id=1, source_target_pairs={{0,4},{4,8},{8,12},{12,16},{16,20},{20,24},{24,28},{28,0},{1,5},{5... | collective-permute-start | bytes 983048 | tf_op jit(solution)/shard_map/ppermute | solution.py:305
  43.1 0.2 constant_dynamic-slice_fusion
  43.9 1.4 collective-permute-start.8
  45.3 0.8 copy.41
  46.1 0.7 stack.58.z_ref
  46.7 0.5 copy.18
  47.2 0.3 copy.36
  47.5 1.4 copy.19.weights_ref
  48.8 1.1 collective-permute-done.10.refs_5_
  50.0 0.7 copy-done.7
  50.8 11.4 %shard_map.50 = (f32[8,4,128,128]{3,2,1,0:T(8,128)}, bf16[10,6,128,128]{3,2,1,0:T(8,128)(2,1)}) custom-call(s32[5]{0:T(128)} %stack.58.z_ref, bf16[10,4,32,128]{3,2,1,0:T(8,128)(2,1)} %get-tuple-element.84.refs_0_, bf16[10,4,32,128]{3,2,1,0:T(8,128)(2,1)} %copy-done.4, bf16[10,4,32,128]{3,2,1,0:T(8,128)(2,1)} %copy-done.5, ...), custom_call_target="tpu_custom_call" | custom-call | tf_op jit(solution)/shard_map/pallas_call | solution.py:227
  62.2 3.1 %collective-permute-done.6.refs_2_ = bf16[8,4,32,128]{3,2,1,0:T(8,128)(2,1)S(1)} collective-permute-done((bf16[8,4,32,128]{3,2,1,0:T(8,128)(2,1)S(1)}, bf16[8,4,32,128]{3,2,1,0:T(8,128)(2,1)S(1)}, u32[]{:S(2)}, u32[]{:S(2)}) %collective-permute-start.6) | collective-permute-done | bytes 262176 | tf_op jit(solution)/shard_map/ppermute | solution.py:253
  65.3 1.8 %collective-permute-done.8.refs_3_ = bf16[8,4,32,128]{3,2,1,0:T(8,128)(2,1)} collective-permute-done((bf16[8,4,32,128]{3,2,1,0:T(8,128)(2,1)S(1)}, bf16[8,4,32,128]{3,2,1,0:T(8,128)(2,1)}, u32[]{:S(2)}, u32[]{:S(2)}) %collective-permute-start.8) | collective-permute-done | bytes 262176 | tf_op jit(solution)/shard_map/ppermute | solution.py:253
  67.1 3.9 %shard_map.51 = (bf16[8,4,128,128]{3,2,1,0:T(8,128)(2,1)}, bf16[8,128,128]{2,1,0:T(8,128)(2,1)}, bf16[8,128,128]{2,1,0:T(8,128)(2,1)}) custom-call(s32[5]{0:T(128)} %stack.58.z_ref, bf16[8,4,32,128]{3,2,1,0:T(8,128)(2,1)} %bitcast.89, bf16[8,4,32,128]{3,2,1,0:T(8,128)(2,1)} %copy-done.9, bf16[8,4,32,128]{3,2,1,0:T(8,128)(2,1)} %copy-done.10, ...), custom_call_target="tpu_custom_call" | custom-call | flops 5242880 | bytes 4718592 | tf_op jit(solution)/shard_map/pallas_call | solution.py:227
  71.0 1.6 %collective-permute-start.11 = (bf16[8,128,128]{2,1,0:T(8,128)(2,1)}, bf16[8,128,128]{2,1,0:T(8,128)(2,1)S(1)}, u32[]{:S(2)}, u32[]{:S(2)}) collective-permute-start(bf16[8,128,128]{2,1,0:T(8,128)(2,1)} %get-tuple-element.44), channel_id=1, source_target_pairs={{0,4},{4,8},{8,12},{12,16},{16,20},{20,24},{24,28},{28,0},{1,5},{5... | collective-permute-start | bytes 786440 | tf_op jit(solution)/shard_map/ppermute | solution.py:331
  72.6 9.7 %shard_map.52 = (f32[4,4,112,128]{3,2,1,0:T(8,128)}, f32[4,4,112,128]{3,2,1,0:T(8,128)}) custom-call(s32[1]{0:T(128)} %bitcast.17.core_ref, bf16[10,6,128,128]{3,2,1,0:T(8,128)(2,1)} %get-tuple-element.46.x_ref, bf16[8,4,128,128]{3,2,1,0:T(8,128)(2,1)} %get-tuple-element.43.grad_ref), custom_call_target="tpu_custom_call" | custom-call | flops 10871635968 | bytes 4849664 | tf_op jit(solution)/shard_map/pallas_call | solution.py:227
  82.3 0.5 collective-permute-start.12
  82.8 1.0 slice_bitcast_fusion
  83.9 5.2 %collective-permute-done.12.high_ref = bf16[8,128,128]{2,1,0:T(8,128)(2,1)S(1)} collective-permute-done((bf16[8,128,128]{2,1,0:T(8,128)(2,1)S(1)}, bf16[8,128,128]{2,1,0:T(8,128)(2,1)S(1)}, u32[]{:S(2)}, u32[]{:S(2)}) %collective-permute-start.12) | collective-permute-done | bytes 262176 | tf_op jit(solution)/shard_map/ppermute | solution.py:332
  89.2 1.5 %collective-permute-start.14 = (bf16[6,128,128]{2,1,0:T(8,128)(2,1)S(1)}, bf16[6,128,128]{2,1,0:T(8,128)(2,1)S(1)}, u32[]{:S(2)}, u32[]{:S(2)}) collective-permute-start(bf16[6,128,128]{2,1,0:T(8,128)(2,1)S(1)} %pad_maximum_fusion.2), channel_id=1, source_target_pairs={{0,1},{1,2},{2,3},{3,0},{4,5},{5,6},{6,7},{7,4},{8,9},{9,10},{10,1... | collective-permute-start | bytes 589832 | tf_op jit(solution)/shard_map/ppermute | solution.py:354
  91.0 0.3 collective-permute-start.17
  91.3 2.3 %collective-permute-start.18 = (bf16[4,112,128]{2,1,0:T(8,128)(2,1)S(1)}, bf16[4,112,128]{2,1,0:T(8,128)(2,1)S(1)}, u32[]{:S(2)}, u32[]{:S(2)}) collective-permute-start(bf16[4,112,128]{2,1,0:T(8,128)(2,1)S(1)} %get-tuple-element.92), channel_id=1, source_target_pairs={{0,24},{4,28},{8,16},{12,20},{16,8},{20,12},{24,0},{28,4},{1,25},{... | collective-permute-start | bytes 344072 | tf_op jit(solution)/shard_map/ppermute | solution.py:363
  93.7 7.9 %shard_map.53 = (bf16[6,4,32,128]{3,2,1,0:T(8,128)(2,1)}, bf16[6,4,32,128]{3,2,1,0:T(8,128)(2,1)}, bf16[6,4,32,128]{3,2,1,0:T(8,128)(2,1)}, bf16[6,4,32,128]{3,2,1,0:T(8,128)(2,1)}) custom-call(s32[5]{0:T(128)} %stack.58.z_ref, bf16[8,4,128,128]{3,2,1,0:T(8,128)(2,1)} %get-tuple-element.43.grad_ref, bf16[8,128,128]{2,1,0:T(8,128)(2,1)} %copy-done.11, ...), custom_call_target="tpu_custom_call" | custom-call | flops 9059696640 | bytes 3244032 | tf_op jit(solution)/shard_map/pallas_call | solution.py:227
  101.7 1.3 collective-permute-start.22
  103.0 3.0 %collective-permute-start.23 = (f32[112,128]{1,0:T(8,128)S(1)}, f32[112,128]{1,0:T(8,128)S(1)}, u32[]{:S(2)}, u32[]{:S(2)}) collective-permute-start(f32[112,128]{1,0:T(8,128)S(1)} %get-tuple-element.106), channel_id=1, source_target_pairs={{0,2},{1,3},{2,0},{3,1},{4,6},{5,7},{6,4},{7,5},{8,10},{9,11},{10,... | collective-permute-start | bytes 172040 | tf_op jit(solution)/shard_map/ppermute | solution.py:253
  106.1 1.4 collective-permute-start.24
  107.5 4.6 %shard_map.54 = (bf16[8,4,32,128]{3,2,1,0:T(8,128)(2,1)}, bf16[8,4,32,128]{3,2,1,0:T(8,128)(2,1)}, bf16[8,4,32,128]{3,2,1,0:T(8,128)(2,1)}, bf16[8,4,32,128]{3,2,1,0:T(8,128)(2,1)}) custom-call(s32[5]{0:T(128)} %stack.58.z_ref, bf16[8,4,128,128]{3,2,1,0:T(8,128)(2,1)} %get-tuple-element.43.grad_ref, bf16[8,128,128]{2,1,0:T(8,128)(2,1)} %copy-done.11, ...), custom_call_target="tpu_custom_call" | custom-call | flops 3623878656 | bytes 4685824 | tf_op jit(solution)/shard_map/pallas_call | solution.py:227
  112.1 2.0 %collective-permute-start.20 = (bf16[8,4,32,128]{3,2,1,0:T(8,128)(2,1)}, bf16[8,4,32,128]{3,2,1,0:T(8,128)(2,1)S(1)}, u32[]{:S(2)}, u32[]{:S(2)}) collective-permute-start(bf16[8,4,32,128]{3,2,1,0:T(8,128)(2,1)} %get-tuple-element.64), channel_id=1, source_target_pairs={{0,2},{1,3},{2,0},{3,1},{4,6},{5,7},{6,4},{7,5},{8,10},{9,11},{10,... | collective-permute-start | bytes 786440 | tf_op jit(solution)/shard_map/ppermute | solution.py:253
  114.2 9.9 %all_gather.7 = f32[896,128]{1,0:T(8,128)S(1)} all-gather(f32[112,128]{1,0:T(8,128)S(1)} %add_multiply_fusion), channel_id=1, replica_groups=mesh['space'=8,'chan'=4] {'space'}, dimensions={0}, use_global_device_ids=true | all-gather | bytes 516096 | tf_op jit(solution)/shard_map/all_gather | solution.py:397
  124.1 0.8 slice.73
  124.9 10.5 %collective-permute-done.20 = bf16[8,4,32,128]{3,2,1,0:T(8,128)(2,1)S(1)} collective-permute-done((bf16[8,4,32,128]{3,2,1,0:T(8,128)(2,1)}, bf16[8,4,32,128]{3,2,1,0:T(8,128)(2,1)S(1)}, u32[]{:S(2)}, u32[]{:S(2)}) %collective-permute-start.20) | collective-permute-done | bytes 262176 | tf_op jit(solution)/shard_map/ppermute | solution.py:253
  135.4 2.7 %collective-permute-done.21 = bf16[8,4,32,128]{3,2,1,0:T(8,128)(2,1)S(1)} collective-permute-done((bf16[8,4,32,128]{3,2,1,0:T(8,128)(2,1)}, bf16[8,4,32,128]{3,2,1,0:T(8,128)(2,1)S(1)}, u32[]{:S(2)}, u32[]{:S(2)}) %collective-permute-start.21) | collective-permute-done | bytes 262176 | tf_op jit(solution)/shard_map/ppermute | solution.py:253
  138.5 1.7 %copy.21 = bf16[32,4,32,128]{3,2,1,0:T(8,128)(2,1)} copy(bf16[32,4,32,128]{3,0,1,2:T(8,128)(2,1)S(1)} %dynamic-slice_bitcast_fusion) | data formatting | bytes 2097152
  (92 shorter events, 1.9 us)
Async XLA Ops:
  1.4 9.0 %collective-permute-start.1 = (bf16[112,128]{1,0:T(8,128)(2,1)S(1)}, bf16[112,128]{1,0:T(8,128)(2,1)S(1)}, u32[]{:S(2)}, u32[]{:S(2)}) collective-permute-start(bf16[112,128]{1,0:T(8,128)(2,1)S(1)} %pad_dynamic-slice_fusion.6), channel_id=1, source_target_pairs={{0,3},{1,0},{2,1},{3,2},{4,7},{5,4},{6,5},{7,6},{8,11},{9,8},{10,9... | collective-permute-start | bytes 86024 | tf_op jit(solution)/shard_map/ppermute | solution.py:268
  1.6 9.9 %collective-permute-start.2 = (bf16[112,128]{1,0:T(8,128)(2,1)S(1)}, bf16[112,128]{1,0:T(8,128)(2,1)S(1)}, u32[]{:S(2)}, u32[]{:S(2)}) collective-permute-start(bf16[112,128]{1,0:T(8,128)(2,1)S(1)} %pad_dynamic-slice_fusion.6), channel_id=1, source_target_pairs={{0,2},{1,3},{2,0},{3,1},{4,6},{5,7},{6,4},{7,5},{8,10},{9,11},{10,... | collective-permute-start | bytes 86024 | tf_op jit(solution)/shard_map/ppermute | solution.py:268
  3.9 7.6 %collective-permute-start.3 = (bf16[112,128]{1,0:T(8,128)(2,1)S(1)}, bf16[112,128]{1,0:T(8,128)(2,1)S(1)}, u32[]{:S(2)}, u32[]{:S(2)}) collective-permute-start(bf16[112,128]{1,0:T(8,128)(2,1)S(1)} %pad_dynamic-slice_fusion.6), channel_id=1, source_target_pairs={{0,1},{1,2},{2,3},{3,0},{4,5},{5,6},{6,7},{7,4},{8,9},{9,10},{10,1... | collective-permute-start | bytes 86024 | tf_op jit(solution)/shard_map/ppermute | solution.py:268
  8.0 3.6 %copy-start = (bf16[27,32,128]{2,1,0:T(8,128)(2,1)S(1)}, bf16[27,32,128]{2,1,0:T(8,128)(2,1)}, u32[]{:S(2)}) copy-start(bf16[27,32,128]{2,1,0:T(8,128)(2,1)} %param.4) | copy-start | bytes 663556
  9.0 17.3 %collective-permute-start = (bf16[10,4,32,128]{3,2,1,0:T(8,128)(2,1)S(1)}, bf16[10,4,32,128]{3,2,1,0:T(8,128)(2,1)S(1)}, u32[]{:S(2)}, u32[]{:S(2)}) collective-permute-start(bf16[10,4,32,128]{3,2,1,0:T(8,128)(2,1)S(1)} %get-tuple-element.87), channel_id=1, source_target_pairs={{0,1},{1,2},{2,3},{3,0},{4,5},{5,6},{6,7},{7,4},{8,9},{9,10},{10,1... | collective-permute-start | bytes 983048 | tf_op jit(solution)/shard_map/ppermute | solution.py:253
  9.0 26.8 %collective-permute-start.5 = (bf16[10,4,32,128]{3,2,1,0:T(8,128)(2,1)S(1)}, bf16[10,4,32,128]{3,2,1,0:T(8,128)(2,1)S(1)}, u32[]{:S(2)}, u32[]{:S(2)}) collective-permute-start(bf16[10,4,32,128]{3,2,1,0:T(8,128)(2,1)S(1)} %get-tuple-element.85), channel_id=1, source_target_pairs={{0,2},{1,3},{2,0},{3,1},{4,6},{5,7},{6,4},{7,5},{8,10},{9,11},{10,... | collective-permute-start | bytes 983048 | tf_op jit(solution)/shard_map/ppermute | solution.py:253
  10.4 29.2 %collective-permute-start.7 = (bf16[10,4,32,128]{3,2,1,0:T(8,128)(2,1)S(1)}, bf16[10,4,32,128]{3,2,1,0:T(8,128)(2,1)S(1)}, u32[]{:S(2)}, u32[]{:S(2)}) collective-permute-start(bf16[10,4,32,128]{3,2,1,0:T(8,128)(2,1)S(1)} %get-tuple-element.86), channel_id=1, source_target_pairs={{0,3},{1,0},{2,1},{3,2},{4,7},{5,4},{6,5},{7,6},{8,11},{9,8},{10,9... | collective-permute-start | bytes 983048 | tf_op jit(solution)/shard_map/ppermute | solution.py:253
  25.3 17.9 %copy-start.1 = (bf16[32,4,32,128]{3,2,1,0:T(8,128)(2,1)S(1)}, bf16[32,4,32,128]{3,2,1,0:T(8,128)(2,1)}, u32[]{:S(2)}) copy-start(bf16[32,4,32,128]{3,2,1,0:T(8,128)(2,1)} %param.5) | copy-start | bytes 3145732
  26.3 17.0 %copy-start.4 = (bf16[10,4,32,128]{3,2,1,0:T(8,128)(2,1)}, bf16[10,4,32,128]{3,2,1,0:T(8,128)(2,1)S(1)}, u32[]{:S(2)}) copy-start(bf16[10,4,32,128]{3,2,1,0:T(8,128)(2,1)S(1)} %collective-permute-done.refs_1_) | copy-start | bytes 983044
  35.8 7.6 %copy-start.5 = (bf16[10,4,32,128]{3,2,1,0:T(8,128)(2,1)}, bf16[10,4,32,128]{3,2,1,0:T(8,128)(2,1)S(1)}, u32[]{:S(2)}) copy-start(bf16[10,4,32,128]{3,2,1,0:T(8,128)(2,1)S(1)} %collective-permute-done.5.refs_2_) | copy-start | bytes 983044
  39.6 3.9 %copy-start.6 = (bf16[10,4,32,128]{3,2,1,0:T(8,128)(2,1)}, bf16[10,4,32,128]{3,2,1,0:T(8,128)(2,1)S(1)}, u32[]{:S(2)}) copy-start(bf16[10,4,32,128]{3,2,1,0:T(8,128)(2,1)S(1)} %collective-permute-done.7.refs_3_) | copy-start | bytes 983044
  39.7 10.3 %collective-permute-start.10 = (bf16[10,1,128,128]{3,2,1,0:T(8,128)(2,1)S(1)}, bf16[10,1,128,128]{3,2,1,0:T(8,128)(2,1)S(1)}, u32[]{:S(2)}, u32[]{:S(2)}) collective-permute-start(bf16[10,1,128,128]{3,2,1,0:T(8,128)(2,1)S(1)} %pad_maximum_fusion.1), channel_id=1, source_target_pairs={{0,28},{4,0},{8,4},{12,8},{16,12},{20,16},{24,20},{28,24},{1,29},{... | collective-permute-start | bytes 983048 | tf_op jit(solution)/shard_map/ppermute | solution.py:306
  41.0 9.0 %collective-permute-start.9 = (bf16[10,1,128,128]{3,2,1,0:T(8,128)(2,1)}, bf16[10,1,128,128]{3,2,1,0:T(8,128)(2,1)S(1)}, u32[]{:S(2)}, u32[]{:S(2)}) collective-permute-start(bf16[10,1,128,128]{3,2,1,0:T(8,128)(2,1)} %pad_maximum_fusion), channel_id=1, source_target_pairs={{0,4},{4,8},{8,12},{12,16},{16,20},{20,24},{24,28},{28,0},{1,5},{5... | collective-permute-start | bytes 983048 | tf_op jit(solution)/shard_map/ppermute | solution.py:305
  43.7 18.5 %collective-permute-start.4 = (bf16[8,4,32,128]{3,2,1,0:T(8,128)(2,1)S(1)}, bf16[8,4,32,128]{3,2,1,0:T(8,128)(2,1)S(1)}, u32[]{:S(2)}, u32[]{:S(2)}) collective-permute-start(bf16[8,4,32,128]{3,2,1,0:T(8,128)(2,1)S(1)} %bitcast.93), channel_id=1, source_target_pairs={{0,1},{1,2},{2,3},{3,0},{4,5},{5,6},{6,7},{7,4},{8,9},{9,10},{10,1... | collective-permute-start | bytes 786440 | tf_op jit(solution)/shard_map/ppermute | solution.py:253
  43.8 21.5 %collective-permute-start.6 = (bf16[8,4,32,128]{3,2,1,0:T(8,128)(2,1)S(1)}, bf16[8,4,32,128]{3,2,1,0:T(8,128)(2,1)S(1)}, u32[]{:S(2)}, u32[]{:S(2)}) collective-permute-start(bf16[8,4,32,128]{3,2,1,0:T(8,128)(2,1)S(1)} %bitcast.92), channel_id=1, source_target_pairs={{0,2},{1,3},{2,0},{3,1},{4,6},{5,7},{6,4},{7,5},{8,10},{9,11},{10,... | collective-permute-start | bytes 786440 | tf_op jit(solution)/shard_map/ppermute | solution.py:253
  43.9 23.2 %collective-permute-start.8 = (bf16[8,4,32,128]{3,2,1,0:T(8,128)(2,1)S(1)}, bf16[8,4,32,128]{3,2,1,0:T(8,128)(2,1)}, u32[]{:S(2)}, u32[]{:S(2)}) collective-permute-start(bf16[8,4,32,128]{3,2,1,0:T(8,128)(2,1)S(1)} %bitcast.91), channel_id=1, source_target_pairs={{0,3},{1,0},{2,1},{3,2},{4,7},{5,4},{6,5},{7,6},{8,11},{9,8},{10,9... | collective-permute-start | bytes 786440 | tf_op jit(solution)/shard_map/ppermute | solution.py:253
  50.0 0.7 copy-start.7
  50.0 0.8 copy-start.8
  62.2 4.9 %copy-start.9 = (bf16[8,4,32,128]{3,2,1,0:T(8,128)(2,1)}, bf16[8,4,32,128]{3,2,1,0:T(8,128)(2,1)S(1)}, u32[]{:S(2)}) copy-start(bf16[8,4,32,128]{3,2,1,0:T(8,128)(2,1)S(1)} %collective-permute-done.4.refs_1_) | copy-start | bytes 786436
  65.3 1.8 %copy-start.10 = (bf16[8,4,32,128]{3,2,1,0:T(8,128)(2,1)}, bf16[8,4,32,128]{3,2,1,0:T(8,128)(2,1)S(1)}, u32[]{:S(2)}) copy-start(bf16[8,4,32,128]{3,2,1,0:T(8,128)(2,1)S(1)} %collective-permute-done.6.refs_2_) | copy-start | bytes 786436
  71.0 12.8 %collective-permute-start.11 = (bf16[8,128,128]{2,1,0:T(8,128)(2,1)}, bf16[8,128,128]{2,1,0:T(8,128)(2,1)S(1)}, u32[]{:S(2)}, u32[]{:S(2)}) collective-permute-start(bf16[8,128,128]{2,1,0:T(8,128)(2,1)} %get-tuple-element.44), channel_id=1, source_target_pairs={{0,4},{4,8},{8,12},{12,16},{16,20},{20,24},{24,28},{28,0},{1,5},{5... | collective-permute-start | bytes 786440 | tf_op jit(solution)/shard_map/ppermute | solution.py:331
  72.6 9.7 %copy-start.13 = (bf16[8,128,128]{2,1,0:T(8,128)(2,1)S(1)}, bf16[8,128,128]{2,1,0:T(8,128)(2,1)}, u32[]{:S(2)}) copy-start(bf16[8,128,128]{2,1,0:T(8,128)(2,1)} %get-tuple-element.45) | copy-start | bytes 786436
  82.3 8.4 %copy-start.3 = (f32[4,4,112,128]{3,2,1,0:T(8,128)S(1)}, f32[4,4,112,128]{3,2,1,0:T(8,128)}, u32[]{:S(2)}) copy-start(f32[4,4,112,128]{3,2,1,0:T(8,128)} %get-tuple-element.47) | copy-start | bytes 2752516
  82.3 8.4 %collective-permute-start.13 = (f32[4,4,112,128]{3,2,1,0:T(8,128)}, f32[4,4,112,128]{3,2,1,0:T(8,128)S(1)}, u32[]{:S(2)}, u32[]{:S(2)}) collective-permute-start(f32[4,4,112,128]{3,2,1,0:T(8,128)} %get-tuple-element.48), channel_id=1, source_target_pairs={{0,4},{4,0},{8,12},{12,8},{16,20},{20,16},{24,28},{28,24},{1,5},{5... | collective-permute-start | bytes 2752520 | tf_op jit(solution)/shard_map/ppermute | solution.py:348
  82.3 6.7 %collective-permute-start.12 = (bf16[8,128,128]{2,1,0:T(8,128)(2,1)S(1)}, bf16[8,128,128]{2,1,0:T(8,128)(2,1)S(1)}, u32[]{:S(2)}, u32[]{:S(2)}) collective-permute-start(bf16[8,128,128]{2,1,0:T(8,128)(2,1)S(1)} %copy-done.13), channel_id=1, source_target_pairs={{0,28},{4,0},{8,4},{12,8},{16,12},{20,16},{24,20},{28,24},{1,29},{... | collective-permute-start | bytes 786440 | tf_op jit(solution)/shard_map/ppermute | solution.py:332
  83.8 7.0 %copy-start.11 = (bf16[8,128,128]{2,1,0:T(8,128)(2,1)}, bf16[8,128,128]{2,1,0:T(8,128)(2,1)S(1)}, u32[]{:S(2)}) copy-start(bf16[8,128,128]{2,1,0:T(8,128)(2,1)S(1)} %collective-permute-done.11.low_ref) | copy-start | bytes 786436
  89.1 1.9 %copy-start.12 = (bf16[8,128,128]{2,1,0:T(8,128)(2,1)}, bf16[8,128,128]{2,1,0:T(8,128)(2,1)S(1)}, u32[]{:S(2)}) copy-start(bf16[8,128,128]{2,1,0:T(8,128)(2,1)S(1)} %collective-permute-done.12.high_ref) | copy-start | bytes 786436
  89.1 12.4 %collective-permute-start.15 = (bf16[6,128,128]{2,1,0:T(8,128)(2,1)S(1)}, bf16[6,128,128]{2,1,0:T(8,128)(2,1)S(1)}, u32[]{:S(2)}, u32[]{:S(2)}) collective-permute-start(bf16[6,128,128]{2,1,0:T(8,128)(2,1)S(1)} %pad_maximum_fusion.3), channel_id=1, source_target_pairs={{0,3},{1,0},{2,1},{3,2},{4,7},{5,4},{6,5},{7,6},{8,11},{9,8},{10,9... | collective-permute-start | bytes 589832 | tf_op jit(solution)/shard_map/ppermute | solution.py:355
  89.2 12.3 %collective-permute-start.14 = (bf16[6,128,128]{2,1,0:T(8,128)(2,1)S(1)}, bf16[6,128,128]{2,1,0:T(8,128)(2,1)S(1)}, u32[]{:S(2)}, u32[]{:S(2)}) collective-permute-start(bf16[6,128,128]{2,1,0:T(8,128)(2,1)S(1)} %pad_maximum_fusion.2), channel_id=1, source_target_pairs={{0,1},{1,2},{2,3},{3,0},{4,5},{5,6},{6,7},{7,4},{8,9},{9,10},{10,1... | collective-permute-start | bytes 589832 | tf_op jit(solution)/shard_map/ppermute | solution.py:354
  91.0 10.6 %collective-permute-start.16 = (bf16[4,112,128]{2,1,0:T(8,128)(2,1)S(1)}, bf16[4,112,128]{2,1,0:T(8,128)(2,1)S(1)}, u32[]{:S(2)}, u32[]{:S(2)}) collective-permute-start(bf16[4,112,128]{2,1,0:T(8,128)(2,1)S(1)} %get-tuple-element.94), channel_id=1, source_target_pairs={{0,8},{4,12},{8,0},{12,4},{16,24},{20,28},{24,16},{28,20},{1,9},{5... | collective-permute-start | bytes 344072 | tf_op jit(solution)/shard_map/ppermute | solution.py:363
  91.0 10.6 %collective-permute-start.17 = (bf16[4,112,128]{2,1,0:T(8,128)(2,1)S(1)}, bf16[4,112,128]{2,1,0:T(8,128)(2,1)S(1)}, u32[]{:S(2)}, u32[]{:S(2)}) collective-permute-start(bf16[4,112,128]{2,1,0:T(8,128)(2,1)S(1)} %get-tuple-element.93), channel_id=1, source_target_pairs={{0,16},{4,20},{8,24},{12,28},{16,0},{20,4},{24,8},{28,12},{1,17},{... | collective-permute-start | bytes 344072 | tf_op jit(solution)/shard_map/ppermute | solution.py:363
  91.3 10.3 %collective-permute-start.18 = (bf16[4,112,128]{2,1,0:T(8,128)(2,1)S(1)}, bf16[4,112,128]{2,1,0:T(8,128)(2,1)S(1)}, u32[]{:S(2)}, u32[]{:S(2)}) collective-permute-start(bf16[4,112,128]{2,1,0:T(8,128)(2,1)S(1)} %get-tuple-element.92), channel_id=1, source_target_pairs={{0,24},{4,28},{8,16},{12,20},{16,8},{20,12},{24,0},{28,4},{1,25},{... | collective-permute-start | bytes 344072 | tf_op jit(solution)/shard_map/ppermute | solution.py:363
  101.5 5.9 %copy-start.14 = (bf16[6,128,128]{2,1,0:T(8,128)(2,1)}, bf16[6,128,128]{2,1,0:T(8,128)(2,1)S(1)}, u32[]{:S(2)}) copy-start(bf16[6,128,128]{2,1,0:T(8,128)(2,1)S(1)} %collective-permute-done.15.down_ref) | copy-start | bytes 589828
  101.6 5.9 %copy-start.15 = (bf16[6,128,128]{2,1,0:T(8,128)(2,1)}, bf16[6,128,128]{2,1,0:T(8,128)(2,1)S(1)}, u32[]{:S(2)}) copy-start(bf16[6,128,128]{2,1,0:T(8,128)(2,1)S(1)} %collective-permute-done.14.up_ref) | copy-start | bytes 589828
  101.7 12.5 %collective-permute-start.22 = (f32[112,128]{1,0:T(8,128)S(1)}, f32[112,128]{1,0:T(8,128)S(1)}, u32[]{:S(2)}, u32[]{:S(2)}) collective-permute-start(f32[112,128]{1,0:T(8,128)S(1)} %get-tuple-element.107), channel_id=1, source_target_pairs={{0,1},{1,2},{2,3},{3,0},{4,5},{5,6},{6,7},{7,4},{8,9},{9,10},{10,1... | collective-permute-start | bytes 172040 | tf_op jit(solution)/shard_map/ppermute | solution.py:253
  103.0 11.1 %collective-permute-start.23 = (f32[112,128]{1,0:T(8,128)S(1)}, f32[112,128]{1,0:T(8,128)S(1)}, u32[]{:S(2)}, u32[]{:S(2)}) collective-permute-start(f32[112,128]{1,0:T(8,128)S(1)} %get-tuple-element.106), channel_id=1, source_target_pairs={{0,2},{1,3},{2,0},{3,1},{4,6},{5,7},{6,4},{7,5},{8,10},{9,11},{10,... | collective-permute-start | bytes 172040 | tf_op jit(solution)/shard_map/ppermute | solution.py:253
  106.1 8.1 %collective-permute-start.24 = (f32[112,128]{1,0:T(8,128)S(1)}, f32[112,128]{1,0:T(8,128)S(1)}, u32[]{:S(2)}, u32[]{:S(2)}) collective-permute-start(f32[112,128]{1,0:T(8,128)S(1)} %get-tuple-element.105), channel_id=1, source_target_pairs={{0,3},{1,0},{2,1},{3,2},{4,7},{5,4},{6,5},{7,6},{8,11},{9,8},{10,9... | collective-permute-start | bytes 172040 | tf_op jit(solution)/shard_map/ppermute | solution.py:253
  112.1 26.1 %copy-start.2 = (bf16[8,4,32,128]{3,2,1,0:T(8,128)(2,1)S(1)}, bf16[8,4,32,128]{3,2,1,0:T(8,128)(2,1)}, u32[]{:S(2)}) copy-start(bf16[8,4,32,128]{3,2,1,0:T(8,128)(2,1)} %get-tuple-element.73) | copy-start | bytes 786436
  112.1 12.8 %collective-permute-start.19 = (bf16[8,4,32,128]{3,2,1,0:T(8,128)(2,1)}, bf16[8,4,32,128]{3,2,1,0:T(8,128)(2,1)S(1)}, u32[]{:S(2)}, u32[]{:S(2)}) collective-permute-start(bf16[8,4,32,128]{3,2,1,0:T(8,128)(2,1)} %get-tuple-element.63), channel_id=1, source_target_pairs={{0,1},{1,2},{2,3},{3,0},{4,5},{5,6},{6,7},{7,4},{8,9},{9,10},{10,1... | collective-permute-start | bytes 786440 | tf_op jit(solution)/shard_map/ppermute | solution.py:253
  112.1 23.2 %collective-permute-start.20 = (bf16[8,4,32,128]{3,2,1,0:T(8,128)(2,1)}, bf16[8,4,32,128]{3,2,1,0:T(8,128)(2,1)S(1)}, u32[]{:S(2)}, u32[]{:S(2)}) collective-permute-start(bf16[8,4,32,128]{3,2,1,0:T(8,128)(2,1)} %get-tuple-element.64), channel_id=1, source_target_pairs={{0,2},{1,3},{2,0},{3,1},{4,6},{5,7},{6,4},{7,5},{8,10},{9,11},{10,... | collective-permute-start | bytes 786440 | tf_op jit(solution)/shard_map/ppermute | solution.py:253
  114.2 23.9 %collective-permute-start.21 = (bf16[8,4,32,128]{3,2,1,0:T(8,128)(2,1)}, bf16[8,4,32,128]{3,2,1,0:T(8,128)(2,1)S(1)}, u32[]{:S(2)}, u32[]{:S(2)}) collective-permute-start(bf16[8,4,32,128]{3,2,1,0:T(8,128)(2,1)} %get-tuple-element.65), channel_id=1, source_target_pairs={{0,3},{1,0},{2,1},{3,2},{4,7},{5,4},{6,5},{7,6},{8,11},{9,8},{10,9... | collective-permute-start | bytes 786440 | tf_op jit(solution)/shard_map/ppermute | solution.py:253

commit v3 on v0

v3 whole, which is shorter than its diff:
```python
import functools
import math

import jax
import jax.numpy as jnp
from jax import lax
from jax.experimental import pallas as pl
from jax.experimental.pallas import tpu as pltpu
from jax.sharding import PartitionSpec as P

BF16 = jnp.bfloat16
F32 = jnp.float32
VMEM_BYTES = 56 * 1024 * 1024


def ring(count, step):
    return [(i, (i + step) % count) for i in range(count)]


def after(value, *others):
    return lax.optimization_barrier((value, *others))[0]


def kept(flag, value):
    return jnp.where(flag > 0, value, jnp.zeros_like(value))


def window(mid, low, high, a, height):
    if a == 0:
        return jnp.concatenate([low, mid[:, :-height]], axis=1)
    if a == 2:
        return jnp.concatenate([mid[:, height:], high], axis=1)
    return mid


def row_shifts(value, height):
    split = value.reshape(-1, height, value.shape[-1])
    row = lax.broadcasted_iota(jnp.int32, split.shape, 1)
    later = jnp.where(row == height - 1, 0.0, pltpu.roll(split, height - 1, 1))
    earlier = jnp.where(row == 0, 0.0, pltpu.roll(split, 1, 1))
    return later.reshape(value.shape), earlier.reshape(value.shape)


def convolve(columns, weights, channels, height, mirrored):
    lhs = jnp.concatenate([c.reshape(-1, channels) for c in columns], axis=1)
    out = jnp.dot(lhs, weights, preferred_element_type=F32)
    first, mid, last = (out[:, t * channels : (t + 1) * channels] for t in range(3))
    if mirrored:
        first, last = last, first
    return mid + row_shifts(first, height)[1] + row_shifts(last, height)[0]


def group_offsets(z, chan_count, group, sign):
    return [
        pl.multiple_of(lax.rem(z + sign * j + chan_count, chan_count) * group, group)
        for j in range(chan_count)
    ]


def block_step(rows):
    return max(1, 1024 // rows)


def over_columns(count, rows, visit):
    step = block_step(rows)
    loops, rest = count // step, count % step
    if loops:
        pl.loop(0, loops)(lambda i: visit(i * step, step))
    if rest:
        visit(loops * step, rest)


def turn_kernel(chan_count, height, z_ref, *refs):
    pieces = refs[:chan_count]
    first_ref, cells_ref, bottom_ref, top_ref = refs[chan_count:]
    columns, group, cells = pieces[0].shape
    offsets = group_offsets(z_ref[0], chan_count, group, -1)

    def visit(k, count):
        for n in range(count):
            for j in range(chan_count):
                first_ref[k + n, pl.ds(offsets[j], group), :] = pieces[j][k + n]
        for n in range(count):
            tile = first_ref[k + n].T
            cells_ref[k + n] = tile
            bottom_ref[k + n] = tile[:height]
            top_ref[k + n] = tile[cells - height :]

    over_columns(columns, cells, visit)


def weights_kernel(_, weights_ref, out_ref):
    size = weights_ref.shape[1] // 3
    for k in range(9):
        for t in range(3):
            tile = (slice(k * size, (k + 1) * size), slice(t * size, (t + 1) * size))
            out_ref[tile] = weights_ref[tile].T


def slope_of(pre):
    sigma = 1.0 / (1.0 + jnp.exp(-pre))
    return sigma * (1.0 + pre * (1.0 - sigma))


def forward_inner_kernel(height, _, x_ref, weights_ref, slope_ref):
    columns, cells, channels = slope_ref.shape

    def visit(k, count):
        parts = [
            x_ref[pl.ds(k + b, count), a * height : a * height + cells]
            for a in range(3)
            for b in range(3)
        ]
        pre = convolve(parts, weights_ref[...], channels, height, False)
        slope_ref[pl.ds(k, count)] = slope_of(pre).reshape(count, cells, channels)

    over_columns(columns, cells, visit)


def forward_outer_kernel(z_ref, x_ref, low_ref, high_ref, weights_ref, slope_ref):
    columns, cells, channels = slope_ref.shape
    height = cells // 2
    top = x_ref.shape[1]

    def visit(k, count):
        parts = []
        for a in range(3):
            for b in range(3):
                near = pl.ds(k + b, count)
                if a == 0:
                    first = kept(z_ref[1], low_ref[near])
                else:
                    first = x_ref[near, (a - 1) * height : a * height]
                if a == 2:
                    last = kept(z_ref[2], high_ref[near])
                else:
                    last = x_ref[near, top - (2 - a) * height : top - (1 - a) * height]
                parts.append(jnp.concatenate([first, last], axis=1))
        pre = convolve(parts, weights_ref[...], channels, height, False)
        slope_ref[pl.ds(k, count)] = slope_of(pre).reshape(count, cells, channels)

    over_columns(columns, cells, visit)


def windows_kernel(z_ref, x_ref, low_ref, high_ref, out_ref):
    columns, _, cells = out_ref.shape[1:]
    height = low_ref.shape[1]

    def visit(k, count):
        for n in range(count):
            mid = x_ref[pl.ds(k + n + 1, 1)]
            low = kept(z_ref[1], low_ref[pl.ds(k + n + 1, 1)])
            high = kept(z_ref[2], high_ref[pl.ds(k + n + 1, 1)])
            out_ref[0, k + n] = window(mid, low, high, 0, height)[0].T
            out_ref[1, k + n] = window(mid, low, high, 2, height)[0].T

    over_columns(columns, cells, visit)


def grad_out_kernel(chan_count, height, z_ref, *refs):
    pieces = refs[:chan_count]
    inner_ref, outer_ref, grad_ref, bottom_ref, top_ref, hold_ref = refs[chan_count:]
    group = pieces[0].shape[1]
    columns, cells, _ = grad_ref.shape
    offsets = group_offsets(z_ref[0], chan_count, group, -1)

    def visit(k, count):
        for n in range(count):
            for j in range(chan_count):
                hold_ref[n, pl.ds(offsets[j], group), :] = pieces[j][k + n]
        for n in range(count):
            cot = hold_ref[n].T.astype(F32)
            outer = outer_ref[k + n]
            slope = jnp.concatenate([outer[:height], inner_ref[k + n], outer[height:]], axis=0)
            grad = (cot * slope).astype(BF16)
            grad_ref[k + n] = grad
            bottom_ref[k + n] = grad[:height]
            top_ref[k + n] = grad[cells - height :]

    over_columns(columns, cells, visit)


def filter_kernel(
    chan_count, space_count, shard, height, core_ref, x_ref, sides_ref, grad_ref, keep_ref, send_ref, acc_ref, pack_ref
):
    columns, cells, channels = grad_ref.shape
    group = channels // chan_count
    acc_ref[...] = jnp.zeros_like(acc_ref)

    def visit(k, count):
        lhs = jnp.concatenate(
            [
                jnp.concatenate(
                    [
                        x_ref[k + n + b + 1] if a == 1 else sides_ref[a // 2, k + n + b]
                        for n in range(count)
                    ],
                    axis=1,
                )
                for a in range(3)
                for b in range(3)
            ],
            axis=0,
        )
        grad = grad_ref[pl.ds(k + 1, count)].reshape(count * cells, channels).astype(F32)
        later, earlier = row_shifts(grad, height)
        rhs = jnp.concatenate([v.astype(BF16) for v in (later, grad, earlier)], axis=1)
        acc_ref[...] += jnp.dot(lhs, rhs, preferred_element_type=F32)

    over_columns(columns - 2, cells, visit)
    used = 27 * group
    for z in range(chan_count):
        for offset in range(27):
            a, t, m = offset // 9, offset // 3 % 3, offset % 3
            row = (3 * a + m) * channels + z * group
            pack_ref[z, offset * group : (offset + 1) * group, :] = acc_ref[
                row : row + group, t * channels : (t + 1) * channels
            ]
        pack_ref[z, used:, :] = jnp.zeros((space_count * shard - used, channels), F32)
    core = core_ref[0]
    for chip in range(space_count // 2):
        mine = pl.multiple_of((2 * chip + core) * shard, 8)
        other = pl.multiple_of((2 * chip + 1 - core) * shard, 8)
        for z in range(chan_count):
            keep_ref[chip, z] = pack_ref[z, pl.ds(mine, shard), :]
            send_ref[chip, z] = pack_ref[z, pl.ds(other, shard), :]


def input_kernel(chan_count, base, made, z_ref, grad_ref, low_ref, high_ref, weights_ref, *refs):
    earlier, outs, hold_ref = refs[: -1 - chan_count], refs[-1 - chan_count : -1], refs[-1]
    for out, old in zip(outs, earlier):
        out[:made] = old[...]
    columns, cells, channels = grad_ref.shape
    height = low_ref.shape[1]
    group = channels // chan_count
    offsets = group_offsets(z_ref[0], chan_count, group, 1)

    def visit(k, count):
        parts = [
            window(
                grad_ref[pl.ds(base + k + 2 - b, count)],
                kept(z_ref[1], low_ref[pl.ds(base + k + 2 - b, count)]),
                kept(z_ref[2], high_ref[pl.ds(base + k + 2 - b, count)]),
                2 - a,
                height,
            )
            for a in range(3)
            for b in range(3)
        ]
        total = convolve(parts, weights_ref[...], channels, height, True).astype(BF16)
        total = total.reshape(count, cells, channels)
        for n in range(count):
            hold_ref[n] = total[n].T
        for j in range(chan_count):
            for n in range(count):
                outs[j][made + k + n] = hold_ref[n, pl.ds(offsets[j], group), :]

    over_columns(outs[0].shape[0] - made, cells, visit)


def call(kernel, outs, scratch, flops, args, scalar):
    nbytes = sum(math.prod(a.shape) * a.dtype.itemsize for a in list(args) + list(outs))
    return pl.pallas_call(
        kernel,
        out_shape=outs,
        in_specs=[pl.BlockSpec(memory_space=pltpu.SMEM)]
        + [pl.BlockSpec(memory_space=pltpu.VMEM)] * len(args),
        out_specs=[pl.BlockSpec(memory_space=pltpu.VMEM)] * len(outs),
        scratch_shapes=scratch,
        compiler_params=pltpu.CompilerParams(vmem_limit_bytes=VMEM_BYTES),
        cost_estimate=pl.CostEstimate(
            flops=flops, bytes_accessed=nbytes if flops else 0, transcendentals=0
        ),
    )(scalar, *args)


def column_blocks(array, before, behind, z, chan_count):
    group, planes, height, width = array.shape
    turned = array.reshape(group, planes * height, width).transpose(2, 0, 1)
    turned = jnp.pad(turned, ((before, behind), (0, 0), (0, 0)))
    columns = width // chan_count
    return [
        lax.dynamic_slice_in_dim(
            turned, lax.rem(z + j, chan_count) * columns, columns + before + behind, axis=0
        )
        for j in range(chan_count)
    ]


def exchange(blocks, axis):
    count = len(blocks)
    return [blocks[0]] + [
        lax.ppermute(blocks[j], axis, ring(count, j)) for j in range(1, count)
    ]


def gather_filters(filters, z, s, chan_count, space_count, shard):
    offsets, group, channels = filters.shape
    rows = offsets * group
    flat = jnp.pad(filters.reshape(rows, channels), ((0, space_count * shard - rows), (0, 0)))
    mine = lax.dynamic_slice_in_dim(flat, s * shard, shard, axis=0)
    got = [mine] + [
        lax.ppermute(mine, "chan", ring(chan_count, j)) for j in range(1, chan_count)
    ]
    doubled = jnp.stack(got[::-1] + got[::-1])
    shares = lax.dynamic_slice_in_dim(doubled, chan_count - 1 - z, chan_count, axis=0)
    whole = lax.all_gather(shares, "space", axis=1, tiled=True)
    return whole[:, :rows].reshape(chan_count, 3, 3, 3, group, channels)


def body(inputs, filters, cotangent):
    chan_count = lax.axis_size("chan")
    space_count = lax.axis_size("space")
    group, planes, height, width = inputs.shape
    channels = group * chan_count
    columns = width // chan_count
    cells = planes * height
    z = lax.axis_index("chan").astype(jnp.int32)
    s = lax.axis_index("space").astype(jnp.int32)
    upward, downward = ring(space_count, 1), ring(space_count, -1)
    shape = jax.ShapeDtypeStruct
    flags = [(s > 0).astype(jnp.int32), (s < space_count - 1).astype(jnp.int32)]
    z_arg = jnp.stack([z] + flags)
    macs = 27 * channels * channels * columns * cells

    x_pieces = exchange(column_blocks(inputs, 2, 2, z, chan_count), "chan")
    shard = -(-27 * group // (16 * space_count)) * 16
    by_offset = gather_filters(filters, z, s, chan_count, space_count, shard)
    weights_f = by_offset.transpose(1, 3, 0, 4, 2, 5).reshape(9 * channels, 3 * channels)
    c_blocks = column_blocks(cotangent, 1, 4, z, chan_count)
    weights_b = call(
        weights_kernel, [shape(weights_f.shape, BF16)], [], 0, [weights_f], z_arg
    )[0]
    x_pieces = after(x_pieces, weights_b, z_arg, c_blocks)

    x_first, x_cells, x_bottom, x_top = call(
        functools.partial(turn_kernel, chan_count, height),
        [
            shape((columns + 4, channels, cells), BF16),
            shape((columns + 4, cells, channels), BF16),
        ]
        + [shape((columns + 4, height, channels), BF16)] * 2,
        [],
        0,
        x_pieces,
        z_arg,
    )
    x_low = lax.ppermute(x_top, "space", upward)
    x_high = lax.ppermute(x_bottom, "space", downward)
    c_pieces = exchange(
        c_blocks[:1] + [after(c, x) for c, x in zip(c_blocks[1:], x_pieces[1:])], "chan"
    )
    slope_inner = call(
        functools.partial(forward_inner_kernel, height),
        [shape((columns + 2, cells - 2 * height, channels), F32)],
        [],
        0,
        [x_cells, weights_f],
        z_arg,
    )[0]
    slope_outer = call(
        forward_outer_kernel,
        [shape((columns + 2, 2 * height, channels), F32)],
        [],
        0,
        [after(x_cells, slope_inner), x_low, x_high, weights_f],
        z_arg,
    )[0]
    x_windows = call(
        windows_kernel,
        [shape((2, columns + 2, channels, cells), BF16)],
        [],
        0,
        [x_cells, x_low, x_high],
        z_arg,
    )[0]
    slope_outer = after(slope_outer, x_windows)
    grad, g_bottom, g_top = call(
        functools.partial(grad_out_kernel, chan_count, height),
        [shape((columns + 2, cells, channels), BF16)]
        + [shape((columns + 2, height, channels), BF16)] * 2,
        [pltpu.VMEM((block_step(cells), channels, cells), BF16)],
        10 * columns * cells * channels,
        [*c_pieces, slope_inner, slope_outer],
        z_arg,
    )
    g_low = lax.ppermute(g_top, "space", upward)
    g_high = lax.ppermute(g_bottom, "space", downward)

    chips = space_count // 2
    half = shape((chips, chan_count, shard, channels), F32)
    keep, send = call(
        functools.partial(filter_kernel, chan_count, space_count, shard, height),
        [half, half],
        [
            pltpu.VMEM((9 * channels, 3 * channels), F32),
            pltpu.VMEM((chan_count, space_count * shard, channels), F32),
        ],
        0,
        [x_first, x_windows, grad],
        lax.rem(s, 2).reshape(1),
    )
    g_low, g_high, send = lax.optimization_barrier((g_low, g_high, send))
    from_core = lax.ppermute(send, "space", [(i, i ^ 1) for i in range(space_count)])
    half_columns = columns // 2
    hold = [pltpu.VMEM((block_step(cells), channels, cells), BF16)]
    first = call(
        functools.partial(input_kernel, chan_count, 0, 0),
        [shape((half_columns, group, cells), BF16)] * chan_count,
        hold,
        3 * macs,
        [grad, g_low, g_high, weights_b],
        z_arg,
    )
    pair_sum = keep + after(from_core, first[0])
    chip = s // 2
    chip_sum = lax.dynamic_index_in_dim(pair_sum, chip, 0, keepdims=False)
    rounded = pair_sum.astype(BF16)
    g_low, g_high = after((g_low, g_high), rounded)
    from_chips = []
    for k in range(1, chips):
        block = lax.dynamic_index_in_dim(rounded, chip ^ k, 0, keepdims=False)
        from_chips.append(
            lax.ppermute(block, "space", [(i, i ^ (2 * k)) for i in range(space_count)])
        )
    back = call(
        functools.partial(input_kernel, chan_count, half_columns, half_columns),
        [shape((columns, group, cells), BF16)] * chan_count,
        hold,
        3 * macs,
        [grad, g_low, g_high, weights_b, *first],
        z_arg,
    )
    returned = exchange(back, "chan")
    for got in after(from_chips, back[0]):
        chip_sum = chip_sum + got.astype(F32)
    parts = [
        lax.dynamic_index_in_dim(chip_sum, lax.rem(z + j, chan_count), 0, keepdims=False)
        for j in range(chan_count)
    ]
    shard_sum = sum(exchange(parts, "chan"))
    returned = after(returned, shard_sum)
    cell_total = planes * space_count * height * width
    shard_sum = shard_sum * (1.0 / math.sqrt(cell_total))
    whole = lax.all_gather(shard_sum, "space", axis=0, tiled=True)
    grad_w = whole[: 27 * group].reshape(27, group, channels)

    reverse = returned[::-1]
    doubled = jnp.concatenate(reverse + reverse, axis=0)
    start = lax.rem(chan_count - 1 - z + chan_count, chan_count) * columns
    ordered = lax.dynamic_slice_in_dim(doubled, start, width, axis=0)
    return ordered.transpose(1, 2, 0).reshape(group, planes, height, width), grad_w


def solution(mesh):
    placed = (P("chan", "space", None, None), P(None, "chan", None), P("chan", "space", None, None))
    return jax.shard_map(
        body,
        mesh=mesh,
        in_specs=placed,
        out_specs=(P("chan", "space", None, None), P(None, "chan", None)),
        check_vma=False,
    )
```

time: 511 us -> 134 us (0.26); the launches traced: 501 us -> 133 us
  waiting for transfers between devices: 245 us -> 10.7 us
  matrix products: 137 us -> 0 us
  local copies, waits for them, and re-layouts: 72.6 us -> 16.2 us
  Pallas kernels: 0 us -> 46.6 us
  starting transfers between devices: 10.4 us -> 36.6 us
  other arithmetic: 22.2 us -> 0.76 us
  blocking collectives: 0 us -> 21.1 us
  between operations: 14.5 us -> 1.02 us
    reduce_scatter x1 -> x0, waiting for transfers between devices: 148 us -> none  [body(): lax.psum_scatter(partial_sum, 'chan', scatter_dimension=0, tiled=True)]
    dot_general x31 -> x0, matrix products: 137 us -> none  [the longest x27 89.9 us: body(): jnp.einsum('io,odhw->idhw', filters[offset], window, preferred_element_ty...]
    all_gather x1 -> x0, waiting for transfers between devices: 48.5 us -> none  [body(): grad_all = lax.all_gather(grad_out, 'chan', axis=0, tiled=True)]
    psum x1 -> x0, waiting for transfers between devices: 48 us -> none  [body(): grad_w = lax.psum(grad_w, 'space')]
    pallas_call x0 -> x9, Pallas kernels: none -> 46.6 us  [call(): pl.pallas_call(kernel, out_shape=outs, in_specs=[pl.BlockSpec(memory_spac...]
    unnamed x63 -> x41, local copies, waits for them, and re-layouts: 51.9 us -> 6.54 us
    ppermute x4 -> x23, starting transfers between devices: 10 us -> 36.6 us  [the longest x12 21.2 us: exchange(): lax.ppermute(blocks[j], axis, ring(count, j))]
    all_gather x0 -> x2, blocking collectives: none -> 21.1 us  [the longest x1 11 us: gather_filters(): whole = lax.all_gather(shares, 'space', axis=1, tiled=True)]
  transfers between devices with their start and end apart: 7 -> 23, of which waited for: 4 -> 1; matrix products, arithmetic and copies ran while one was open for 12% -> 7% of each run, Pallas kernels for 0% -> 32%
where the time goes in v3:
time: 134 us; the launch traced here: 133 us
  Pallas kernels  46.6 us (35%)
  starting transfers between devices  36.6 us (27%)
  blocking collectives  21.1 us (16%)
  local copies, waits for them, and re-layouts  16.2 us (12%)
  waiting for transfers between devices  10.7 us (8%)
    pallas_call x9, Pallas kernels, call(): pl.pallas_call(kernel, out_shape=outs, in_specs=[pl.BlockSpec(memory_spac...  46.6 us
    ppermute x12, starting transfers between devices, exchange(): lax.ppermute(blocks[j], axis, ring(count, j))  21.2 us
    all_gather x1, blocking collectives, gather_filters(): whole = lax.all_gather(shares, 'space', axis=1, tiled=True)  11 us
    ppermute x12, waiting for transfers between devices, exchange(): lax.ppermute(blocks[j], axis, ring(count, j))  10.7 us
    all_gather x1, blocking collectives, body(): whole = lax.all_gather(shard_sum, 'space', axis=0, tiled=True)  10 us
    unnamed x41, local copies, waits for them, and re-layouts  6.54 us
    ppermute x3, starting transfers between devices, gather_filters(): lax.ppermute(mine, 'chan', ring(chan_count, j))  6.06 us
    ppermute x3, starting transfers between devices, body(): lax.ppermute(block, 'space', [(i, i ^ 2 * k) for i in range(space_count)])  3.94 us
  transfers between devices with their start and end apart: 23, of which 1 were waited for; matrix products, arithmetic and copies ran while one was open for 7% of the time, Pallas kernels for 32%

profile of v3, /device:TPU:0, one launch (start us, length us, event | category | flops | bytes accessed | tf_op | source)
XLA Modules:
  0.0 132.9 jit_solution(2045372868531052075)
XLA Ops:
  0.6 1.4 %pad_dynamic-slice_fusion.8 = bf16[112,128]{1,0:T(8,128)(2,1)} fusion(s32[]{:T(128)S(6)} %select_n.71, bf16[864,128]{1,0:T(8,128)(2,1)} %bitcast.65), kind=kLoop, calls=%fused_computation.13 | loop fusion | bytes 249860 | tf_op jit(solution)/shard_map/dynamic_slice | solution.py:301
  2.0 5.0 %collective-permute-start.3 = (bf16[112,128]{1,0:T(8,128)(2,1)}, bf16[112,128]{1,0:T(8,128)(2,1)S(1)}, u32[]{:S(2)}, u32[]{:S(2)}) collective-permute-start(bf16[112,128]{1,0:T(8,128)(2,1)} %pad_dynamic-slice_fusion.8), channel_id=1, source_target_pairs={{0,3},{1,0},{2,1},{3,2},{4,7},{5,4},{6,5},{7,6},{8,11},{9,8},{10,9... | collective-permute-start | bytes 86024 | tf_op jit(solution)/shard_map/ppermute | solution.py:303
  7.1 1.0 collective-permute-start.5
  8.1 2.0 %copy.9 = bf16[32,128,128]{1,0,2:T(8,128)(2,1)S(1)} copy(bf16[32,128,128]{2,1,0:T(8,128)(2,1)} %bitcast.68) | data formatting | bytes 2097152 | tf_op jit(solution)/shard_map/reshape | solution.py:279
  10.1 1.0 pad_dynamic-slice_fusion.4
  11.1 2.5 %collective-permute-start = (bf16[36,32,128]{2,1,0:T(8,128)(2,1)S(1)}, bf16[36,32,128]{2,1,0:T(8,128)(2,1)S(1)}, u32[]{:S(2)}, u32[]{:S(2)}) collective-permute-start(bf16[36,32,128]{2,1,0:T(8,128)(2,1)S(1)} %get-tuple-element.91), channel_id=1, source_target_pairs={{0,1},{1,2},{2,3},{3,0},{4,5},{5,6},{6,7},{7,4},{8,9},{9,10},{10,1... | collective-permute-start | bytes 884744 | tf_op jit(solution)/shard_map/ppermute | solution.py:293
  13.6 0.9 collective-permute-start.1
  14.5 1.0 copy.8
  15.5 1.0 pad_dynamic-slice_fusion
  16.5 0.6 pad_add_fusion._.z_ref
  17.0 1.5 %collective-permute-start.2 = (bf16[36,32,128]{2,1,0:T(8,128)(2,1)S(1)}, bf16[36,32,128]{2,1,0:T(8,128)(2,1)S(1)}, u32[]{:S(2)}, u32[]{:S(2)}) collective-permute-start(bf16[36,32,128]{2,1,0:T(8,128)(2,1)S(1)} %get-tuple-element.90), channel_id=1, source_target_pairs={{0,3},{1,0},{2,1},{3,2},{4,7},{5,4},{6,5},{7,6},{8,11},{9,8},{10,9... | collective-permute-start | bytes 884744 | tf_op jit(solution)/shard_map/ppermute | solution.py:293
  18.5 0.8 constant_dynamic-update-slice_fusion.5
  19.3 0.8 constant_dynamic-update-slice_fusion.1
  20.1 11.0 %all_gather.6 = bf16[4,896,128]{2,1,0:T(8,128)(2,1)S(1)} all-gather(bf16[4,112,128]{2,1,0:T(8,128)(2,1)S(1)} %constant_dynamic-slice_fusion), channel_id=1, replica_groups=mesh['space'=8,'chan'=4] {'space'}, dimensions={1}, use_global_device_ids=true | all-gather | bytes 1032192 | tf_op jit(solution)/shard_map/all_gather | solution.py:307
  31.2 0.6 copy.10
  31.9 1.1 copy.14
  32.9 2.4 %shard_map.50.weights_ref = bf16[1152,384]{1,0:T(8,128)(2,1)} custom-call(s32[3]{0:T(128)} %pad_add_fusion._.z_ref, bf16[1152,384]{1,0:T(8,128)(2,1)} %bitcast.58), custom_call_target="tpu_custom_call" | custom-call | tf_op jit(solution)/shard_map/pallas_call | solution.py:263
  35.3 5.0 %collective-permute-start.6 = (bf16[37,32,128]{2,1,0:T(8,128)(2,1)S(1)}, bf16[37,32,128]{2,1,0:T(8,128)(2,1)S(1)}, u32[]{:S(2)}, u32[]{:S(2)}) collective-permute-start(bf16[37,32,128]{2,1,0:T(8,128)(2,1)S(1)} %get-tuple-element.42), channel_id=1, source_target_pairs={{0,1},{1,2},{2,3},{3,0},{4,5},{5,6},{6,7},{7,4},{8,9},{9,10},{10,1... | collective-permute-start | bytes 909320 | tf_op jit(solution)/shard_map/ppermute | solution.py:293
  40.3 1.4 %collective-permute-start.7 = (bf16[37,32,128]{2,1,0:T(8,128)(2,1)S(1)}, bf16[37,32,128]{2,1,0:T(8,128)(2,1)S(1)}, u32[]{:S(2)}, u32[]{:S(2)}) collective-permute-start(bf16[37,32,128]{2,1,0:T(8,128)(2,1)S(1)} %get-tuple-element.44), channel_id=1, source_target_pairs={{0,2},{1,3},{2,0},{3,1},{4,6},{5,7},{6,4},{7,5},{8,10},{9,11},{10,... | collective-permute-start | bytes 909320 | tf_op jit(solution)/shard_map/ppermute | solution.py:293
  41.7 1.0 collective-permute-start.8
  42.7 3.4 %shard_map.51 = (bf16[36,128,128]{2,1,0:T(8,128)(2,1)}, bf16[36,128,128]{2,1,0:T(8,128)(2,1)}, bf16[36,32,128]{2,1,0:T(8,128)(2,1)}, bf16[36,32,128]{2,1,0:T(8,128)(2,1)}) custom-call(s32[3]{0:T(128)} %pad_add_fusion._.z_ref, bf16[36,32,128]{2,1,0:T(8,128)(2,1)} %get-tuple-element.47.refs_0_, bf16[36,32,128]{2,1,0:T(8,128)(2,1)} %copy-done.9, ...), custom_call_target="tpu_custom_call" | custom-call | tf_op jit(solution)/shard_map/pallas_call | solution.py:263
  46.1 2.6 %collective-permute-start.10 = (bf16[36,32,128]{2,1,0:T(8,128)(2,1)}, bf16[36,32,128]{2,1,0:T(8,128)(2,1)S(1)}, u32[]{:S(2)}, u32[]{:S(2)}) collective-permute-start(bf16[36,32,128]{2,1,0:T(8,128)(2,1)} %get-tuple-element.51), channel_id=1, source_target_pairs={{0,28},{4,0},{8,4},{12,8},{16,12},{20,16},{24,20},{28,24},{1,29},{... | collective-permute-start | bytes 884744 | tf_op jit(solution)/shard_map/ppermute | solution.py:349
  48.8 6.1 %shard_map.52.refs_4_ = f32[34,64,128]{2,1,0:T(8,128)} custom-call(s32[3]{0:T(128)} %pad_add_fusion._.z_ref, bf16[36,128,128]{2,1,0:T(8,128)(2,1)} %get-tuple-element.49.x_ref, bf16[1152,384]{1,0:T(8,128)(2,1)} %bitcast.59), custom_call_target="tpu_custom_call" | custom-call | tf_op jit(solution)/shard_map/pallas_call | solution.py:263
  54.9 0.7 copy-done.1
  55.6 0.7 copy-done.2
  56.3 3.7 %shard_map.54.sides_ref = bf16[2,34,128,128]{3,2,1,0:T(8,128)(2,1)} custom-call(s32[3]{0:T(128)} %pad_add_fusion._.z_ref, bf16[36,128,128]{2,1,0:T(8,128)(2,1)} %get-tuple-element.49.x_ref, bf16[36,32,128]{2,1,0:T(8,128)(2,1)} %copy-done.1, bf16[36,32,128]{2,1,0:T(8,128)(2,1)} %copy-done.2), custom_call_target="tpu_custom_call" | custom-call | tf_op jit(solution)/shard_map/pallas_call | solution.py:263
  59.9 6.3 %shard_map.53.refs_5_ = f32[34,64,128]{2,1,0:T(8,128)} custom-call(s32[3]{0:T(128)} %pad_add_fusion._.z_ref, bf16[36,128,128]{2,1,0:T(8,128)(2,1)} %get-tuple-element.49.x_ref, bf16[36,32,128]{2,1,0:T(8,128)(2,1)} %copy-done.1, bf16[36,32,128]{2,1,0:T(8,128)(2,1)} %copy-done.2, bf16[1152,384]{1,0:T(8,128)(2,1)} %bitcast.60), custom_call_target="tpu_custom_call" | custom-call | tf_op jit(solution)/shard_map/pallas_call | solution.py:263
  66.3 0.7 copy-done.6
  67.1 0.8 copy-done.8
  67.8 3.8 %shard_map.55 = (bf16[34,128,128]{2,1,0:T(8,128)(2,1)}, bf16[34,32,128]{2,1,0:T(8,128)(2,1)}, bf16[34,32,128]{2,1,0:T(8,128)(2,1)}) custom-call(s32[3]{0:T(128)} %pad_add_fusion._.z_ref, bf16[37,32,128]{2,1,0:T(8,128)(2,1)} %get-tuple-element.89.refs_0_, bf16[37,32,128]{2,1,0:T(8,128)(2,1)} %copy-done.6, bf16[37,32,128]{2,1,0:T(8,128)(2,1)} %copy-done.7, ...), custom_call_target="tpu_custom_call" | custom-call | flops 5242880 | bytes 5111808 | tf_op jit(solution)/shard_map/pallas_call | solution.py:263
  71.7 1.1 collective-permute-start.11
  72.8 1.5 %collective-permute-start.12 = (bf16[34,32,128]{2,1,0:T(8,128)(2,1)}, bf16[34,32,128]{2,1,0:T(8,128)(2,1)S(1)}, u32[]{:S(2)}, u32[]{:S(2)}) collective-permute-start(bf16[34,32,128]{2,1,0:T(8,128)(2,1)} %get-tuple-element.55), channel_id=1, source_target_pairs={{0,28},{4,0},{8,4},{12,8},{16,12},{20,16},{24,20},{28,24},{1,29},{... | collective-permute-start | bytes 835592 | tf_op jit(solution)/shard_map/ppermute | solution.py:388
  74.3 9.4 %shard_map.56 = (f32[4,4,112,128]{3,2,1,0:T(8,128)}, f32[4,4,112,128]{3,2,1,0:T(8,128)}) custom-call(s32[1]{0:T(128)} %bitcast.14.core_ref, bf16[36,128,128]{2,1,0:T(8,128)(2,1)} %get-tuple-element.56.x_ref, bf16[2,34,128,128]{3,2,1,0:T(8,128)(2,1)} %shard_map.54.sides_ref, bf16[34,128,128]{2,1,0:T(8,128)(2,1)} %get-tuple-element.53.grad_ref), custom_call_target="tpu_custom_call" | custom-call | tf_op jit(solution)/shard_map/pallas_call | solution.py:263
  83.9 0.6 copy-done.11
  84.6 5.6 %shard_map.57 = (bf16[16,32,128]{2,1,0:T(8,128)(2,1)}, bf16[16,32,128]{2,1,0:T(8,128)(2,1)}, bf16[16,32,128]{2,1,0:T(8,128)(2,1)}, bf16[16,32,128]{2,1,0:T(8,128)(2,1)}) custom-call(s32[3]{0:T(128)} %pad_add_fusion._.z_ref, bf16[34,128,128]{2,1,0:T(8,128)(2,1)} %get-tuple-element.53.grad_ref, bf16[34,32,128]{2,1,0:T(8,128)(2,1)} %copy-done.11, ...), custom_call_target="tpu_custom_call" | custom-call | flops 5435817984 | bytes 3080192 | tf_op jit(solution)/shard_map/pallas_call | solution.py:263
  90.4 0.7 collective-permute-start.17
  91.1 1.8 %collective-permute-start.18 = (bf16[4,112,128]{2,1,0:T(8,128)(2,1)S(1)}, bf16[4,112,128]{2,1,0:T(8,128)(2,1)S(1)}, u32[]{:S(2)}, u32[]{:S(2)}) collective-permute-start(bf16[4,112,128]{2,1,0:T(8,128)(2,1)S(1)} %get-tuple-element.95), channel_id=1, source_target_pairs={{0,16},{4,20},{8,24},{12,28},{16,0},{20,4},{24,8},{28,12},{1,17},{... | collective-permute-start | bytes 344072 | tf_op jit(solution)/shard_map/ppermute | solution.py:424
  92.9 1.4 %collective-permute-start.19 = (bf16[4,112,128]{2,1,0:T(8,128)(2,1)S(1)}, bf16[4,112,128]{2,1,0:T(8,128)(2,1)S(1)}, u32[]{:S(2)}, u32[]{:S(2)}) collective-permute-start(bf16[4,112,128]{2,1,0:T(8,128)(2,1)S(1)} %get-tuple-element.94), channel_id=1, source_target_pairs={{0,24},{4,28},{8,16},{12,20},{16,8},{20,12},{24,0},{28,4},{1,25},{... | collective-permute-start | bytes 344072 | tf_op jit(solution)/shard_map/ppermute | solution.py:424
  94.3 5.9 %shard_map.58 = (bf16[32,32,128]{2,1,0:T(8,128)(2,1)}, bf16[32,32,128]{2,1,0:T(8,128)(2,1)}, bf16[32,32,128]{2,1,0:T(8,128)(2,1)}, bf16[32,32,128]{2,1,0:T(8,128)(2,1)}) custom-call(s32[3]{0:T(128)} %pad_add_fusion._.z_ref, bf16[34,128,128]{2,1,0:T(8,128)(2,1)} %get-tuple-element.53.grad_ref, bf16[34,32,128]{2,1,0:T(8,128)(2,1)} %copy-done.11, ...), custom_call_target="tpu_custom_call" | custom-call | flops 5435817984 | bytes 4128768 | tf_op jit(solution)/shard_map/pallas_call | solution.py:263
  100.3 2.9 %collective-permute-start.22 = (f32[112,128]{1,0:T(8,128)S(1)}, f32[112,128]{1,0:T(8,128)S(1)}, u32[]{:S(2)}, u32[]{:S(2)}) collective-permute-start(f32[112,128]{1,0:T(8,128)S(1)} %get-tuple-element.98), channel_id=1, source_target_pairs={{0,3},{1,0},{2,1},{3,2},{4,7},{5,4},{6,5},{7,6},{8,11},{9,8},{10,9... | collective-permute-start | bytes 172040 | tf_op jit(solution)/shard_map/ppermute | solution.py:293
  103.2 0.6 collective-permute-start.20
  103.8 2.8 %collective-permute-start.14 = (bf16[32,32,128]{2,1,0:T(8,128)(2,1)}, bf16[32,32,128]{2,1,0:T(8,128)(2,1)S(1)}, u32[]{:S(2)}, u32[]{:S(2)}) collective-permute-start(bf16[32,32,128]{2,1,0:T(8,128)(2,1)} %get-tuple-element.70), channel_id=1, source_target_pairs={{0,1},{1,2},{2,3},{3,0},{4,5},{5,6},{6,7},{7,4},{8,9},{9,10},{10,1... | collective-permute-start | bytes 786440 | tf_op jit(solution)/shard_map/ppermute | solution.py:293
  106.7 0.9 collective-permute-start.15
  107.6 1.7 %collective-permute-start.16 = (bf16[32,32,128]{2,1,0:T(8,128)(2,1)}, bf16[32,32,128]{2,1,0:T(8,128)(2,1)S(1)}, u32[]{:S(2)}, u32[]{:S(2)}) collective-permute-start(bf16[32,32,128]{2,1,0:T(8,128)(2,1)} %get-tuple-element.72), channel_id=1, source_target_pairs={{0,3},{1,0},{2,1},{3,2},{4,7},{5,4},{6,5},{7,6},{8,11},{9,8},{10,9... | collective-permute-start | bytes 786440 | tf_op jit(solution)/shard_map/ppermute | solution.py:293
  109.3 10.6 %collective-permute-done.21 = f32[112,128]{1,0:T(8,128)S(1)} collective-permute-done((f32[112,128]{1,0:T(8,128)S(1)}, f32[112,128]{1,0:T(8,128)S(1)}, u32[]{:S(2)}, u32[]{:S(2)}) %collective-permute-start.21) | collective-permute-done | bytes 57376 | tf_op jit(solution)/shard_map/ppermute | solution.py:293
  120.0 10.0 %all_gather.7 = f32[896,128]{1,0:T(8,128)S(1)} all-gather(f32[112,128]{1,0:T(8,128)S(1)} %broadcast_multiply_fusion), channel_id=1, replica_groups=mesh['space'=8,'chan'=4] {'space'}, dimensions={0}, use_global_device_ids=true | all-gather | bytes 516096 | tf_op jit(solution)/shard_map/all_gather | solution.py:445
  130.0 0.8 slice.9
  131.2 1.7 %copy.11 = bf16[32,128,128]{2,1,0:T(8,128)(2,1)} copy(bf16[32,128,128]{1,0,2:T(8,128)(2,1)S(1)} %dynamic-slice_bitcast_fusion) | data formatting | bytes 2097152 | tf_op jit(solution)/shard_map/transpose | solution.py:452
  (69 shorter events, 1.1 us)
Async XLA Ops:
  2.0 15.0 %collective-permute-start.3 = (bf16[112,128]{1,0:T(8,128)(2,1)}, bf16[112,128]{1,0:T(8,128)(2,1)S(1)}, u32[]{:S(2)}, u32[]{:S(2)}) collective-permute-start(bf16[112,128]{1,0:T(8,128)(2,1)} %pad_dynamic-slice_fusion.8), channel_id=1, source_target_pairs={{0,3},{1,0},{2,1},{3,2},{4,7},{5,4},{6,5},{7,6},{8,11},{9,8},{10,9... | collective-permute-start | bytes 86024 | tf_op jit(solution)/shard_map/ppermute | solution.py:303
  7.1 11.4 %collective-permute-start.4 = (bf16[112,128]{1,0:T(8,128)(2,1)}, bf16[112,128]{1,0:T(8,128)(2,1)S(1)}, u32[]{:S(2)}, u32[]{:S(2)}) collective-permute-start(bf16[112,128]{1,0:T(8,128)(2,1)} %pad_dynamic-slice_fusion.8), channel_id=1, source_target_pairs={{0,2},{1,3},{2,0},{3,1},{4,6},{5,7},{6,4},{7,5},{8,10},{9,11},{10,... | collective-permute-start | bytes 86024 | tf_op jit(solution)/shard_map/ppermute | solution.py:303
  7.1 11.4 %collective-permute-start.5 = (bf16[112,128]{1,0:T(8,128)(2,1)}, bf16[112,128]{1,0:T(8,128)(2,1)}, u32[]{:S(2)}, u32[]{:S(2)}) collective-permute-start(bf16[112,128]{1,0:T(8,128)(2,1)} %pad_dynamic-slice_fusion.8), channel_id=1, source_target_pairs={{0,1},{1,2},{2,3},{3,0},{4,5},{5,6},{6,7},{7,4},{8,9},{9,10},{10,1... | collective-permute-start | bytes 86024 | tf_op jit(solution)/shard_map/ppermute | solution.py:303
  8.1 6.4 %copy-start.3 = (bf16[32,4,32,128]{3,2,1,0:T(8,128)(2,1)S(1)}, bf16[32,4,32,128]{3,2,1,0:T(8,128)(2,1)}, u32[]{:S(2)}) copy-start(bf16[32,4,32,128]{3,2,1,0:T(8,128)(2,1)} %param.5) | copy-start | bytes 3145732
  11.1 24.2 %collective-permute-start = (bf16[36,32,128]{2,1,0:T(8,128)(2,1)S(1)}, bf16[36,32,128]{2,1,0:T(8,128)(2,1)S(1)}, u32[]{:S(2)}, u32[]{:S(2)}) collective-permute-start(bf16[36,32,128]{2,1,0:T(8,128)(2,1)S(1)} %get-tuple-element.91), channel_id=1, source_target_pairs={{0,1},{1,2},{2,3},{3,0},{4,5},{5,6},{6,7},{7,4},{8,9},{9,10},{10,1... | collective-permute-start | bytes 884744 | tf_op jit(solution)/shard_map/ppermute | solution.py:293
  13.6 21.7 %collective-permute-start.1 = (bf16[36,32,128]{2,1,0:T(8,128)(2,1)S(1)}, bf16[36,32,128]{2,1,0:T(8,128)(2,1)}, u32[]{:S(2)}, u32[]{:S(2)}) collective-permute-start(bf16[36,32,128]{2,1,0:T(8,128)(2,1)S(1)} %get-tuple-element.92), channel_id=1, source_target_pairs={{0,2},{1,3},{2,0},{3,1},{4,6},{5,7},{6,4},{7,5},{8,10},{9,11},{10,... | collective-permute-start | bytes 884744 | tf_op jit(solution)/shard_map/ppermute | solution.py:293
  14.5 4.8 %copy-start = (bf16[27,32,128]{2,1,0:T(8,128)(2,1)S(1)}, bf16[27,32,128]{2,1,0:T(8,128)(2,1)}, u32[]{:S(2)}) copy-start(bf16[27,32,128]{2,1,0:T(8,128)(2,1)} %param.4) | copy-start | bytes 663556
  17.0 18.3 %collective-permute-start.2 = (bf16[36,32,128]{2,1,0:T(8,128)(2,1)S(1)}, bf16[36,32,128]{2,1,0:T(8,128)(2,1)S(1)}, u32[]{:S(2)}, u32[]{:S(2)}) collective-permute-start(bf16[36,32,128]{2,1,0:T(8,128)(2,1)S(1)} %get-tuple-element.90), channel_id=1, source_target_pairs={{0,3},{1,0},{2,1},{3,2},{4,7},{5,4},{6,5},{7,6},{8,11},{9,8},{10,9... | collective-permute-start | bytes 884744 | tf_op jit(solution)/shard_map/ppermute | solution.py:293
  35.3 7.4 %copy-start.9 = (bf16[36,32,128]{2,1,0:T(8,128)(2,1)}, bf16[36,32,128]{2,1,0:T(8,128)(2,1)S(1)}, u32[]{:S(2)}) copy-start(bf16[36,32,128]{2,1,0:T(8,128)(2,1)S(1)} %collective-permute-done.refs_1_) | copy-start | bytes 884740
  35.3 7.4 %copy-start.10 = (bf16[36,32,128]{2,1,0:T(8,128)(2,1)}, bf16[36,32,128]{2,1,0:T(8,128)(2,1)S(1)}, u32[]{:S(2)}) copy-start(bf16[36,32,128]{2,1,0:T(8,128)(2,1)S(1)} %collective-permute-done.2.refs_3_) | copy-start | bytes 884740
  35.3 30.9 %collective-permute-start.6 = (bf16[37,32,128]{2,1,0:T(8,128)(2,1)S(1)}, bf16[37,32,128]{2,1,0:T(8,128)(2,1)S(1)}, u32[]{:S(2)}, u32[]{:S(2)}) collective-permute-start(bf16[37,32,128]{2,1,0:T(8,128)(2,1)S(1)} %get-tuple-element.42), channel_id=1, source_target_pairs={{0,1},{1,2},{2,3},{3,0},{4,5},{5,6},{6,7},{7,4},{8,9},{9,10},{10,1... | collective-permute-start | bytes 909320 | tf_op jit(solution)/shard_map/ppermute | solution.py:293
  40.3 25.9 %collective-permute-start.7 = (bf16[37,32,128]{2,1,0:T(8,128)(2,1)S(1)}, bf16[37,32,128]{2,1,0:T(8,128)(2,1)S(1)}, u32[]{:S(2)}, u32[]{:S(2)}) collective-permute-start(bf16[37,32,128]{2,1,0:T(8,128)(2,1)S(1)} %get-tuple-element.44), channel_id=1, source_target_pairs={{0,2},{1,3},{2,0},{3,1},{4,6},{5,7},{6,4},{7,5},{8,10},{9,11},{10,... | collective-permute-start | bytes 909320 | tf_op jit(solution)/shard_map/ppermute | solution.py:293
  41.7 24.5 %collective-permute-start.8 = (bf16[37,32,128]{2,1,0:T(8,128)(2,1)S(1)}, bf16[37,32,128]{2,1,0:T(8,128)(2,1)S(1)}, u32[]{:S(2)}, u32[]{:S(2)}) collective-permute-start(bf16[37,32,128]{2,1,0:T(8,128)(2,1)S(1)} %get-tuple-element.46), channel_id=1, source_target_pairs={{0,3},{1,0},{2,1},{3,2},{4,7},{5,4},{6,5},{7,6},{8,11},{9,8},{10,9... | collective-permute-start | bytes 909320 | tf_op jit(solution)/shard_map/ppermute | solution.py:293
  46.1 8.7 %collective-permute-start.9 = (bf16[36,32,128]{2,1,0:T(8,128)(2,1)}, bf16[36,32,128]{2,1,0:T(8,128)(2,1)S(1)}, u32[]{:S(2)}, u32[]{:S(2)}) collective-permute-start(bf16[36,32,128]{2,1,0:T(8,128)(2,1)} %get-tuple-element.50), channel_id=1, source_target_pairs={{0,4},{4,8},{8,12},{12,16},{16,20},{20,24},{24,28},{28,0},{1,5},{5... | collective-permute-start | bytes 884744 | tf_op jit(solution)/shard_map/ppermute | solution.py:348
  46.1 8.7 %collective-permute-start.10 = (bf16[36,32,128]{2,1,0:T(8,128)(2,1)}, bf16[36,32,128]{2,1,0:T(8,128)(2,1)S(1)}, u32[]{:S(2)}, u32[]{:S(2)}) collective-permute-start(bf16[36,32,128]{2,1,0:T(8,128)(2,1)} %get-tuple-element.51), channel_id=1, source_target_pairs={{0,28},{4,0},{8,4},{12,8},{16,12},{20,16},{24,20},{28,24},{1,29},{... | collective-permute-start | bytes 884744 | tf_op jit(solution)/shard_map/ppermute | solution.py:349
  54.8 0.7 copy-start.1
  55.6 0.7 copy-start.2
  66.2 0.7 copy-start.6
  66.3 0.8 copy-start.7
  67.1 0.8 copy-start.8
  71.7 12.1 %collective-permute-start.11 = (bf16[34,32,128]{2,1,0:T(8,128)(2,1)}, bf16[34,32,128]{2,1,0:T(8,128)(2,1)S(1)}, u32[]{:S(2)}, u32[]{:S(2)}) collective-permute-start(bf16[34,32,128]{2,1,0:T(8,128)(2,1)} %get-tuple-element.54), channel_id=1, source_target_pairs={{0,4},{4,8},{8,12},{12,16},{16,20},{20,24},{24,28},{28,0},{1,5},{5... | collective-permute-start | bytes 835592 | tf_op jit(solution)/shard_map/ppermute | solution.py:387
  72.8 10.9 %collective-permute-start.12 = (bf16[34,32,128]{2,1,0:T(8,128)(2,1)}, bf16[34,32,128]{2,1,0:T(8,128)(2,1)S(1)}, u32[]{:S(2)}, u32[]{:S(2)}) collective-permute-start(bf16[34,32,128]{2,1,0:T(8,128)(2,1)} %get-tuple-element.55), channel_id=1, source_target_pairs={{0,28},{4,0},{8,4},{12,8},{16,12},{20,16},{24,20},{28,24},{1,29},{... | collective-permute-start | bytes 835592 | tf_op jit(solution)/shard_map/ppermute | solution.py:388
  83.8 0.7 copy-start.11
  83.8 0.8 copy-start.12
  83.8 6.4 %collective-permute-start.13 = (f32[4,4,112,128]{3,2,1,0:T(8,128)}, f32[4,4,112,128]{3,2,1,0:T(8,128)S(1)}, u32[]{:S(2)}, u32[]{:S(2)}) collective-permute-start(f32[4,4,112,128]{3,2,1,0:T(8,128)} %get-tuple-element.61), channel_id=1, source_target_pairs={{0,4},{4,0},{8,12},{12,8},{16,20},{20,16},{24,28},{28,24},{1,5},{5... | collective-permute-start | bytes 2752520 | tf_op jit(solution)/shard_map/ppermute | solution.py:404
  84.6 5.6 %copy-start.5 = (f32[4,4,112,128]{3,2,1,0:T(8,128)S(1)}, f32[4,4,112,128]{3,2,1,0:T(8,128)}, u32[]{:S(2)}) copy-start(f32[4,4,112,128]{3,2,1,0:T(8,128)} %get-tuple-element.60) | copy-start | bytes 2752516
  90.4 9.8 %collective-permute-start.17 = (bf16[4,112,128]{2,1,0:T(8,128)(2,1)S(1)}, bf16[4,112,128]{2,1,0:T(8,128)(2,1)S(1)}, u32[]{:S(2)}, u32[]{:S(2)}) collective-permute-start(bf16[4,112,128]{2,1,0:T(8,128)(2,1)S(1)} %get-tuple-element.96), channel_id=1, source_target_pairs={{0,8},{4,12},{8,0},{12,4},{16,24},{20,28},{24,16},{28,20},{1,9},{5... | collective-permute-start | bytes 344072 | tf_op jit(solution)/shard_map/ppermute | solution.py:424
  91.1 9.1 %collective-permute-start.18 = (bf16[4,112,128]{2,1,0:T(8,128)(2,1)S(1)}, bf16[4,112,128]{2,1,0:T(8,128)(2,1)S(1)}, u32[]{:S(2)}, u32[]{:S(2)}) collective-permute-start(bf16[4,112,128]{2,1,0:T(8,128)(2,1)S(1)} %get-tuple-element.95), channel_id=1, source_target_pairs={{0,16},{4,20},{8,24},{12,28},{16,0},{20,4},{24,8},{28,12},{1,17},{... | collective-permute-start | bytes 344072 | tf_op jit(solution)/shard_map/ppermute | solution.py:424
  92.9 7.3 %collective-permute-start.19 = (bf16[4,112,128]{2,1,0:T(8,128)(2,1)S(1)}, bf16[4,112,128]{2,1,0:T(8,128)(2,1)S(1)}, u32[]{:S(2)}, u32[]{:S(2)}) collective-permute-start(bf16[4,112,128]{2,1,0:T(8,128)(2,1)S(1)} %get-tuple-element.94), channel_id=1, source_target_pairs={{0,24},{4,28},{8,16},{12,20},{16,8},{20,12},{24,0},{28,4},{1,25},{... | collective-permute-start | bytes 344072 | tf_op jit(solution)/shard_map/ppermute | solution.py:424
  100.2 30.7 %copy-start.4 = (bf16[32,32,128]{2,1,0:T(8,128)(2,1)S(1)}, bf16[32,32,128]{2,1,0:T(8,128)(2,1)}, u32[]{:S(2)}) copy-start(bf16[32,32,128]{2,1,0:T(8,128)(2,1)} %get-tuple-element.79) | copy-start | bytes 786436
  100.3 7.3 %collective-permute-start.22 = (f32[112,128]{1,0:T(8,128)S(1)}, f32[112,128]{1,0:T(8,128)S(1)}, u32[]{:S(2)}, u32[]{:S(2)}) collective-permute-start(f32[112,128]{1,0:T(8,128)S(1)} %get-tuple-element.98), channel_id=1, source_target_pairs={{0,3},{1,0},{2,1},{3,2},{4,7},{5,4},{6,5},{7,6},{8,11},{9,8},{10,9... | collective-permute-start | bytes 172040 | tf_op jit(solution)/shard_map/ppermute | solution.py:293
  103.2 16.8 %collective-permute-start.21 = (f32[112,128]{1,0:T(8,128)S(1)}, f32[112,128]{1,0:T(8,128)S(1)}, u32[]{:S(2)}, u32[]{:S(2)}) collective-permute-start(f32[112,128]{1,0:T(8,128)S(1)} %get-tuple-element.99), channel_id=1, source_target_pairs={{0,2},{1,3},{2,0},{3,1},{4,6},{5,7},{6,4},{7,5},{8,10},{9,11},{10,... | collective-permute-start | bytes 172040 | tf_op jit(solution)/shard_map/ppermute | solution.py:293
  103.2 16.8 %collective-permute-start.20 = (f32[112,128]{1,0:T(8,128)S(1)}, f32[112,128]{1,0:T(8,128)S(1)}, u32[]{:S(2)}, u32[]{:S(2)}) collective-permute-start(f32[112,128]{1,0:T(8,128)S(1)} %get-tuple-element.97), channel_id=1, source_target_pairs={{0,1},{1,2},{2,3},{3,0},{4,5},{5,6},{6,7},{7,4},{8,9},{9,10},{10,1... | collective-permute-start | bytes 172040 | tf_op jit(solution)/shard_map/ppermute | solution.py:293
  103.8 27.0 %collective-permute-start.14 = (bf16[32,32,128]{2,1,0:T(8,128)(2,1)}, bf16[32,32,128]{2,1,0:T(8,128)(2,1)S(1)}, u32[]{:S(2)}, u32[]{:S(2)}) collective-permute-start(bf16[32,32,128]{2,1,0:T(8,128)(2,1)} %get-tuple-element.70), channel_id=1, source_target_pairs={{0,1},{1,2},{2,3},{3,0},{4,5},{5,6},{6,7},{7,4},{8,9},{9,10},{10,1... | collective-permute-start | bytes 786440 | tf_op jit(solution)/shard_map/ppermute | solution.py:293
  106.7 24.1 %collective-permute-start.15 = (bf16[32,32,128]{2,1,0:T(8,128)(2,1)}, bf16[32,32,128]{2,1,0:T(8,128)(2,1)S(1)}, u32[]{:S(2)}, u32[]{:S(2)}) collective-permute-start(bf16[32,32,128]{2,1,0:T(8,128)(2,1)} %get-tuple-element.71), channel_id=1, source_target_pairs={{0,2},{1,3},{2,0},{3,1},{4,6},{5,7},{6,4},{7,5},{8,10},{9,11},{10,... | collective-permute-start | bytes 786440 | tf_op jit(solution)/shard_map/ppermute | solution.py:293
  107.6 23.2 %collective-permute-start.16 = (bf16[32,32,128]{2,1,0:T(8,128)(2,1)}, bf16[32,32,128]{2,1,0:T(8,128)(2,1)S(1)}, u32[]{:S(2)}, u32[]{:S(2)}) collective-permute-start(bf16[32,32,128]{2,1,0:T(8,128)(2,1)} %get-tuple-element.72), channel_id=1, source_target_pairs={{0,3},{1,0},{2,1},{3,2},{4,7},{5,4},{6,5},{7,6},{8,11},{9,8},{10,9... | collective-permute-start | bytes 786440 | tf_op jit(solution)/shard_map/ppermute | solution.py:293

commit v4 on v3

--- a/solution.py
+++ b/solution.py
@@ -57,6 +57,10 @@
     ]
 
 
+def pair_offsets(z, chan_count, group):
+    return [pl.multiple_of((z ^ j) * group, group) for j in range(chan_count)]
+
+
 def block_step(rows):
     return max(1, 1024 // rows)
 
@@ -74,7 +78,7 @@
     pieces = refs[:chan_count]
     first_ref, cells_ref, bottom_ref, top_ref = refs[chan_count:]
     columns, group, cells = pieces[0].shape
-    offsets = group_offsets(z_ref[0], chan_count, group, -1)
+    offsets = pair_offsets(z_ref[0], chan_count, group)
 
     def visit(k, count):
         for n in range(count):
@@ -89,12 +93,36 @@
     over_columns(columns, cells, visit)
 
 
-def weights_kernel(_, weights_ref, out_ref):
-    size = weights_ref.shape[1] // 3
+def share_plan(chan_count, space_count, rows):
+    far = chan_count - 1
+    plan = [(s % far + 1, s // far) for s in range(space_count)]
+    counts = [0] + [sum(step == k for step, _ in plan) for k in range(1, chan_count)]
+    return plan, [0] + [-(-rows // (16 * n)) * 16 for n in counts[1:]]
+
+
+def weights_kernel(chan_count, z_ref, own_ref, shares_ref, forward_ref, backward_ref):
+    offsets, group, channels = own_ref.shape
+    plan, sizes = share_plan(chan_count, shares_ref.shape[0], offsets * group)
+    places = group_offsets(z_ref[0], chan_count, group, -1)
+    for offset in range(offsets):
+        a, t, m = offset // 9, offset // 3 % 3, offset % 3
+        for j in range(chan_count):
+            for i in range(0, group, 16):
+                if j == 0:
+                    rows = own_ref[offset, i : i + 16]
+                else:
+                    source = offset * group + i
+                    part, row = divmod(source, sizes[j])
+                    rows = shares_ref[plan.index((j, part)), row : row + 16]
+                row = pl.multiple_of((3 * a + m) * channels + places[j] + i, 16)
+                forward_ref[pl.ds(row, 16), t * channels : (t + 1) * channels] = rows
     for k in range(9):
         for t in range(3):
-            tile = (slice(k * size, (k + 1) * size), slice(t * size, (t + 1) * size))
-            out_ref[tile] = weights_ref[tile].T
+            tile = (
+                slice(k * channels, (k + 1) * channels),
+                slice(t * channels, (t + 1) * channels),
+            )
+            backward_ref[tile] = forward_ref[tile].T
 
 
 def slope_of(pre):
@@ -162,7 +190,7 @@
     inner_ref, outer_ref, grad_ref, bottom_ref, top_ref, hold_ref = refs[chan_count:]
     group = pieces[0].shape[1]
     columns, cells, _ = grad_ref.shape
-    offsets = group_offsets(z_ref[0], chan_count, group, -1)
+    offsets = pair_offsets(z_ref[0], chan_count, group)
 
     def visit(k, count):
         for n in range(count):
@@ -226,21 +254,22 @@
             send_ref[chip, z] = pack_ref[z, pl.ds(other, shard), :]
 
 
-def input_kernel(chan_count, base, made, z_ref, grad_ref, low_ref, high_ref, weights_ref, *refs):
-    earlier, outs, hold_ref = refs[: -1 - chan_count], refs[-1 - chan_count : -1], refs[-1]
-    for out, old in zip(outs, earlier):
-        out[:made] = old[...]
+def input_kernel(chan_count, base, count, z_ref, grad_ref, low_ref, high_ref, weights_ref, *refs):
+    made, outs, hold_ref = refs[: -1 - chan_count], refs[-1 - chan_count : -1], refs[-1]
+    starts = [out.shape[0] - count for out in outs]
+    for out, old in zip([out for out, start in zip(outs, starts) if start], made):
+        out[: old.shape[0]] = old[...]
     columns, cells, channels = grad_ref.shape
     height = low_ref.shape[1]
     group = channels // chan_count
     offsets = group_offsets(z_ref[0], chan_count, group, 1)
 
-    def visit(k, count):
+    def visit(k, width):
         parts = [
             window(
-                grad_ref[pl.ds(base + k + 2 - b, count)],
-                kept(z_ref[1], low_ref[pl.ds(base + k + 2 - b, count)]),
-                kept(z_ref[2], high_ref[pl.ds(base + k + 2 - b, count)]),
+                grad_ref[pl.ds(base + k + 2 - b, width)],
+                kept(z_ref[1], low_ref[pl.ds(base + k + 2 - b, width)]),
+                kept(z_ref[2], high_ref[pl.ds(base + k + 2 - b, width)]),
                 2 - a,
                 height,
             )
@@ -248,14 +277,14 @@
             for b in range(3)
         ]
         total = convolve(parts, weights_ref[...], channels, height, True).astype(BF16)
-        total = total.reshape(count, cells, channels)
-        for n in range(count):
+        total = total.reshape(width, cells, channels)
+        for n in range(width):
             hold_ref[n] = total[n].T
         for j in range(chan_count):
-            for n in range(count):
-                outs[j][made + k + n] = hold_ref[n, pl.ds(offsets[j], group), :]
-
-    over_columns(outs[0].shape[0] - made, cells, visit)
+            for n in range(width):
+                outs[j][starts[j] + k + n] = hold_ref[n, pl.ds(offsets[j], group), :]
+
+    over_columns(count, cells, visit)
 
 
 def call(kernel, outs, scratch, flops, args, scalar):
@@ -281,10 +310,19 @@
     columns = width // chan_count
     return [
         lax.dynamic_slice_in_dim(
-            turned, lax.rem(z + j, chan_count) * columns, columns + before + behind, axis=0
+            turned, (z ^ j) * columns, columns + before + behind, axis=0
         )
         for j in range(chan_count)
     ]
+
+
+def swap(blocks):
+    count = len(blocks)
+    got = {
+        j: lax.ppermute(blocks[j], "chan", [(i, i ^ j) for i in range(count)])
+        for j in range(count - 1, 0, -1)
+    }
+    return [blocks[0]] + [got[j] for j in range(1, count)]
 
 
 def exchange(blocks, axis):
@@ -294,18 +332,22 @@
     ]
 
 
-def gather_filters(filters, z, s, chan_count, space_count, shard):
+def fetch_filters(filters, s, chan_count, space_count):
     offsets, group, channels = filters.shape
     rows = offsets * group
-    flat = jnp.pad(filters.reshape(rows, channels), ((0, space_count * shard - rows), (0, 0)))
-    mine = lax.dynamic_slice_in_dim(flat, s * shard, shard, axis=0)
-    got = [mine] + [
-        lax.ppermute(mine, "chan", ring(chan_count, j)) for j in range(1, chan_count)
+    plan, sizes = share_plan(chan_count, space_count, rows)
+    starts = [part * sizes[step] for step, part in plan]
+    size = max(sizes)
+    flat = jnp.pad(filters.reshape(rows, channels), ((0, max(starts) + size - rows), (0, 0)))
+    far = chan_count - 1
+    per_part = sum((s % far + 1 == k) * sizes[k] for k in range(1, chan_count))
+    mine = lax.dynamic_slice_in_dim(flat, s // far * per_part, size, axis=0)
+    route = [
+        (place * chan_count + z, place * chan_count + (z + step) % chan_count)
+        for place, (step, _) in enumerate(plan)
+        for z in range(chan_count)
     ]
-    doubled = jnp.stack(got[::-1] + got[::-1])
-    shares = lax.dynamic_slice_in_dim(doubled, chan_count - 1 - z, chan_count, axis=0)
-    whole = lax.all_gather(shares, "space", axis=1, tiled=True)
-    return whole[:, :rows].reshape(chan_count, 3, 3, 3, group, channels)
+    return lax.ppermute(mine, ("space", "chan"), route)
 
 
 def body(inputs, filters, cotangent):
@@ -323,14 +365,18 @@
     z_arg = jnp.stack([z] + flags)
     macs = 27 * channels * channels * columns * cells
 
-    x_pieces = exchange(column_blocks(inputs, 2, 2, z, chan_count), "chan")
-    shard = -(-27 * group // (16 * space_count)) * 16
-    by_offset = gather_filters(filters, z, s, chan_count, space_count, shard)
-    weights_f = by_offset.transpose(1, 3, 0, 4, 2, 5).reshape(9 * channels, 3 * channels)
-    c_blocks = column_blocks(cotangent, 1, 4, z, chan_count)
-    weights_b = call(
-        weights_kernel, [shape(weights_f.shape, BF16)], [], 0, [weights_f], z_arg
-    )[0]
+    share = fetch_filters(filters, s, chan_count, space_count)
+    x_pieces = swap(after(column_blocks(inputs, 2, 2, z, chan_count), share))
+    shares = lax.all_gather(share, "space", axis=0, tiled=False)
+    c_blocks = column_blocks(after(cotangent, shares), 1, 4, z, chan_count)
+    weights_f, weights_b = call(
+        functools.partial(weights_kernel, chan_count),
+        [shape((9 * channels, 3 * channels), BF16)] * 2,
+        [],
+        0,
+        [filters, shares],
+        z_arg,
+    )
     x_pieces = after(x_pieces, weights_b, z_arg, c_blocks)
 
     x_first, x_cells, x_bottom, x_top = call(
@@ -347,9 +393,7 @@
     )
     x_low = lax.ppermute(x_top, "space", upward)
     x_high = lax.ppermute(x_bottom, "space", downward)
-    c_pieces = exchange(
-        c_blocks[:1] + [after(c, x) for c, x in zip(c_blocks[1:], x_pieces[1:])], "chan"
-    )
+    c_pieces = swap(c_blocks[:1] + [after(c, x) for c, x in zip(c_blocks[1:], x_pieces[1:])])
     slope_inner = call(
         functools.partial(forward_inner_kernel, height),
         [shape((columns + 2, cells - 2 * height, channels), F32)],
@@ -388,6 +432,7 @@
     g_high = lax.ppermute(g_bottom, "space", downward)
 
     chips = space_count // 2
+    shard = -(-27 * group // (16 * space_count)) * 16
     half = shape((chips, chan_count, shard, channels), F32)
     keep, send = call(
         functools.partial(filter_kernel, chan_count, space_count, shard, height),
@@ -402,16 +447,18 @@
     )
     g_low, g_high, send = lax.optimization_barrier((g_low, g_high, send))
     from_core = lax.ppermute(send, "space", [(i, i ^ 1) for i in range(space_count)])
-    half_columns = columns // 2
+    early = columns // 2
+    split = range(1, min(3, chan_count))
     hold = [pltpu.VMEM((block_step(cells), channels, cells), BF16)]
     first = call(
-        functools.partial(input_kernel, chan_count, 0, 0),
-        [shape((half_columns, group, cells), BF16)] * chan_count,
+        functools.partial(input_kernel, chan_count, 0, early),
+        [shape((early, group, cells), BF16)] * chan_count,
         hold,
         3 * macs,
         [grad, g_low, g_high, weights_b],
         z_arg,
     )
+    returned_first = {j: lax.ppermute(first[j], "chan", ring(chan_count, j)) for j in split}
     pair_sum = keep + after(from_core, first[0])
     chip = s // 2
     chip_sum = lax.dynamic_index_in_dim(pair_sum, chip, 0, keepdims=False)
@@ -423,17 +470,23 @@
         from_chips.append(
             lax.ppermute(block, "space", [(i, i ^ (2 * k)) for i in range(space_count)])
         )
+    whole_blocks = [j for j in range(chan_count) if j not in split]
     back = call(
-        functools.partial(input_kernel, chan_count, half_columns, half_columns),
-        [shape((columns, group, cells), BF16)] * chan_count,
+        functools.partial(input_kernel, chan_count, early, columns - early),
+        [
+            shape((columns if j in whole_blocks else columns - early, group, cells), BF16)
+            for j in range(chan_count)
+        ],
         hold,
         3 * macs,
-        [grad, g_low, g_high, weights_b, *first],
+        [grad, g_low, g_high, weights_b] + [first[j] for j in whole_blocks],
         z_arg,
     )
     returned = exchange(back, "chan")
-    for got in after(from_chips, back[0]):
+    from_chips, returned_first = after((from_chips, returned_first), back[0])
+    for got in from_chips:
         chip_sum = chip_sum + got.astype(F32)
+    chip_sum = after(chip_sum, returned_first)
     parts = [
         lax.dynamic_index_in_dim(chip_sum, lax.rem(z + j, chan_count), 0, keepdims=False)
         for j in range(chan_count)
@@ -445,7 +498,11 @@
     whole = lax.all_gather(shard_sum, "space", axis=0, tiled=True)
     grad_w = whole[: 27 * group].reshape(27, group, channels)
 
-    reverse = returned[::-1]
+    reverse = [
+        part
+        for j in range(chan_count)[::-1]
+        for part in ([returned_first[j]] if j in split else []) + [returned[j]]
+    ]
     doubled = jnp.concatenate(reverse + reverse, axis=0)
     start = lax.rem(chan_count - 1 - z + chan_count, chan_count) * columns
     ordered = lax.dynamic_slice_in_dim(doubled, start, width, axis=0)

time: 134 us -> 130 us (0.970)
  local copies, waits for them, and re-layouts: 16.2 us -> 12.3 us
    ppermute x12 -> x6, starting transfers between devices: 21.2 us -> 8.14 us  [exchange(): lax.ppermute(blocks[j], axis, ring(count, j))]
    ppermute x3 -> x9, starting transfers between devices: 6.06 us -> 18.9 us  [the longest x6 12.9 us: swap(): lax.ppermute(blocks[j], 'chan', [(i, i ^ j) for i in range(count)])]
    ppermute x12 -> x6, waiting for transfers between devices: 10.7 us -> 5.94 us  [exchange(): lax.ppermute(blocks[j], axis, ring(count, j))]
    ppermute x3 -> x9, waiting for transfers between devices: 0.01 us -> 4.43 us  [the longest x6 2.69 us: swap(): lax.ppermute(blocks[j], 'chan', [(i, i ^ j) for i in range(count)])]
    unnamed x41 -> x33, local copies, waits for them, and re-layouts: 6.54 us -> 3.91 us
    all_gather x1, blocking collectives: 11 us -> 12.4 us  [body(): shares = lax.all_gather(share, 'space', axis=0, tiled=False)]
    dynamic_slice x4 -> x3, local copies, waits for them, and re-layouts: 3.36 us -> 2.88 us  [the longest x2 1.95 us: column_blocks(): lax.dynamic_slice_in_dim(turned, (z ^ j) * columns, columns + before + be...]
  transfers between devices with their start and end apart: 23 -> 23, of which waited for: 1 -> 4; matrix products, arithmetic and copies ran while one was open for 7% -> 5% of each run, Pallas kernels for 32% -> 33%
where the time goes in v4:
time: 130 us
  Pallas kernels  46.8 us (36%)
  starting transfers between devices  36.3 us (28%)
  blocking collectives  22 us (17%)
  local copies, waits for them, and re-layouts  12.3 us (9%)
  waiting for transfers between devices  10.4 us (8%)
    pallas_call x9, Pallas kernels, call(): pl.pallas_call(kernel, out_shape=outs, in_specs=[pl.BlockSpec(memory_spac...  46.8 us
    ppermute x6, starting transfers between devices, swap(): lax.ppermute(blocks[j], 'chan', [(i, i ^ j) for i in range(count)])  12.9 us
    all_gather x1, blocking collectives, body(): shares = lax.all_gather(share, 'space', axis=0, tiled=False)  12.4 us
    all_gather x1, blocking collectives, body(): whole = lax.all_gather(shard_sum, 'space', axis=0, tiled=True)  9.64 us
    ppermute x6, starting transfers between devices, exchange(): lax.ppermute(blocks[j], axis, ring(count, j))  8.14 us
    ppermute x6, waiting for transfers between devices, exchange(): lax.ppermute(blocks[j], axis, ring(count, j))  5.94 us
    ppermute x3, starting transfers between devices, body(): lax.ppermute(block, 'space', [(i, i ^ 2 * k) for i in range(space_count)])  3.94 us
    unnamed x33, local copies, waits for them, and re-layouts  3.91 us
  transfers between devices with their start and end apart: 23, of which 4 were waited for; matrix products, arithmetic and copies ran while one was open for 5% of the time, Pallas kernels for 33%

profile of v4, /device:TPU:0, one launch (start us, length us, event | category | flops | bytes accessed | tf_op | source)
XLA Modules:
  0.0 129.8 jit_solution(12699695801926443061)
XLA Ops:
  0.7 0.9 pad_dynamic-slice_fusion.8
  1.6 3.1 %collective-permute-start = (bf16[432,128]{1,0:T(8,128)(2,1)S(1)}, bf16[432,128]{1,0:T(8,128)(2,1)S(1)}, u32[]{:S(2)}, u32[]{:S(2)}) collective-permute-start(bf16[432,128]{1,0:T(8,128)(2,1)S(1)} %pad_dynamic-slice_fusion.8), channel_id=1, source_target_pairs={{0,1},{1,2},{2,3},{3,0},{4,6},{5,7},{6,4},{7,5},{8,11},{9,8},{10,9... | collective-permute-start | bytes 331784 | tf_op jit(solution)/shard_map/ppermute | solution.py:350
  4.7 1.9 %copy.9 = bf16[32,128,128]{1,0,2:T(8,128)(2,1)S(1)} copy(bf16[32,128,128]{2,1,0:T(8,128)(2,1)} %bitcast.42) | data formatting | bytes 2097152 | tf_op jit(solution)/shard_map/reshape | solution.py:308
  6.6 1.0 pad_dynamic-slice_fusion.4
  7.6 0.6 pad_add_fusion.z_ref._
  8.3 1.6 %collective-permute-done = bf16[432,128]{1,0:T(8,128)(2,1)S(1)} collective-permute-done((bf16[432,128]{1,0:T(8,128)(2,1)S(1)}, bf16[432,128]{1,0:T(8,128)(2,1)S(1)}, u32[]{:S(2)}, u32[]{:S(2)}) %collective-permute-start) | collective-permute-done | bytes 110624 | tf_op jit(solution)/shard_map/ppermute | solution.py:350
  9.9 0.8 collective-permute-start.1
  10.7 1.9 %collective-permute-start.2 = (bf16[36,32,128]{2,1,0:T(8,128)(2,1)S(1)}, bf16[36,32,128]{2,1,0:T(8,128)(2,1)}, u32[]{:S(2)}, u32[]{:S(2)}) collective-permute-start(bf16[36,32,128]{2,1,0:T(8,128)(2,1)S(1)} %get-tuple-element.54), channel_id=1, source_target_pairs={{0,2},{1,3},{2,0},{3,1},{4,6},{5,7},{6,4},{7,5},{8,10},{9,11},{10,... | collective-permute-start | bytes 884744 | tf_op jit(solution)/shard_map/ppermute | solution.py:322
  12.6 1.7 %collective-permute-start.3 = (bf16[36,32,128]{2,1,0:T(8,128)(2,1)S(1)}, bf16[36,32,128]{2,1,0:T(8,128)(2,1)}, u32[]{:S(2)}, u32[]{:S(2)}) collective-permute-start(bf16[36,32,128]{2,1,0:T(8,128)(2,1)S(1)} %get-tuple-element.55), channel_id=1, source_target_pairs={{0,3},{1,2},{2,1},{3,0},{4,7},{5,6},{6,5},{7,4},{8,11},{9,10},{10,... | collective-permute-start | bytes 884744 | tf_op jit(solution)/shard_map/ppermute | solution.py:322
  14.3 12.4 %all-gather = bf16[3456,128]{1,0:T(8,128)(2,1)} all-gather(bf16[432,128]{1,0:T(8,128)(2,1)S(1)} %collective-permute-done), channel_id=2, replica_groups=mesh['space'=8,'chan'=4] {'space'}, dimensions={0}, use_global_device_ids=true | all-gather | bytes 995328 | tf_op jit(solution)/shard_map/all_gather | solution.py:370
  26.7 1.0 copy.8
  27.7 2.9 %shard_map.50 = (bf16[1152,384]{1,0:T(8,128)(2,1)}, bf16[1152,384]{1,0:T(8,128)(2,1)}) custom-call(s32[3]{0:T(128)} %pad_add_fusion.z_ref._, bf16[27,32,128]{2,1,0:T(8,128)(2,1)} %own_ref.1, bf16[8,432,128]{2,1,0:T(8,128)(2,1)} %bitcast.41), custom_call_target="tpu_custom_call" | custom-call | tf_op jit(solution)/shard_map/pallas_call | solution.py:292
  30.6 1.0 pad_dynamic-slice_fusion
  31.5 2.7 %collective-permute-done.2.refs_2_ = bf16[36,32,128]{2,1,0:T(8,128)(2,1)} collective-permute-done((bf16[36,32,128]{2,1,0:T(8,128)(2,1)S(1)}, bf16[36,32,128]{2,1,0:T(8,128)(2,1)}, u32[]{:S(2)}, u32[]{:S(2)}) %collective-permute-start.2) | collective-permute-done | bytes 294944 | tf_op jit(solution)/shard_map/ppermute | solution.py:322
  34.2 6.1 %collective-permute-start.4 = (bf16[37,32,128]{2,1,0:T(8,128)(2,1)S(1)}, bf16[37,32,128]{2,1,0:T(8,128)(2,1)S(1)}, u32[]{:S(2)}, u32[]{:S(2)}) collective-permute-start(bf16[37,32,128]{2,1,0:T(8,128)(2,1)S(1)} %get-tuple-element.58), channel_id=1, source_target_pairs={{0,1},{1,0},{2,3},{3,2},{4,5},{5,4},{6,7},{7,6},{8,9},{9,8},{10,11... | collective-permute-start | bytes 909320 | tf_op jit(solution)/shard_map/ppermute | solution.py:322
  40.4 0.9 collective-permute-start.5
  41.3 1.5 %collective-permute-start.6 = (bf16[37,32,128]{2,1,0:T(8,128)(2,1)S(1)}, bf16[37,32,128]{2,1,0:T(8,128)(2,1)S(1)}, u32[]{:S(2)}, u32[]{:S(2)}) collective-permute-start(bf16[37,32,128]{2,1,0:T(8,128)(2,1)S(1)} %get-tuple-element.62), channel_id=1, source_target_pairs={{0,3},{1,2},{2,1},{3,0},{4,7},{5,6},{6,5},{7,4},{8,11},{9,10},{10,... | collective-permute-start | bytes 909320 | tf_op jit(solution)/shard_map/ppermute | solution.py:322
  42.7 3.4 %shard_map.51 = (bf16[36,128,128]{2,1,0:T(8,128)(2,1)}, bf16[36,128,128]{2,1,0:T(8,128)(2,1)}, bf16[36,32,128]{2,1,0:T(8,128)(2,1)}, bf16[36,32,128]{2,1,0:T(8,128)(2,1)}) custom-call(s32[3]{0:T(128)} %pad_add_fusion.z_ref._, bf16[36,32,128]{2,1,0:T(8,128)(2,1)} %get-tuple-element.63.refs_0_, bf16[36,32,128]{2,1,0:T(8,128)(2,1)} %copy-done.8, ...), custom_call_target="tpu_custom_call" | custom-call | tf_op jit(solution)/shard_map/pallas_call | solution.py:292
  46.1 2.6 %collective-permute-start.8 = (bf16[36,32,128]{2,1,0:T(8,128)(2,1)}, bf16[36,32,128]{2,1,0:T(8,128)(2,1)S(1)}, u32[]{:S(2)}, u32[]{:S(2)}) collective-permute-start(bf16[36,32,128]{2,1,0:T(8,128)(2,1)} %get-tuple-element.68), channel_id=1, source_target_pairs={{0,28},{4,0},{8,4},{12,8},{16,12},{20,16},{24,20},{28,24},{1,29},{... | collective-permute-start | bytes 884744 | tf_op jit(solution)/shard_map/ppermute | solution.py:395
  48.8 6.1 %shard_map.52.refs_4_ = f32[34,64,128]{2,1,0:T(8,128)} custom-call(s32[3]{0:T(128)} %pad_add_fusion.z_ref._, bf16[36,128,128]{2,1,0:T(8,128)(2,1)} %get-tuple-element.66.x_ref, bf16[1152,384]{1,0:T(8,128)(2,1)} %get-tuple-element.65.weights_ref), custom_call_target="tpu_custom_call" | custom-call | tf_op jit(solution)/shard_map/pallas_call | solution.py:292
  54.9 0.7 copy-done
  55.6 0.7 copy-done.1
  56.3 3.7 %shard_map.54.sides_ref = bf16[2,34,128,128]{3,2,1,0:T(8,128)(2,1)} custom-call(s32[3]{0:T(128)} %pad_add_fusion.z_ref._, bf16[36,128,128]{2,1,0:T(8,128)(2,1)} %get-tuple-element.66.x_ref, bf16[36,32,128]{2,1,0:T(8,128)(2,1)} %copy-done, bf16[36,32,128]{2,1,0:T(8,128)(2,1)} %copy-done.1), custom_call_target="tpu_custom_call" | custom-call | tf_op jit(solution)/shard_map/pallas_call | solution.py:292
  60.0 6.3 %shard_map.53.refs_5_ = f32[34,64,128]{2,1,0:T(8,128)} custom-call(s32[3]{0:T(128)} %pad_add_fusion.z_ref._, bf16[36,128,128]{2,1,0:T(8,128)(2,1)} %get-tuple-element.66.x_ref, bf16[36,32,128]{2,1,0:T(8,128)(2,1)} %copy-done, bf16[36,32,128]{2,1,0:T(8,128)(2,1)} %copy-done.1, bf16[1152,384]{1,0:T(8,128)(2,1)} %get-tuple-element.65.weights_ref), custom_call_target="tpu_custom_call" | custom-call | tf_op jit(solution)/shard_map/pallas_call | solution.py:292
  66.3 0.7 copy-done.5
  67.1 0.8 copy-done.7
  67.8 3.8 %shard_map.55 = (bf16[34,128,128]{2,1,0:T(8,128)(2,1)}, bf16[34,32,128]{2,1,0:T(8,128)(2,1)}, bf16[34,32,128]{2,1,0:T(8,128)(2,1)}) custom-call(s32[3]{0:T(128)} %pad_add_fusion.z_ref._, bf16[37,32,128]{2,1,0:T(8,128)(2,1)} %get-tuple-element.109.refs_0_, bf16[37,32,128]{2,1,0:T(8,128)(2,1)} %copy-done.5, bf16[37,32,128]{2,1,0:T(8,128)(2,1)} %copy-done.6, ...), custom_call_target="tpu_custom_call" | custom-call | flops 5242880 | bytes 5111808 | tf_op jit(solution)/shard_map/pallas_call | solution.py:292
  71.6 2.6 %collective-permute-start.10 = (bf16[34,32,128]{2,1,0:T(8,128)(2,1)}, bf16[34,32,128]{2,1,0:T(8,128)(2,1)S(1)}, u32[]{:S(2)}, u32[]{:S(2)}) collective-permute-start(bf16[34,32,128]{2,1,0:T(8,128)(2,1)} %get-tuple-element.72), channel_id=1, source_target_pairs={{0,28},{4,0},{8,4},{12,8},{16,12},{20,16},{24,20},{28,24},{1,29},{... | collective-permute-start | bytes 835592 | tf_op jit(solution)/shard_map/ppermute | solution.py:432
  74.3 9.4 %shard_map.56 = (f32[4,4,112,128]{3,2,1,0:T(8,128)}, f32[4,4,112,128]{3,2,1,0:T(8,128)}) custom-call(s32[1]{0:T(128)} %bitcast.9.core_ref, bf16[36,128,128]{2,1,0:T(8,128)(2,1)} %get-tuple-element.73.x_ref, bf16[2,34,128,128]{3,2,1,0:T(8,128)(2,1)} %shard_map.54.sides_ref, bf16[34,128,128]{2,1,0:T(8,128)(2,1)} %get-tuple-element.70.grad_ref), custom_call_target="tpu_custom_call" | custom-call | tf_op jit(solution)/shard_map/pallas_call | solution.py:292
  83.9 0.6 copy-done.9
  84.5 5.6 %shard_map.57 = (bf16[16,32,128]{2,1,0:T(8,128)(2,1)}, bf16[16,32,128]{2,1,0:T(8,128)(2,1)}, bf16[16,32,128]{2,1,0:T(8,128)(2,1)}, bf16[16,32,128]{2,1,0:T(8,128)(2,1)}) custom-call(s32[3]{0:T(128)} %pad_add_fusion.z_ref._, bf16[34,128,128]{2,1,0:T(8,128)(2,1)} %get-tuple-element.70.grad_ref, bf16[34,32,128]{2,1,0:T(8,128)(2,1)} %copy-done.9, ...), custom_call_target="tpu_custom_call" | custom-call | flops 5435817984 | bytes 3080192 | tf_op jit(solution)/shard_map/pallas_call | solution.py:292
  90.1 2.5 %collective-permute-start.18 = (bf16[16,32,128]{2,1,0:T(8,128)(2,1)}, bf16[16,32,128]{2,1,0:T(8,128)(2,1)S(1)}, u32[]{:S(2)}, u32[]{:S(2)}) collective-permute-start(bf16[16,32,128]{2,1,0:T(8,128)(2,1)} %get-tuple-element.88), channel_id=1, source_target_pairs={{0,1},{1,2},{2,3},{3,0},{4,5},{5,6},{6,7},{7,4},{8,9},{9,10},{10,1... | collective-permute-start | bytes 393224 | tf_op jit(solution)/shard_map/ppermute | solution.py:461
  92.6 0.5 collective-permute-start.19
  93.1 0.1 fusion.5
  93.3 0.7 collective-permute-start.15
  94.0 1.8 %collective-permute-start.16 = (bf16[4,112,128]{2,1,0:T(8,128)(2,1)S(1)}, bf16[4,112,128]{2,1,0:T(8,128)(2,1)S(1)}, u32[]{:S(2)}, u32[]{:S(2)}) collective-permute-start(bf16[4,112,128]{2,1,0:T(8,128)(2,1)S(1)} %get-tuple-element.115), channel_id=1, source_target_pairs={{0,16},{4,20},{8,24},{12,28},{16,0},{20,4},{24,8},{28,12},{1,17},{... | collective-permute-start | bytes 344072 | tf_op jit(solution)/shard_map/ppermute | solution.py:471
  95.8 1.4 %collective-permute-start.17 = (bf16[4,112,128]{2,1,0:T(8,128)(2,1)S(1)}, bf16[4,112,128]{2,1,0:T(8,128)(2,1)S(1)}, u32[]{:S(2)}, u32[]{:S(2)}) collective-permute-start(bf16[4,112,128]{2,1,0:T(8,128)(2,1)S(1)} %get-tuple-element.114), channel_id=1, source_target_pairs={{0,24},{4,28},{8,16},{12,20},{16,8},{20,12},{24,0},{28,4},{1,25},{... | collective-permute-start | bytes 344072 | tf_op jit(solution)/shard_map/ppermute | solution.py:471
  97.2 5.7 %shard_map.58 = (bf16[32,32,128]{2,1,0:T(8,128)(2,1)}, bf16[16,32,128]{2,1,0:T(8,128)(2,1)}, bf16[16,32,128]{2,1,0:T(8,128)(2,1)}, bf16[32,32,128]{2,1,0:T(8,128)(2,1)}) custom-call(s32[3]{0:T(128)} %pad_add_fusion.z_ref._, bf16[34,128,128]{2,1,0:T(8,128)(2,1)} %get-tuple-element.70.grad_ref, bf16[34,32,128]{2,1,0:T(8,128)(2,1)} %copy-done.9, ...), custom_call_target="tpu_custom_call" | custom-call | flops 5435817984 | bytes 3604480 | tf_op jit(solution)/shard_map/pallas_call | solution.py:292
  103.1 2.0 %collective-permute-start.22 = (f32[112,128]{1,0:T(8,128)S(1)}, f32[112,128]{1,0:T(8,128)S(1)}, u32[]{:S(2)}, u32[]{:S(2)}) collective-permute-start(f32[112,128]{1,0:T(8,128)S(1)} %get-tuple-element.118), channel_id=1, source_target_pairs={{0,3},{1,0},{2,1},{3,2},{4,7},{5,4},{6,5},{7,6},{8,11},{9,8},{10,9... | collective-permute-start | bytes 172040 | tf_op jit(solution)/shard_map/ppermute | solution.py:331
  105.1 0.9 collective-permute-start.21
  106.0 1.2 collective-permute-start.20
  107.2 1.4 %collective-permute-start.12 = (bf16[16,32,128]{2,1,0:T(8,128)(2,1)}, bf16[16,32,128]{2,1,0:T(8,128)(2,1)S(1)}, u32[]{:S(2)}, u32[]{:S(2)}) collective-permute-start(bf16[16,32,128]{2,1,0:T(8,128)(2,1)} %get-tuple-element.85), channel_id=1, source_target_pairs={{0,1},{1,2},{2,3},{3,0},{4,5},{5,6},{6,7},{7,4},{8,9},{9,10},{10,1... | collective-permute-start | bytes 393224 | tf_op jit(solution)/shard_map/ppermute | solution.py:331
  108.6 1.8 %collective-permute-start.13 = (bf16[16,32,128]{2,1,0:T(8,128)(2,1)}, bf16[16,32,128]{2,1,0:T(8,128)(2,1)S(1)}, u32[]{:S(2)}, u32[]{:S(2)}) collective-permute-start(bf16[16,32,128]{2,1,0:T(8,128)(2,1)} %get-tuple-element.86), channel_id=1, source_target_pairs={{0,2},{1,3},{2,0},{3,1},{4,6},{5,7},{6,4},{7,5},{8,10},{9,11},{10,... | collective-permute-start | bytes 393224 | tf_op jit(solution)/shard_map/ppermute | solution.py:331
  110.4 0.9 collective-permute-start.14
  111.2 5.9 %collective-permute-done.21 = f32[112,128]{1,0:T(8,128)S(1)} collective-permute-done((f32[112,128]{1,0:T(8,128)S(1)}, f32[112,128]{1,0:T(8,128)S(1)}, u32[]{:S(2)}, u32[]{:S(2)}) %collective-permute-start.21) | collective-permute-done | bytes 57376 | tf_op jit(solution)/shard_map/ppermute | solution.py:331
  117.2 9.6 %all_gather.11 = f32[896,128]{1,0:T(8,128)S(1)} all-gather(f32[112,128]{1,0:T(8,128)S(1)} %broadcast_multiply_fusion), channel_id=1, replica_groups=mesh['space'=8,'chan'=4] {'space'}, dimensions={0}, use_global_device_ids=true | all-gather | bytes 516096 | tf_op jit(solution)/shard_map/all_gather | solution.py:498
  126.8 0.8 slice.4
  128.1 1.7 %copy.10 = bf16[32,128,128]{2,1,0:T(8,128)(2,1)} copy(bf16[32,128,128]{1,0,2:T(8,128)(2,1)S(1)} %dynamic-slice_bitcast_fusion) | data formatting | bytes 2097152 | tf_op jit(solution)/shard_map/transpose | solution.py:509
  (57 shorter events, 0.9 us)
Async XLA Ops:
  1.6 8.3 %collective-permute-start = (bf16[432,128]{1,0:T(8,128)(2,1)S(1)}, bf16[432,128]{1,0:T(8,128)(2,1)S(1)}, u32[]{:S(2)}, u32[]{:S(2)}) collective-permute-start(bf16[432,128]{1,0:T(8,128)(2,1)S(1)} %pad_dynamic-slice_fusion.8), channel_id=1, source_target_pairs={{0,1},{1,2},{2,3},{3,0},{4,6},{5,7},{6,4},{7,5},{8,11},{9,8},{10,9... | collective-permute-start | bytes 331784 | tf_op jit(solution)/shard_map/ppermute | solution.py:350
  6.6 20.1 %copy-start.2 = (bf16[32,4,32,128]{3,2,1,0:T(8,128)(2,1)S(1)}, bf16[32,4,32,128]{3,2,1,0:T(8,128)(2,1)}, u32[]{:S(2)}) copy-start(bf16[32,4,32,128]{3,2,1,0:T(8,128)(2,1)} %param.5) | copy-start | bytes 3145732
  9.9 21.6 %collective-permute-start.1 = (bf16[36,32,128]{2,1,0:T(8,128)(2,1)S(1)}, bf16[36,32,128]{2,1,0:T(8,128)(2,1)S(1)}, u32[]{:S(2)}, u32[]{:S(2)}) collective-permute-start(bf16[36,32,128]{2,1,0:T(8,128)(2,1)S(1)} %get-tuple-element.53), channel_id=1, source_target_pairs={{0,1},{1,0},{2,3},{3,2},{4,5},{5,4},{6,7},{7,6},{8,9},{9,8},{10,11... | collective-permute-start | bytes 884744 | tf_op jit(solution)/shard_map/ppermute | solution.py:322
  10.7 23.5 %collective-permute-start.2 = (bf16[36,32,128]{2,1,0:T(8,128)(2,1)S(1)}, bf16[36,32,128]{2,1,0:T(8,128)(2,1)}, u32[]{:S(2)}, u32[]{:S(2)}) collective-permute-start(bf16[36,32,128]{2,1,0:T(8,128)(2,1)S(1)} %get-tuple-element.54), channel_id=1, source_target_pairs={{0,2},{1,3},{2,0},{3,1},{4,6},{5,7},{6,4},{7,5},{8,10},{9,11},{10,... | collective-permute-start | bytes 884744 | tf_op jit(solution)/shard_map/ppermute | solution.py:322
  12.6 21.6 %collective-permute-start.3 = (bf16[36,32,128]{2,1,0:T(8,128)(2,1)S(1)}, bf16[36,32,128]{2,1,0:T(8,128)(2,1)}, u32[]{:S(2)}, u32[]{:S(2)}) collective-permute-start(bf16[36,32,128]{2,1,0:T(8,128)(2,1)S(1)} %get-tuple-element.55), channel_id=1, source_target_pairs={{0,3},{1,2},{2,1},{3,0},{4,7},{5,6},{6,5},{7,4},{8,11},{9,10},{10,... | collective-permute-start | bytes 884744 | tf_op jit(solution)/shard_map/ppermute | solution.py:322
  31.5 11.2 %copy-start.8 = (bf16[36,32,128]{2,1,0:T(8,128)(2,1)}, bf16[36,32,128]{2,1,0:T(8,128)(2,1)S(1)}, u32[]{:S(2)}) copy-start(bf16[36,32,128]{2,1,0:T(8,128)(2,1)S(1)} %collective-permute-done.1.refs_1_) | copy-start | bytes 884740
  34.2 32.0 %collective-permute-start.4 = (bf16[37,32,128]{2,1,0:T(8,128)(2,1)S(1)}, bf16[37,32,128]{2,1,0:T(8,128)(2,1)S(1)}, u32[]{:S(2)}, u32[]{:S(2)}) collective-permute-start(bf16[37,32,128]{2,1,0:T(8,128)(2,1)S(1)} %get-tuple-element.58), channel_id=1, source_target_pairs={{0,1},{1,0},{2,3},{3,2},{4,5},{5,4},{6,7},{7,6},{8,9},{9,8},{10,11... | collective-permute-start | bytes 909320 | tf_op jit(solution)/shard_map/ppermute | solution.py:322
  40.4 25.9 %collective-permute-start.5 = (bf16[37,32,128]{2,1,0:T(8,128)(2,1)S(1)}, bf16[37,32,128]{2,1,0:T(8,128)(2,1)S(1)}, u32[]{:S(2)}, u32[]{:S(2)}) collective-permute-start(bf16[37,32,128]{2,1,0:T(8,128)(2,1)S(1)} %get-tuple-element.60), channel_id=1, source_target_pairs={{0,2},{1,3},{2,0},{3,1},{4,6},{5,7},{6,4},{7,5},{8,10},{9,11},{10,... | collective-permute-start | bytes 909320 | tf_op jit(solution)/shard_map/ppermute | solution.py:322
  41.3 25.0 %collective-permute-start.6 = (bf16[37,32,128]{2,1,0:T(8,128)(2,1)S(1)}, bf16[37,32,128]{2,1,0:T(8,128)(2,1)S(1)}, u32[]{:S(2)}, u32[]{:S(2)}) collective-permute-start(bf16[37,32,128]{2,1,0:T(8,128)(2,1)S(1)} %get-tuple-element.62), channel_id=1, source_target_pairs={{0,3},{1,2},{2,1},{3,0},{4,7},{5,6},{6,5},{7,4},{8,11},{9,10},{10,... | collective-permute-start | bytes 909320 | tf_op jit(solution)/shard_map/ppermute | solution.py:322
  46.1 8.7 %collective-permute-start.7 = (bf16[36,32,128]{2,1,0:T(8,128)(2,1)}, bf16[36,32,128]{2,1,0:T(8,128)(2,1)S(1)}, u32[]{:S(2)}, u32[]{:S(2)}) collective-permute-start(bf16[36,32,128]{2,1,0:T(8,128)(2,1)} %get-tuple-element.67), channel_id=1, source_target_pairs={{0,4},{4,8},{8,12},{12,16},{16,20},{20,24},{24,28},{28,0},{1,5},{5... | collective-permute-start | bytes 884744 | tf_op jit(solution)/shard_map/ppermute | solution.py:394
  46.1 8.7 %collective-permute-start.8 = (bf16[36,32,128]{2,1,0:T(8,128)(2,1)}, bf16[36,32,128]{2,1,0:T(8,128)(2,1)S(1)}, u32[]{:S(2)}, u32[]{:S(2)}) collective-permute-start(bf16[36,32,128]{2,1,0:T(8,128)(2,1)} %get-tuple-element.68), channel_id=1, source_target_pairs={{0,28},{4,0},{8,4},{12,8},{16,12},{20,16},{24,20},{28,24},{1,29},{... | collective-permute-start | bytes 884744 | tf_op jit(solution)/shard_map/ppermute | solution.py:395
  54.8 0.7 copy-start
  55.6 0.7 copy-start.1
  66.3 0.7 copy-start.5
  66.3 0.8 copy-start.6
  67.1 0.8 copy-start.7
  71.6 12.1 %collective-permute-start.9 = (bf16[34,32,128]{2,1,0:T(8,128)(2,1)}, bf16[34,32,128]{2,1,0:T(8,128)(2,1)S(1)}, u32[]{:S(2)}, u32[]{:S(2)}) collective-permute-start(bf16[34,32,128]{2,1,0:T(8,128)(2,1)} %get-tuple-element.71), channel_id=1, source_target_pairs={{0,4},{4,8},{8,12},{12,16},{16,20},{20,24},{24,28},{28,0},{1,5},{5... | collective-permute-start | bytes 835592 | tf_op jit(solution)/shard_map/ppermute | solution.py:431
  71.6 12.1 %collective-permute-start.10 = (bf16[34,32,128]{2,1,0:T(8,128)(2,1)}, bf16[34,32,128]{2,1,0:T(8,128)(2,1)S(1)}, u32[]{:S(2)}, u32[]{:S(2)}) collective-permute-start(bf16[34,32,128]{2,1,0:T(8,128)(2,1)} %get-tuple-element.72), channel_id=1, source_target_pairs={{0,28},{4,0},{8,4},{12,8},{16,12},{20,16},{24,20},{28,24},{1,29},{... | collective-permute-start | bytes 835592 | tf_op jit(solution)/shard_map/ppermute | solution.py:432
  83.7 0.7 copy-start.9
  83.7 0.8 copy-start.10
  83.7 9.4 %collective-permute-start.11 = (f32[4,4,112,128]{3,2,1,0:T(8,128)}, f32[4,4,112,128]{3,2,1,0:T(8,128)S(1)}, u32[]{:S(2)}, u32[]{:S(2)}) collective-permute-start(f32[4,4,112,128]{3,2,1,0:T(8,128)} %get-tuple-element.78), channel_id=1, source_target_pairs={{0,4},{4,0},{8,12},{12,8},{16,20},{20,16},{24,28},{28,24},{1,5},{5... | collective-permute-start | bytes 2752520 | tf_op jit(solution)/shard_map/ppermute | solution.py:449
  84.5 8.6 %copy-start.4 = (f32[4,4,112,128]{3,2,1,0:T(8,128)S(1)}, f32[4,4,112,128]{3,2,1,0:T(8,128)}, u32[]{:S(2)}) copy-start(f32[4,4,112,128]{3,2,1,0:T(8,128)} %get-tuple-element.77) | copy-start | bytes 2752516
  90.1 12.7 %collective-permute-start.18 = (bf16[16,32,128]{2,1,0:T(8,128)(2,1)}, bf16[16,32,128]{2,1,0:T(8,128)(2,1)S(1)}, u32[]{:S(2)}, u32[]{:S(2)}) collective-permute-start(bf16[16,32,128]{2,1,0:T(8,128)(2,1)} %get-tuple-element.88), channel_id=1, source_target_pairs={{0,1},{1,2},{2,3},{3,0},{4,5},{5,6},{6,7},{7,4},{8,9},{9,10},{10,1... | collective-permute-start | bytes 393224 | tf_op jit(solution)/shard_map/ppermute | solution.py:461
  92.6 10.4 %collective-permute-start.19 = (bf16[16,32,128]{2,1,0:T(8,128)(2,1)}, bf16[16,32,128]{2,1,0:T(8,128)(2,1)S(1)}, u32[]{:S(2)}, u32[]{:S(2)}) collective-permute-start(bf16[16,32,128]{2,1,0:T(8,128)(2,1)} %get-tuple-element.89), channel_id=1, source_target_pairs={{0,2},{1,3},{2,0},{3,1},{4,6},{5,7},{6,4},{7,5},{8,10},{9,11},{10,... | collective-permute-start | bytes 393224 | tf_op jit(solution)/shard_map/ppermute | solution.py:461
  93.3 9.7 %collective-permute-start.15 = (bf16[4,112,128]{2,1,0:T(8,128)(2,1)S(1)}, bf16[4,112,128]{2,1,0:T(8,128)(2,1)S(1)}, u32[]{:S(2)}, u32[]{:S(2)}) collective-permute-start(bf16[4,112,128]{2,1,0:T(8,128)(2,1)S(1)} %get-tuple-element.116), channel_id=1, source_target_pairs={{0,8},{4,12},{8,0},{12,4},{16,24},{20,28},{24,16},{28,20},{1,9},{5... | collective-permute-start | bytes 344072 | tf_op jit(solution)/shard_map/ppermute | solution.py:471
  94.0 9.0 %collective-permute-start.16 = (bf16[4,112,128]{2,1,0:T(8,128)(2,1)S(1)}, bf16[4,112,128]{2,1,0:T(8,128)(2,1)S(1)}, u32[]{:S(2)}, u32[]{:S(2)}) collective-permute-start(bf16[4,112,128]{2,1,0:T(8,128)(2,1)S(1)} %get-tuple-element.115), channel_id=1, source_target_pairs={{0,16},{4,20},{8,24},{12,28},{16,0},{20,4},{24,8},{28,12},{1,17},{... | collective-permute-start | bytes 344072 | tf_op jit(solution)/shard_map/ppermute | solution.py:471
  95.8 7.2 %collective-permute-start.17 = (bf16[4,112,128]{2,1,0:T(8,128)(2,1)S(1)}, bf16[4,112,128]{2,1,0:T(8,128)(2,1)S(1)}, u32[]{:S(2)}, u32[]{:S(2)}) collective-permute-start(bf16[4,112,128]{2,1,0:T(8,128)(2,1)S(1)} %get-tuple-element.114), channel_id=1, source_target_pairs={{0,24},{4,28},{8,16},{12,20},{16,8},{20,12},{24,0},{28,4},{1,25},{... | collective-permute-start | bytes 344072 | tf_op jit(solution)/shard_map/ppermute | solution.py:471
  103.0 24.8 %copy-start.3 = (bf16[32,32,128]{2,1,0:T(8,128)(2,1)S(1)}, bf16[32,32,128]{2,1,0:T(8,128)(2,1)}, u32[]{:S(2)}) copy-start(bf16[32,32,128]{2,1,0:T(8,128)(2,1)} %get-tuple-element.99) | copy-start | bytes 786436
  103.1 7.3 %collective-permute-start.22 = (f32[112,128]{1,0:T(8,128)S(1)}, f32[112,128]{1,0:T(8,128)S(1)}, u32[]{:S(2)}, u32[]{:S(2)}) collective-permute-start(f32[112,128]{1,0:T(8,128)S(1)} %get-tuple-element.118), channel_id=1, source_target_pairs={{0,3},{1,0},{2,1},{3,2},{4,7},{5,4},{6,5},{7,6},{8,11},{9,8},{10,9... | collective-permute-start | bytes 172040 | tf_op jit(solution)/shard_map/ppermute | solution.py:331
  105.1 12.1 %collective-permute-start.21 = (f32[112,128]{1,0:T(8,128)S(1)}, f32[112,128]{1,0:T(8,128)S(1)}, u32[]{:S(2)}, u32[]{:S(2)}) collective-permute-start(f32[112,128]{1,0:T(8,128)S(1)} %get-tuple-element.119), channel_id=1, source_target_pairs={{0,2},{1,3},{2,0},{3,1},{4,6},{5,7},{6,4},{7,5},{8,10},{9,11},{10,... | collective-permute-start | bytes 172040 | tf_op jit(solution)/shard_map/ppermute | solution.py:331
  106.0 11.2 %collective-permute-start.20 = (f32[112,128]{1,0:T(8,128)S(1)}, f32[112,128]{1,0:T(8,128)S(1)}, u32[]{:S(2)}, u32[]{:S(2)}) collective-permute-start(f32[112,128]{1,0:T(8,128)S(1)} %get-tuple-element.117), channel_id=1, source_target_pairs={{0,1},{1,2},{2,3},{3,0},{4,5},{5,6},{6,7},{7,4},{8,9},{9,10},{10,1... | collective-permute-start | bytes 172040 | tf_op jit(solution)/shard_map/ppermute | solution.py:331
  107.2 20.5 %collective-permute-start.12 = (bf16[16,32,128]{2,1,0:T(8,128)(2,1)}, bf16[16,32,128]{2,1,0:T(8,128)(2,1)S(1)}, u32[]{:S(2)}, u32[]{:S(2)}) collective-permute-start(bf16[16,32,128]{2,1,0:T(8,128)(2,1)} %get-tuple-element.85), channel_id=1, source_target_pairs={{0,1},{1,2},{2,3},{3,0},{4,5},{5,6},{6,7},{7,4},{8,9},{9,10},{10,1... | collective-permute-start | bytes 393224 | tf_op jit(solution)/shard_map/ppermute | solution.py:331
  108.6 19.0 %collective-permute-start.13 = (bf16[16,32,128]{2,1,0:T(8,128)(2,1)}, bf16[16,32,128]{2,1,0:T(8,128)(2,1)S(1)}, u32[]{:S(2)}, u32[]{:S(2)}) collective-permute-start(bf16[16,32,128]{2,1,0:T(8,128)(2,1)} %get-tuple-element.86), channel_id=1, source_target_pairs={{0,2},{1,3},{2,0},{3,1},{4,6},{5,7},{6,4},{7,5},{8,10},{9,11},{10,... | collective-permute-start | bytes 393224 | tf_op jit(solution)/shard_map/ppermute | solution.py:331
  110.4 17.3 %collective-permute-start.14 = (bf16[32,32,128]{2,1,0:T(8,128)(2,1)}, bf16[32,32,128]{2,1,0:T(8,128)(2,1)S(1)}, u32[]{:S(2)}, u32[]{:S(2)}) collective-permute-start(bf16[32,32,128]{2,1,0:T(8,128)(2,1)} %get-tuple-element.87), channel_id=1, source_target_pairs={{0,3},{1,0},{2,1},{3,2},{4,7},{5,4},{6,5},{7,6},{8,11},{9,8},{10,9... | collective-permute-start | bytes 786440 | tf_op jit(solution)/shard_map/ppermute | solution.py:331

commit v5 on v4

--- a/solution.py
+++ b/solution.py
@@ -62,7 +62,7 @@
 
 
 def block_step(rows):
-    return max(1, 1024 // rows)
+    return max(1, 2048 // rows)
 
 
 def over_columns(count, rows, visit):
@@ -482,7 +482,6 @@
         [grad, g_low, g_high, weights_b] + [first[j] for j in whole_blocks],
         z_arg,
     )
-    returned = exchange(back, "chan")
     from_chips, returned_first = after((from_chips, returned_first), back[0])
     for got in from_chips:
         chip_sum = chip_sum + got.astype(F32)
@@ -492,7 +491,7 @@
         for j in range(chan_count)
     ]
     shard_sum = sum(exchange(parts, "chan"))
-    returned = after(returned, shard_sum)
+    returned = exchange(after(back, shard_sum), "chan")
     cell_total = planes * space_count * height * width
     shard_sum = shard_sum * (1.0 / math.sqrt(cell_total))
     whole = lax.all_gather(shard_sum, "space", axis=0, tiled=True)

time: 130 us -> 128 us (0.985)
  Pallas kernels: 46.8 us -> 45.1 us
    pallas_call x9, Pallas kernels: 46.8 us -> 45.1 us  [call(): pl.pallas_call(kernel, out_shape=outs, in_specs=[pl.BlockSpec(memory_spac...]
  transfers between devices with their start and end apart: 23 -> 23, of which waited for: 4 -> 7; matrix products, arithmetic and copies ran while one was open for 5% -> 5% of each run, Pallas kernels for 33% -> 33%
where the time goes in v5:
time: 128 us; the launch traced here: 127 us
  Pallas kernels  45.1 us (35%)
  starting transfers between devices  35.9 us (28%)
  blocking collectives  22.3 us (17%)
  local copies, waits for them, and re-layouts  12.3 us (10%)
  waiting for transfers between devices  9.84 us (8%)
    pallas_call x9, Pallas kernels, call(): pl.pallas_call(kernel, out_shape=outs, in_specs=[pl.BlockSpec(memory_spac...  45.1 us
    ppermute x6, starting transfers between devices, swap(): lax.ppermute(blocks[j], 'chan', [(i, i ^ j) for i in range(count)])  12.9 us
    all_gather x1, blocking collectives, body(): shares = lax.all_gather(share, 'space', axis=0, tiled=False)  12.4 us
    all_gather x1, blocking collectives, body(): whole = lax.all_gather(shard_sum, 'space', axis=0, tiled=True)  9.94 us
    ppermute x6, starting transfers between devices, exchange(): lax.ppermute(blocks[j], axis, ring(count, j))  7.48 us
    ppermute x6, waiting for transfers between devices, exchange(): lax.ppermute(blocks[j], axis, ring(count, j))  5.27 us
    unnamed x33, local copies, waits for them, and re-layouts  3.91 us
    ppermute x3, starting transfers between devices, body(): lax.ppermute(block, 'space', [(i, i ^ 2 * k) for i in range(space_count)])  3.83 us
  transfers between devices with their start and end apart: 23, of which 7 were waited for; matrix products, arithmetic and copies ran while one was open for 5% of the time, Pallas kernels for 33%

profile of v5, /device:TPU:0, one launch (start us, length us, event | category | flops | bytes accessed | tf_op | source)
XLA Modules:
  0.0 127.4 jit_solution(16241373461593497762)
XLA Ops:
  0.7 0.9 pad_dynamic-slice_fusion.8
  1.6 3.1 %collective-permute-start = (bf16[432,128]{1,0:T(8,128)(2,1)S(1)}, bf16[432,128]{1,0:T(8,128)(2,1)S(1)}, u32[]{:S(2)}, u32[]{:S(2)}) collective-permute-start(bf16[432,128]{1,0:T(8,128)(2,1)S(1)} %pad_dynamic-slice_fusion.8), channel_id=1, source_target_pairs={{0,1},{1,2},{2,3},{3,0},{4,6},{5,7},{6,4},{7,5},{8,11},{9,8},{10,9... | collective-permute-start | bytes 331784 | tf_op jit(solution)/shard_map/ppermute | solution.py:350
  4.7 1.9 %copy.9 = bf16[32,128,128]{1,0,2:T(8,128)(2,1)S(1)} copy(bf16[32,128,128]{2,1,0:T(8,128)(2,1)} %bitcast.42) | data formatting | bytes 2097152 | tf_op jit(solution)/shard_map/reshape | solution.py:308
  6.6 1.0 pad_dynamic-slice_fusion.4
  7.6 0.6 pad_add_fusion.z_ref._
  8.3 1.6 %collective-permute-done = bf16[432,128]{1,0:T(8,128)(2,1)S(1)} collective-permute-done((bf16[432,128]{1,0:T(8,128)(2,1)S(1)}, bf16[432,128]{1,0:T(8,128)(2,1)S(1)}, u32[]{:S(2)}, u32[]{:S(2)}) %collective-permute-start) | collective-permute-done | bytes 110624 | tf_op jit(solution)/shard_map/ppermute | solution.py:350
  9.9 0.8 collective-permute-start.1
  10.7 1.9 %collective-permute-start.2 = (bf16[36,32,128]{2,1,0:T(8,128)(2,1)S(1)}, bf16[36,32,128]{2,1,0:T(8,128)(2,1)}, u32[]{:S(2)}, u32[]{:S(2)}) collective-permute-start(bf16[36,32,128]{2,1,0:T(8,128)(2,1)S(1)} %get-tuple-element.54), channel_id=1, source_target_pairs={{0,2},{1,3},{2,0},{3,1},{4,6},{5,7},{6,4},{7,5},{8,10},{9,11},{10,... | collective-permute-start | bytes 884744 | tf_op jit(solution)/shard_map/ppermute | solution.py:322
  12.6 1.7 %collective-permute-start.3 = (bf16[36,32,128]{2,1,0:T(8,128)(2,1)S(1)}, bf16[36,32,128]{2,1,0:T(8,128)(2,1)}, u32[]{:S(2)}, u32[]{:S(2)}) collective-permute-start(bf16[36,32,128]{2,1,0:T(8,128)(2,1)S(1)} %get-tuple-element.55), channel_id=1, source_target_pairs={{0,3},{1,2},{2,1},{3,0},{4,7},{5,6},{6,5},{7,4},{8,11},{9,10},{10,... | collective-permute-start | bytes 884744 | tf_op jit(solution)/shard_map/ppermute | solution.py:322
  14.3 12.4 %all-gather = bf16[3456,128]{1,0:T(8,128)(2,1)} all-gather(bf16[432,128]{1,0:T(8,128)(2,1)S(1)} %collective-permute-done), channel_id=2, replica_groups=mesh['space'=8,'chan'=4] {'space'}, dimensions={0}, use_global_device_ids=true | all-gather | bytes 995328 | tf_op jit(solution)/shard_map/all_gather | solution.py:370
  26.7 1.0 copy.8
  27.7 2.9 %shard_map.50 = (bf16[1152,384]{1,0:T(8,128)(2,1)}, bf16[1152,384]{1,0:T(8,128)(2,1)}) custom-call(s32[3]{0:T(128)} %pad_add_fusion.z_ref._, bf16[27,32,128]{2,1,0:T(8,128)(2,1)} %own_ref.1, bf16[8,432,128]{2,1,0:T(8,128)(2,1)} %bitcast.41), custom_call_target="tpu_custom_call" | custom-call | tf_op jit(solution)/shard_map/pallas_call | solution.py:292
  30.6 1.0 pad_dynamic-slice_fusion
  31.5 2.7 %collective-permute-done.2.refs_2_ = bf16[36,32,128]{2,1,0:T(8,128)(2,1)} collective-permute-done((bf16[36,32,128]{2,1,0:T(8,128)(2,1)S(1)}, bf16[36,32,128]{2,1,0:T(8,128)(2,1)}, u32[]{:S(2)}, u32[]{:S(2)}) %collective-permute-start.2) | collective-permute-done | bytes 294944 | tf_op jit(solution)/shard_map/ppermute | solution.py:322
  34.2 6.1 %collective-permute-start.4 = (bf16[37,32,128]{2,1,0:T(8,128)(2,1)S(1)}, bf16[37,32,128]{2,1,0:T(8,128)(2,1)S(1)}, u32[]{:S(2)}, u32[]{:S(2)}) collective-permute-start(bf16[37,32,128]{2,1,0:T(8,128)(2,1)S(1)} %get-tuple-element.58), channel_id=1, source_target_pairs={{0,1},{1,0},{2,3},{3,2},{4,5},{5,4},{6,7},{7,6},{8,9},{9,8},{10,11... | collective-permute-start | bytes 909320 | tf_op jit(solution)/shard_map/ppermute | solution.py:322
  40.4 0.9 collective-permute-start.5
  41.3 1.5 %collective-permute-start.6 = (bf16[37,32,128]{2,1,0:T(8,128)(2,1)S(1)}, bf16[37,32,128]{2,1,0:T(8,128)(2,1)S(1)}, u32[]{:S(2)}, u32[]{:S(2)}) collective-permute-start(bf16[37,32,128]{2,1,0:T(8,128)(2,1)S(1)} %get-tuple-element.62), channel_id=1, source_target_pairs={{0,3},{1,2},{2,1},{3,0},{4,7},{5,6},{6,5},{7,4},{8,11},{9,10},{10,... | collective-permute-start | bytes 909320 | tf_op jit(solution)/shard_map/ppermute | solution.py:322
  42.7 3.3 %shard_map.51 = (bf16[36,128,128]{2,1,0:T(8,128)(2,1)}, bf16[36,128,128]{2,1,0:T(8,128)(2,1)}, bf16[36,32,128]{2,1,0:T(8,128)(2,1)}, bf16[36,32,128]{2,1,0:T(8,128)(2,1)}) custom-call(s32[3]{0:T(128)} %pad_add_fusion.z_ref._, bf16[36,32,128]{2,1,0:T(8,128)(2,1)} %get-tuple-element.63.refs_0_, bf16[36,32,128]{2,1,0:T(8,128)(2,1)} %copy-done.8, ...), custom_call_target="tpu_custom_call" | custom-call | tf_op jit(solution)/shard_map/pallas_call | solution.py:292
  46.0 2.6 %collective-permute-start.8 = (bf16[36,32,128]{2,1,0:T(8,128)(2,1)}, bf16[36,32,128]{2,1,0:T(8,128)(2,1)S(1)}, u32[]{:S(2)}, u32[]{:S(2)}) collective-permute-start(bf16[36,32,128]{2,1,0:T(8,128)(2,1)} %get-tuple-element.68), channel_id=1, source_target_pairs={{0,28},{4,0},{8,4},{12,8},{16,12},{20,16},{24,20},{28,24},{1,29},{... | collective-permute-start | bytes 884744 | tf_op jit(solution)/shard_map/ppermute | solution.py:395
  48.7 5.7 %shard_map.52.refs_4_ = f32[34,64,128]{2,1,0:T(8,128)} custom-call(s32[3]{0:T(128)} %pad_add_fusion.z_ref._, bf16[36,128,128]{2,1,0:T(8,128)(2,1)} %get-tuple-element.66.x_ref, bf16[1152,384]{1,0:T(8,128)(2,1)} %get-tuple-element.65.weights_ref), custom_call_target="tpu_custom_call" | custom-call | tf_op jit(solution)/shard_map/pallas_call | solution.py:292
  54.5 0.7 copy-done
  55.3 0.7 copy-done.1
  56.0 3.5 %shard_map.54.sides_ref = bf16[2,34,128,128]{3,2,1,0:T(8,128)(2,1)} custom-call(s32[3]{0:T(128)} %pad_add_fusion.z_ref._, bf16[36,128,128]{2,1,0:T(8,128)(2,1)} %get-tuple-element.66.x_ref, bf16[36,32,128]{2,1,0:T(8,128)(2,1)} %copy-done, bf16[36,32,128]{2,1,0:T(8,128)(2,1)} %copy-done.1), custom_call_target="tpu_custom_call" | custom-call | tf_op jit(solution)/shard_map/pallas_call | solution.py:292
  59.5 6.0 %shard_map.53.refs_5_ = f32[34,64,128]{2,1,0:T(8,128)} custom-call(s32[3]{0:T(128)} %pad_add_fusion.z_ref._, bf16[36,128,128]{2,1,0:T(8,128)(2,1)} %get-tuple-element.66.x_ref, bf16[36,32,128]{2,1,0:T(8,128)(2,1)} %copy-done, bf16[36,32,128]{2,1,0:T(8,128)(2,1)} %copy-done.1, bf16[1152,384]{1,0:T(8,128)(2,1)} %get-tuple-element.65.weights_ref), custom_call_target="tpu_custom_call" | custom-call | tf_op jit(solution)/shard_map/pallas_call | solution.py:292
  65.5 0.7 copy-done.5
  66.3 0.8 copy-done.7
  67.1 3.7 %shard_map.55 = (bf16[34,128,128]{2,1,0:T(8,128)(2,1)}, bf16[34,32,128]{2,1,0:T(8,128)(2,1)}, bf16[34,32,128]{2,1,0:T(8,128)(2,1)}) custom-call(s32[3]{0:T(128)} %pad_add_fusion.z_ref._, bf16[37,32,128]{2,1,0:T(8,128)(2,1)} %get-tuple-element.109.refs_0_, bf16[37,32,128]{2,1,0:T(8,128)(2,1)} %copy-done.5, bf16[37,32,128]{2,1,0:T(8,128)(2,1)} %copy-done.6, ...), custom_call_target="tpu_custom_call" | custom-call | flops 5242880 | bytes 5111808 | tf_op jit(solution)/shard_map/pallas_call | solution.py:292
  70.7 2.6 %collective-permute-start.10 = (bf16[34,32,128]{2,1,0:T(8,128)(2,1)}, bf16[34,32,128]{2,1,0:T(8,128)(2,1)S(1)}, u32[]{:S(2)}, u32[]{:S(2)}) collective-permute-start(bf16[34,32,128]{2,1,0:T(8,128)(2,1)} %get-tuple-element.72), channel_id=1, source_target_pairs={{0,28},{4,0},{8,4},{12,8},{16,12},{20,16},{24,20},{28,24},{1,29},{... | collective-permute-start | bytes 835592 | tf_op jit(solution)/shard_map/ppermute | solution.py:432
  73.4 9.1 %shard_map.56 = (f32[4,4,112,128]{3,2,1,0:T(8,128)}, f32[4,4,112,128]{3,2,1,0:T(8,128)}) custom-call(s32[1]{0:T(128)} %bitcast.9.core_ref, bf16[36,128,128]{2,1,0:T(8,128)(2,1)} %get-tuple-element.73.x_ref, bf16[2,34,128,128]{3,2,1,0:T(8,128)(2,1)} %shard_map.54.sides_ref, bf16[34,128,128]{2,1,0:T(8,128)(2,1)} %get-tuple-element.70.grad_ref), custom_call_target="tpu_custom_call" | custom-call | tf_op jit(solution)/shard_map/pallas_call | solution.py:292
  82.6 0.6 copy-done.9
  83.3 5.5 %shard_map.57 = (bf16[16,32,128]{2,1,0:T(8,128)(2,1)}, bf16[16,32,128]{2,1,0:T(8,128)(2,1)}, bf16[16,32,128]{2,1,0:T(8,128)(2,1)}, bf16[16,32,128]{2,1,0:T(8,128)(2,1)}) custom-call(s32[3]{0:T(128)} %pad_add_fusion.z_ref._, bf16[34,128,128]{2,1,0:T(8,128)(2,1)} %get-tuple-element.70.grad_ref, bf16[34,32,128]{2,1,0:T(8,128)(2,1)} %copy-done.9, ...), custom_call_target="tpu_custom_call" | custom-call | flops 5435817984 | bytes 3080192 | tf_op jit(solution)/shard_map/pallas_call | solution.py:292
  88.8 3.2 %collective-permute-start.15 = (bf16[16,32,128]{2,1,0:T(8,128)(2,1)}, bf16[16,32,128]{2,1,0:T(8,128)(2,1)S(1)}, u32[]{:S(2)}, u32[]{:S(2)}) collective-permute-start(bf16[16,32,128]{2,1,0:T(8,128)(2,1)} %get-tuple-element.88), channel_id=1, source_target_pairs={{0,1},{1,2},{2,3},{3,0},{4,5},{5,6},{6,7},{7,4},{8,9},{9,10},{10,1... | collective-permute-start | bytes 393224 | tf_op jit(solution)/shard_map/ppermute | solution.py:461
  92.2 0.6 collective-permute-start.12
  92.8 1.8 %collective-permute-start.13 = (bf16[4,112,128]{2,1,0:T(8,128)(2,1)S(1)}, bf16[4,112,128]{2,1,0:T(8,128)(2,1)S(1)}, u32[]{:S(2)}, u32[]{:S(2)}) collective-permute-start(bf16[4,112,128]{2,1,0:T(8,128)(2,1)S(1)} %get-tuple-element.115), channel_id=1, source_target_pairs={{0,16},{4,20},{8,24},{12,28},{16,0},{20,4},{24,8},{28,12},{1,17},{... | collective-permute-start | bytes 344072 | tf_op jit(solution)/shard_map/ppermute | solution.py:471
  94.6 1.4 %collective-permute-start.14 = (bf16[4,112,128]{2,1,0:T(8,128)(2,1)S(1)}, bf16[4,112,128]{2,1,0:T(8,128)(2,1)S(1)}, u32[]{:S(2)}, u32[]{:S(2)}) collective-permute-start(bf16[4,112,128]{2,1,0:T(8,128)(2,1)S(1)} %get-tuple-element.114), channel_id=1, source_target_pairs={{0,24},{4,28},{8,16},{12,20},{16,8},{20,12},{24,0},{28,4},{1,25},{... | collective-permute-start | bytes 344072 | tf_op jit(solution)/shard_map/ppermute | solution.py:471
  96.0 5.5 %shard_map.58 = (bf16[32,32,128]{2,1,0:T(8,128)(2,1)}, bf16[16,32,128]{2,1,0:T(8,128)(2,1)}, bf16[16,32,128]{2,1,0:T(8,128)(2,1)}, bf16[32,32,128]{2,1,0:T(8,128)(2,1)}) custom-call(s32[3]{0:T(128)} %pad_add_fusion.z_ref._, bf16[34,128,128]{2,1,0:T(8,128)(2,1)} %get-tuple-element.70.grad_ref, bf16[34,32,128]{2,1,0:T(8,128)(2,1)} %copy-done.9, ...), custom_call_target="tpu_custom_call" | custom-call | flops 5435817984 | bytes 3604480 | tf_op jit(solution)/shard_map/pallas_call | solution.py:292
  101.7 2.5 %collective-permute-start.19 = (f32[112,128]{1,0:T(8,128)S(1)}, f32[112,128]{1,0:T(8,128)S(1)}, u32[]{:S(2)}, u32[]{:S(2)}) collective-permute-start(f32[112,128]{1,0:T(8,128)S(1)} %get-tuple-element.118), channel_id=1, source_target_pairs={{0,3},{1,0},{2,1},{3,2},{4,7},{5,4},{6,5},{7,6},{8,11},{9,8},{10,9... | collective-permute-start | bytes 172040 | tf_op jit(solution)/shard_map/ppermute | solution.py:331
  104.2 0.4 collective-permute-start.18
  104.6 1.8 %collective-permute-start.17 = (f32[112,128]{1,0:T(8,128)S(1)}, f32[112,128]{1,0:T(8,128)S(1)}, u32[]{:S(2)}, u32[]{:S(2)}) collective-permute-start(f32[112,128]{1,0:T(8,128)S(1)} %get-tuple-element.117), channel_id=1, source_target_pairs={{0,1},{1,2},{2,3},{3,0},{4,5},{5,6},{6,7},{7,4},{8,9},{9,10},{10,1... | collective-permute-start | bytes 172040 | tf_op jit(solution)/shard_map/ppermute | solution.py:331
  106.4 3.4 %collective-permute-done.18 = f32[112,128]{1,0:T(8,128)S(1)} collective-permute-done((f32[112,128]{1,0:T(8,128)S(1)}, f32[112,128]{1,0:T(8,128)S(1)}, u32[]{:S(2)}, u32[]{:S(2)}) %collective-permute-start.18) | collective-permute-done | bytes 57376 | tf_op jit(solution)/shard_map/ppermute | solution.py:331
  109.8 0.8 collective-permute-done.17
  110.6 1.0 collective-permute-start.20
  111.7 0.4 collective-permute-start.21
  112.1 1.3 %collective-permute-start.22 = (bf16[16,32,128]{2,1,0:T(8,128)(2,1)}, bf16[16,32,128]{2,1,0:T(8,128)(2,1)S(1)}, u32[]{:S(2)}, u32[]{:S(2)}) collective-permute-start(bf16[16,32,128]{2,1,0:T(8,128)(2,1)} %get-tuple-element.98), channel_id=1, source_target_pairs={{0,1},{1,2},{2,3},{3,0},{4,5},{5,6},{6,7},{7,4},{8,9},{9,10},{10,1... | collective-permute-start | bytes 393224 | tf_op jit(solution)/shard_map/ppermute | solution.py:331
  113.4 9.9 %all_gather.11 = f32[896,128]{1,0:T(8,128)S(1)} all-gather(f32[112,128]{1,0:T(8,128)S(1)} %broadcast_multiply_fusion), channel_id=1, replica_groups=mesh['space'=8,'chan'=4] {'space'}, dimensions={0}, use_global_device_ids=true | all-gather | bytes 516096 | tf_op jit(solution)/shard_map/all_gather | solution.py:497
  123.4 0.8 slice.4
  124.2 1.0 collective-permute-done.21
  125.7 1.7 %copy.10 = bf16[32,128,128]{2,1,0:T(8,128)(2,1)} copy(bf16[32,128,128]{1,0,2:T(8,128)(2,1)S(1)} %dynamic-slice_bitcast_fusion) | data formatting | bytes 2097152 | tf_op jit(solution)/shard_map/transpose | solution.py:508
  (57 shorter events, 1.2 us)
Async XLA Ops:
  1.6 8.3 %collective-permute-start = (bf16[432,128]{1,0:T(8,128)(2,1)S(1)}, bf16[432,128]{1,0:T(8,128)(2,1)S(1)}, u32[]{:S(2)}, u32[]{:S(2)}) collective-permute-start(bf16[432,128]{1,0:T(8,128)(2,1)S(1)} %pad_dynamic-slice_fusion.8), channel_id=1, source_target_pairs={{0,1},{1,2},{2,3},{3,0},{4,6},{5,7},{6,4},{7,5},{8,11},{9,8},{10,9... | collective-permute-start | bytes 331784 | tf_op jit(solution)/shard_map/ppermute | solution.py:350
  6.6 20.1 %copy-start.2 = (bf16[32,4,32,128]{3,2,1,0:T(8,128)(2,1)S(1)}, bf16[32,4,32,128]{3,2,1,0:T(8,128)(2,1)}, u32[]{:S(2)}) copy-start(bf16[32,4,32,128]{3,2,1,0:T(8,128)(2,1)} %param.5) | copy-start | bytes 3145732
  9.9 21.6 %collective-permute-start.1 = (bf16[36,32,128]{2,1,0:T(8,128)(2,1)S(1)}, bf16[36,32,128]{2,1,0:T(8,128)(2,1)S(1)}, u32[]{:S(2)}, u32[]{:S(2)}) collective-permute-start(bf16[36,32,128]{2,1,0:T(8,128)(2,1)S(1)} %get-tuple-element.53), channel_id=1, source_target_pairs={{0,1},{1,0},{2,3},{3,2},{4,5},{5,4},{6,7},{7,6},{8,9},{9,8},{10,11... | collective-permute-start | bytes 884744 | tf_op jit(solution)/shard_map/ppermute | solution.py:322
  10.7 23.5 %collective-permute-start.2 = (bf16[36,32,128]{2,1,0:T(8,128)(2,1)S(1)}, bf16[36,32,128]{2,1,0:T(8,128)(2,1)}, u32[]{:S(2)}, u32[]{:S(2)}) collective-permute-start(bf16[36,32,128]{2,1,0:T(8,128)(2,1)S(1)} %get-tuple-element.54), channel_id=1, source_target_pairs={{0,2},{1,3},{2,0},{3,1},{4,6},{5,7},{6,4},{7,5},{8,10},{9,11},{10,... | collective-permute-start | bytes 884744 | tf_op jit(solution)/shard_map/ppermute | solution.py:322
  12.6 21.6 %collective-permute-start.3 = (bf16[36,32,128]{2,1,0:T(8,128)(2,1)S(1)}, bf16[36,32,128]{2,1,0:T(8,128)(2,1)}, u32[]{:S(2)}, u32[]{:S(2)}) collective-permute-start(bf16[36,32,128]{2,1,0:T(8,128)(2,1)S(1)} %get-tuple-element.55), channel_id=1, source_target_pairs={{0,3},{1,2},{2,1},{3,0},{4,7},{5,6},{6,5},{7,4},{8,11},{9,10},{10,... | collective-permute-start | bytes 884744 | tf_op jit(solution)/shard_map/ppermute | solution.py:322
  31.5 11.2 %copy-start.8 = (bf16[36,32,128]{2,1,0:T(8,128)(2,1)}, bf16[36,32,128]{2,1,0:T(8,128)(2,1)S(1)}, u32[]{:S(2)}) copy-start(bf16[36,32,128]{2,1,0:T(8,128)(2,1)S(1)} %collective-permute-done.1.refs_1_) | copy-start | bytes 884740
  34.2 31.3 %collective-permute-start.4 = (bf16[37,32,128]{2,1,0:T(8,128)(2,1)S(1)}, bf16[37,32,128]{2,1,0:T(8,128)(2,1)S(1)}, u32[]{:S(2)}, u32[]{:S(2)}) collective-permute-start(bf16[37,32,128]{2,1,0:T(8,128)(2,1)S(1)} %get-tuple-element.58), channel_id=1, source_target_pairs={{0,1},{1,0},{2,3},{3,2},{4,5},{5,4},{6,7},{7,6},{8,9},{9,8},{10,11... | collective-permute-start | bytes 909320 | tf_op jit(solution)/shard_map/ppermute | solution.py:322
  40.4 25.1 %collective-permute-start.5 = (bf16[37,32,128]{2,1,0:T(8,128)(2,1)S(1)}, bf16[37,32,128]{2,1,0:T(8,128)(2,1)S(1)}, u32[]{:S(2)}, u32[]{:S(2)}) collective-permute-start(bf16[37,32,128]{2,1,0:T(8,128)(2,1)S(1)} %get-tuple-element.60), channel_id=1, source_target_pairs={{0,2},{1,3},{2,0},{3,1},{4,6},{5,7},{6,4},{7,5},{8,10},{9,11},{10,... | collective-permute-start | bytes 909320 | tf_op jit(solution)/shard_map/ppermute | solution.py:322
  41.3 24.2 %collective-permute-start.6 = (bf16[37,32,128]{2,1,0:T(8,128)(2,1)S(1)}, bf16[37,32,128]{2,1,0:T(8,128)(2,1)S(1)}, u32[]{:S(2)}, u32[]{:S(2)}) collective-permute-start(bf16[37,32,128]{2,1,0:T(8,128)(2,1)S(1)} %get-tuple-element.62), channel_id=1, source_target_pairs={{0,3},{1,2},{2,1},{3,0},{4,7},{5,6},{6,5},{7,4},{8,11},{9,10},{10,... | collective-permute-start | bytes 909320 | tf_op jit(solution)/shard_map/ppermute | solution.py:322
  46.0 8.5 %collective-permute-start.7 = (bf16[36,32,128]{2,1,0:T(8,128)(2,1)}, bf16[36,32,128]{2,1,0:T(8,128)(2,1)S(1)}, u32[]{:S(2)}, u32[]{:S(2)}) collective-permute-start(bf16[36,32,128]{2,1,0:T(8,128)(2,1)} %get-tuple-element.67), channel_id=1, source_target_pairs={{0,4},{4,8},{8,12},{12,16},{16,20},{20,24},{24,28},{28,0},{1,5},{5... | collective-permute-start | bytes 884744 | tf_op jit(solution)/shard_map/ppermute | solution.py:394
  46.0 8.5 %collective-permute-start.8 = (bf16[36,32,128]{2,1,0:T(8,128)(2,1)}, bf16[36,32,128]{2,1,0:T(8,128)(2,1)S(1)}, u32[]{:S(2)}, u32[]{:S(2)}) collective-permute-start(bf16[36,32,128]{2,1,0:T(8,128)(2,1)} %get-tuple-element.68), channel_id=1, source_target_pairs={{0,28},{4,0},{8,4},{12,8},{16,12},{20,16},{24,20},{28,24},{1,29},{... | collective-permute-start | bytes 884744 | tf_op jit(solution)/shard_map/ppermute | solution.py:395
  54.5 0.7 copy-start
  55.3 0.7 copy-start.1
  65.5 0.7 copy-start.5
  65.5 0.8 copy-start.6
  66.3 0.8 copy-start.7
  70.7 11.7 %collective-permute-start.9 = (bf16[34,32,128]{2,1,0:T(8,128)(2,1)}, bf16[34,32,128]{2,1,0:T(8,128)(2,1)S(1)}, u32[]{:S(2)}, u32[]{:S(2)}) collective-permute-start(bf16[34,32,128]{2,1,0:T(8,128)(2,1)} %get-tuple-element.71), channel_id=1, source_target_pairs={{0,4},{4,8},{8,12},{12,16},{16,20},{20,24},{24,28},{28,0},{1,5},{5... | collective-permute-start | bytes 835592 | tf_op jit(solution)/shard_map/ppermute | solution.py:431
  70.7 11.8 %collective-permute-start.10 = (bf16[34,32,128]{2,1,0:T(8,128)(2,1)}, bf16[34,32,128]{2,1,0:T(8,128)(2,1)S(1)}, u32[]{:S(2)}, u32[]{:S(2)}) collective-permute-start(bf16[34,32,128]{2,1,0:T(8,128)(2,1)} %get-tuple-element.72), channel_id=1, source_target_pairs={{0,28},{4,0},{8,4},{12,8},{16,12},{20,16},{24,20},{28,24},{1,29},{... | collective-permute-start | bytes 835592 | tf_op jit(solution)/shard_map/ppermute | solution.py:432
  82.5 0.7 copy-start.9
  82.5 0.8 copy-start.10
  82.5 9.5 %collective-permute-start.11 = (f32[4,4,112,128]{3,2,1,0:T(8,128)}, f32[4,4,112,128]{3,2,1,0:T(8,128)S(1)}, u32[]{:S(2)}, u32[]{:S(2)}) collective-permute-start(f32[4,4,112,128]{3,2,1,0:T(8,128)} %get-tuple-element.78), channel_id=1, source_target_pairs={{0,4},{4,0},{8,12},{12,8},{16,20},{20,16},{24,28},{28,24},{1,5},{5... | collective-permute-start | bytes 2752520 | tf_op jit(solution)/shard_map/ppermute | solution.py:449
  83.3 8.7 %copy-start.4 = (f32[4,4,112,128]{3,2,1,0:T(8,128)S(1)}, f32[4,4,112,128]{3,2,1,0:T(8,128)}, u32[]{:S(2)}) copy-start(f32[4,4,112,128]{3,2,1,0:T(8,128)} %get-tuple-element.77) | copy-start | bytes 2752516
  88.8 12.8 %collective-permute-start.15 = (bf16[16,32,128]{2,1,0:T(8,128)(2,1)}, bf16[16,32,128]{2,1,0:T(8,128)(2,1)S(1)}, u32[]{:S(2)}, u32[]{:S(2)}) collective-permute-start(bf16[16,32,128]{2,1,0:T(8,128)(2,1)} %get-tuple-element.88), channel_id=1, source_target_pairs={{0,1},{1,2},{2,3},{3,0},{4,5},{5,6},{6,7},{7,4},{8,9},{9,10},{10,1... | collective-permute-start | bytes 393224 | tf_op jit(solution)/shard_map/ppermute | solution.py:461
  92.0 9.6 %collective-permute-start.16 = (bf16[16,32,128]{2,1,0:T(8,128)(2,1)}, bf16[16,32,128]{2,1,0:T(8,128)(2,1)S(1)}, u32[]{:S(2)}, u32[]{:S(2)}) collective-permute-start(bf16[16,32,128]{2,1,0:T(8,128)(2,1)} %get-tuple-element.89), channel_id=1, source_target_pairs={{0,2},{1,3},{2,0},{3,1},{4,6},{5,7},{6,4},{7,5},{8,10},{9,11},{10,... | collective-permute-start | bytes 393224 | tf_op jit(solution)/shard_map/ppermute | solution.py:461
  92.2 9.4 %collective-permute-start.12 = (bf16[4,112,128]{2,1,0:T(8,128)(2,1)S(1)}, bf16[4,112,128]{2,1,0:T(8,128)(2,1)S(1)}, u32[]{:S(2)}, u32[]{:S(2)}) collective-permute-start(bf16[4,112,128]{2,1,0:T(8,128)(2,1)S(1)} %get-tuple-element.116), channel_id=1, source_target_pairs={{0,8},{4,12},{8,0},{12,4},{16,24},{20,28},{24,16},{28,20},{1,9},{5... | collective-permute-start | bytes 344072 | tf_op jit(solution)/shard_map/ppermute | solution.py:471
  92.8 8.8 %collective-permute-start.13 = (bf16[4,112,128]{2,1,0:T(8,128)(2,1)S(1)}, bf16[4,112,128]{2,1,0:T(8,128)(2,1)S(1)}, u32[]{:S(2)}, u32[]{:S(2)}) collective-permute-start(bf16[4,112,128]{2,1,0:T(8,128)(2,1)S(1)} %get-tuple-element.115), channel_id=1, source_target_pairs={{0,16},{4,20},{8,24},{12,28},{16,0},{20,4},{24,8},{28,12},{1,17},{... | collective-permute-start | bytes 344072 | tf_op jit(solution)/shard_map/ppermute | solution.py:471
  94.6 7.0 %collective-permute-start.14 = (bf16[4,112,128]{2,1,0:T(8,128)(2,1)S(1)}, bf16[4,112,128]{2,1,0:T(8,128)(2,1)S(1)}, u32[]{:S(2)}, u32[]{:S(2)}) collective-permute-start(bf16[4,112,128]{2,1,0:T(8,128)(2,1)S(1)} %get-tuple-element.114), channel_id=1, source_target_pairs={{0,24},{4,28},{8,16},{12,20},{16,8},{20,12},{24,0},{28,4},{1,25},{... | collective-permute-start | bytes 344072 | tf_op jit(solution)/shard_map/ppermute | solution.py:471
  101.6 23.8 %copy-start.3 = (bf16[32,32,128]{2,1,0:T(8,128)(2,1)S(1)}, bf16[32,32,128]{2,1,0:T(8,128)(2,1)}, u32[]{:S(2)}) copy-start(bf16[32,32,128]{2,1,0:T(8,128)(2,1)} %get-tuple-element.99) | copy-start | bytes 786436
  101.7 4.7 %collective-permute-start.19 = (f32[112,128]{1,0:T(8,128)S(1)}, f32[112,128]{1,0:T(8,128)S(1)}, u32[]{:S(2)}, u32[]{:S(2)}) collective-permute-start(f32[112,128]{1,0:T(8,128)S(1)} %get-tuple-element.118), channel_id=1, source_target_pairs={{0,3},{1,0},{2,1},{3,2},{4,7},{5,4},{6,5},{7,6},{8,11},{9,8},{10,9... | collective-permute-start | bytes 172040 | tf_op jit(solution)/shard_map/ppermute | solution.py:331
  104.2 5.6 %collective-permute-start.18 = (f32[112,128]{1,0:T(8,128)S(1)}, f32[112,128]{1,0:T(8,128)S(1)}, u32[]{:S(2)}, u32[]{:S(2)}) collective-permute-start(f32[112,128]{1,0:T(8,128)S(1)} %get-tuple-element.119), channel_id=1, source_target_pairs={{0,2},{1,3},{2,0},{3,1},{4,6},{5,7},{6,4},{7,5},{8,10},{9,11},{10,... | collective-permute-start | bytes 172040 | tf_op jit(solution)/shard_map/ppermute | solution.py:331
  104.6 6.0 %collective-permute-start.17 = (f32[112,128]{1,0:T(8,128)S(1)}, f32[112,128]{1,0:T(8,128)S(1)}, u32[]{:S(2)}, u32[]{:S(2)}) collective-permute-start(f32[112,128]{1,0:T(8,128)S(1)} %get-tuple-element.117), channel_id=1, source_target_pairs={{0,1},{1,2},{2,3},{3,0},{4,5},{5,6},{6,7},{7,4},{8,9},{9,10},{10,1... | collective-permute-start | bytes 172040 | tf_op jit(solution)/shard_map/ppermute | solution.py:331
  110.6 13.5 %collective-permute-start.20 = (bf16[32,32,128]{2,1,0:T(8,128)(2,1)}, bf16[32,32,128]{2,1,0:T(8,128)(2,1)S(1)}, u32[]{:S(2)}, u32[]{:S(2)}) collective-permute-start(bf16[32,32,128]{2,1,0:T(8,128)(2,1)} %get-tuple-element.96), channel_id=1, source_target_pairs={{0,3},{1,0},{2,1},{3,2},{4,7},{5,4},{6,5},{7,6},{8,11},{9,8},{10,9... | collective-permute-start | bytes 786440 | tf_op jit(solution)/shard_map/ppermute | solution.py:331
  111.7 13.6 %collective-permute-start.21 = (bf16[16,32,128]{2,1,0:T(8,128)(2,1)}, bf16[16,32,128]{2,1,0:T(8,128)(2,1)S(1)}, u32[]{:S(2)}, u32[]{:S(2)}) collective-permute-start(bf16[16,32,128]{2,1,0:T(8,128)(2,1)} %get-tuple-element.97), channel_id=1, source_target_pairs={{0,2},{1,3},{2,0},{3,1},{4,6},{5,7},{6,4},{7,5},{8,10},{9,11},{10,... | collective-permute-start | bytes 393224 | tf_op jit(solution)/shard_map/ppermute | solution.py:331
  112.1 13.2 %collective-permute-start.22 = (bf16[16,32,128]{2,1,0:T(8,128)(2,1)}, bf16[16,32,128]{2,1,0:T(8,128)(2,1)S(1)}, u32[]{:S(2)}, u32[]{:S(2)}) collective-permute-start(bf16[16,32,128]{2,1,0:T(8,128)(2,1)} %get-tuple-element.98), channel_id=1, source_target_pairs={{0,1},{1,2},{2,3},{3,0},{4,5},{5,6},{6,7},{7,4},{8,9},{9,10},{10,1... | collective-permute-start | bytes 393224 | tf_op jit(solution)/shard_map/ppermute | solution.py:331

commit v6 on v5

--- a/solution.py
+++ b/solution.py
@@ -377,7 +377,8 @@
         [filters, shares],
         z_arg,
     )
-    x_pieces = after(x_pieces, weights_b, z_arg, c_blocks)
+    gate, weights_b = after((x_pieces[2], weights_b), z_arg, c_blocks)
+    x_pieces = after(x_pieces, weights_b)
 
     x_first, x_cells, x_bottom, x_top = call(
         functools.partial(turn_kernel, chan_count, height),
@@ -393,7 +394,7 @@
     )
     x_low = lax.ppermute(x_top, "space", upward)
     x_high = lax.ppermute(x_bottom, "space", downward)
-    c_pieces = swap(c_blocks[:1] + [after(c, x) for c, x in zip(c_blocks[1:], x_pieces[1:])])
+    c_pieces = swap(c_blocks[:1] + [after(c, gate) for c in c_blocks[1:]])
     slope_inner = call(
         functools.partial(forward_inner_kernel, height),
         [shape((columns + 2, cells - 2 * height, channels), F32)],

time: 128 us -> 123 us (0.961)
  starting transfers between devices: 35.9 us -> 33.7 us
  waiting for transfers between devices: 9.84 us -> 8.41 us
    ppermute x6, starting transfers between devices: 12.9 us -> 8.77 us  [swap(): lax.ppermute(blocks[j], 'chan', [(i, i ^ j) for i in range(count)])]
    ppermute x6, waiting for transfers between devices: 2.69 us -> 0.02 us  [swap(): lax.ppermute(blocks[j], 'chan', [(i, i ^ j) for i in range(count)])]
    ppermute x2, starting transfers between devices: 3.24 us -> 5.32 us  [body(): lax.ppermute(first[j], 'chan', ring(chan_count, j))]
  transfers between devices with their start and end apart: 23 -> 23, of which waited for: 7 -> 6; matrix products, arithmetic and copies ran while one was open for 5% -> 5% of each run, Pallas kernels for 33% -> 34%
where the time goes in v6:
time: 123 us
  Pallas kernels  45.1 us (37%)
  starting transfers between devices  33.7 us (27%)
  blocking collectives  21.4 us (17%)
  local copies, waits for them, and re-layouts  12.3 us (10%)
  waiting for transfers between devices  8.41 us (7%)
    pallas_call x9, Pallas kernels, call(): pl.pallas_call(kernel, out_shape=outs, in_specs=[pl.BlockSpec(memory_spac...  45.1 us
    all_gather x1, blocking collectives, body(): shares = lax.all_gather(share, 'space', axis=0, tiled=False)  12.4 us
    all_gather x1, blocking collectives, body(): whole = lax.all_gather(shard_sum, 'space', axis=0, tiled=True)  8.96 us
    ppermute x6, starting transfers between devices, swap(): lax.ppermute(blocks[j], 'chan', [(i, i ^ j) for i in range(count)])  8.77 us
    ppermute x6, starting transfers between devices, exchange(): lax.ppermute(blocks[j], axis, ring(count, j))  7.58 us
    ppermute x6, waiting for transfers between devices, exchange(): lax.ppermute(blocks[j], axis, ring(count, j))  5.51 us
    ppermute x2, starting transfers between devices, body(): lax.ppermute(first[j], 'chan', ring(chan_count, j))  5.32 us
    unnamed x33, local copies, waits for them, and re-layouts  3.91 us
  transfers between devices with their start and end apart: 23, of which 6 were waited for; matrix products, arithmetic and copies ran while one was open for 5% of the time, Pallas kernels for 34%

profile of v6, /device:TPU:0, one launch (start us, length us, event | category | flops | bytes accessed | tf_op | source)
XLA Modules:
  0.0 122.8 jit_solution(13450026731762875840)
XLA Ops:
  0.7 0.9 pad_dynamic-slice_fusion.8
  1.6 3.1 %collective-permute-start = (bf16[432,128]{1,0:T(8,128)(2,1)S(1)}, bf16[432,128]{1,0:T(8,128)(2,1)S(1)}, u32[]{:S(2)}, u32[]{:S(2)}) collective-permute-start(bf16[432,128]{1,0:T(8,128)(2,1)S(1)} %pad_dynamic-slice_fusion.8), channel_id=1, source_target_pairs={{0,1},{1,2},{2,3},{3,0},{4,6},{5,7},{6,4},{7,5},{8,11},{9,8},{10,9... | collective-permute-start | bytes 331784 | tf_op jit(solution)/shard_map/ppermute | solution.py:350
  4.7 1.9 %copy.9 = bf16[32,128,128]{1,0,2:T(8,128)(2,1)S(1)} copy(bf16[32,128,128]{2,1,0:T(8,128)(2,1)} %bitcast.42) | data formatting | bytes 2097152 | tf_op jit(solution)/shard_map/reshape | solution.py:308
  6.6 1.0 pad_dynamic-slice_fusion.4
  7.6 0.6 pad_add_fusion.z_ref._
  8.3 1.6 %collective-permute-done = bf16[432,128]{1,0:T(8,128)(2,1)S(1)} collective-permute-done((bf16[432,128]{1,0:T(8,128)(2,1)S(1)}, bf16[432,128]{1,0:T(8,128)(2,1)S(1)}, u32[]{:S(2)}, u32[]{:S(2)}) %collective-permute-start) | collective-permute-done | bytes 110624 | tf_op jit(solution)/shard_map/ppermute | solution.py:350
  9.9 2.7 %collective-permute-start.1 = (bf16[36,32,128]{2,1,0:T(8,128)(2,1)S(1)}, bf16[36,32,128]{2,1,0:T(8,128)(2,1)S(1)}, u32[]{:S(2)}, u32[]{:S(2)}) collective-permute-start(bf16[36,32,128]{2,1,0:T(8,128)(2,1)S(1)} %get-tuple-element.54), channel_id=1, source_target_pairs={{0,2},{1,3},{2,0},{3,1},{4,6},{5,7},{6,4},{7,5},{8,10},{9,11},{10,... | collective-permute-start | bytes 884744 | tf_op jit(solution)/shard_map/ppermute | solution.py:322
  12.6 1.7 %collective-permute-start.6 = (bf16[36,32,128]{2,1,0:T(8,128)(2,1)S(1)}, bf16[36,32,128]{2,1,0:T(8,128)(2,1)}, u32[]{:S(2)}, u32[]{:S(2)}) collective-permute-start(bf16[36,32,128]{2,1,0:T(8,128)(2,1)S(1)} %get-tuple-element.62), channel_id=1, source_target_pairs={{0,3},{1,2},{2,1},{3,0},{4,7},{5,6},{6,5},{7,4},{8,11},{9,10},{10,... | collective-permute-start | bytes 884744 | tf_op jit(solution)/shard_map/ppermute | solution.py:322
  14.3 12.4 %all-gather = bf16[3456,128]{1,0:T(8,128)(2,1)} all-gather(bf16[432,128]{1,0:T(8,128)(2,1)S(1)} %collective-permute-done), channel_id=2, replica_groups=mesh['space'=8,'chan'=4] {'space'}, dimensions={0}, use_global_device_ids=true | all-gather | bytes 995328 | tf_op jit(solution)/shard_map/all_gather | solution.py:370
  26.7 1.0 copy.8
  27.7 2.9 %shard_map.50 = (bf16[1152,384]{1,0:T(8,128)(2,1)}, bf16[1152,384]{1,0:T(8,128)(2,1)}) custom-call(s32[3]{0:T(128)} %pad_add_fusion.z_ref._, bf16[27,32,128]{2,1,0:T(8,128)(2,1)} %own_ref.1, bf16[8,432,128]{2,1,0:T(8,128)(2,1)} %bitcast.41), custom_call_target="tpu_custom_call" | custom-call | tf_op jit(solution)/shard_map/pallas_call | solution.py:292
  30.6 1.0 pad_dynamic-slice_fusion
  31.5 0.6 collective-permute-start.2
  32.1 3.8 %collective-permute-start.3 = (bf16[37,32,128]{2,1,0:T(8,128)(2,1)S(1)}, bf16[37,32,128]{2,1,0:T(8,128)(2,1)S(1)}, u32[]{:S(2)}, u32[]{:S(2)}) collective-permute-start(bf16[37,32,128]{2,1,0:T(8,128)(2,1)S(1)} %get-tuple-element.58), channel_id=1, source_target_pairs={{0,2},{1,3},{2,0},{3,1},{4,6},{5,7},{6,4},{7,5},{8,10},{9,11},{10,... | collective-permute-start | bytes 909320 | tf_op jit(solution)/shard_map/ppermute | solution.py:322
  36.0 3.3 %shard_map.51 = (bf16[36,128,128]{2,1,0:T(8,128)(2,1)}, bf16[36,128,128]{2,1,0:T(8,128)(2,1)}, bf16[36,32,128]{2,1,0:T(8,128)(2,1)}, bf16[36,32,128]{2,1,0:T(8,128)(2,1)}) custom-call(s32[3]{0:T(128)} %pad_add_fusion.z_ref._, bf16[36,32,128]{2,1,0:T(8,128)(2,1)} %get-tuple-element.64.refs_0_, bf16[36,32,128]{2,1,0:T(8,128)(2,1)} %collective-permute-done.5.refs_1_, ...), custom_call_target="tpu_custom_call" | custom-call | tf_op jit(solution)/shard_map/pallas_call | solution.py:292
  39.2 2.6 %collective-permute-start.8 = (bf16[36,32,128]{2,1,0:T(8,128)(2,1)}, bf16[36,32,128]{2,1,0:T(8,128)(2,1)S(1)}, u32[]{:S(2)}, u32[]{:S(2)}) collective-permute-start(bf16[36,32,128]{2,1,0:T(8,128)(2,1)} %get-tuple-element.72), channel_id=1, source_target_pairs={{0,28},{4,0},{8,4},{12,8},{16,12},{20,16},{24,20},{28,24},{1,29},{... | collective-permute-start | bytes 884744 | tf_op jit(solution)/shard_map/ppermute | solution.py:396
  41.9 5.7 %shard_map.52.refs_4_ = f32[34,64,128]{2,1,0:T(8,128)} custom-call(s32[3]{0:T(128)} %pad_add_fusion.z_ref._, bf16[36,128,128]{2,1,0:T(8,128)(2,1)} %get-tuple-element.70.x_ref, bf16[1152,384]{1,0:T(8,128)(2,1)} %get-tuple-element.69.weights_ref), custom_call_target="tpu_custom_call" | custom-call | tf_op jit(solution)/shard_map/pallas_call | solution.py:292
  47.6 1.2 %collective-permute-done.7.low_ref = bf16[36,32,128]{2,1,0:T(8,128)(2,1)S(1)} collective-permute-done((bf16[36,32,128]{2,1,0:T(8,128)(2,1)}, bf16[36,32,128]{2,1,0:T(8,128)(2,1)S(1)}, u32[]{:S(2)}, u32[]{:S(2)}) %collective-permute-start.7) | collective-permute-done | bytes 294944 | tf_op jit(solution)/shard_map/ppermute | solution.py:395
  48.8 0.7 copy-done
  49.5 0.7 copy-done.1
  50.3 3.5 %shard_map.54.sides_ref = bf16[2,34,128,128]{3,2,1,0:T(8,128)(2,1)} custom-call(s32[3]{0:T(128)} %pad_add_fusion.z_ref._, bf16[36,128,128]{2,1,0:T(8,128)(2,1)} %get-tuple-element.70.x_ref, bf16[36,32,128]{2,1,0:T(8,128)(2,1)} %copy-done, bf16[36,32,128]{2,1,0:T(8,128)(2,1)} %copy-done.1), custom_call_target="tpu_custom_call" | custom-call | tf_op jit(solution)/shard_map/pallas_call | solution.py:292
  53.8 6.0 %shard_map.53.refs_5_ = f32[34,64,128]{2,1,0:T(8,128)} custom-call(s32[3]{0:T(128)} %pad_add_fusion.z_ref._, bf16[36,128,128]{2,1,0:T(8,128)(2,1)} %get-tuple-element.70.x_ref, bf16[36,32,128]{2,1,0:T(8,128)(2,1)} %copy-done, bf16[36,32,128]{2,1,0:T(8,128)(2,1)} %copy-done.1, bf16[1152,384]{1,0:T(8,128)(2,1)} %get-tuple-element.69.weights_ref), custom_call_target="tpu_custom_call" | custom-call | tf_op jit(solution)/shard_map/pallas_call | solution.py:292
  59.8 0.7 copy-done.5
  60.5 0.1 copy-done.6
  60.6 0.8 copy-done.7
  61.4 3.7 %shard_map.55 = (bf16[34,128,128]{2,1,0:T(8,128)(2,1)}, bf16[34,32,128]{2,1,0:T(8,128)(2,1)}, bf16[34,32,128]{2,1,0:T(8,128)(2,1)}) custom-call(s32[3]{0:T(128)} %pad_add_fusion.z_ref._, bf16[37,32,128]{2,1,0:T(8,128)(2,1)} %get-tuple-element.113.refs_0_, bf16[37,32,128]{2,1,0:T(8,128)(2,1)} %copy-done.5, bf16[37,32,128]{2,1,0:T(8,128)(2,1)} %copy-done.6, ...), custom_call_target="tpu_custom_call" | custom-call | flops 5242880 | bytes 5111808 | tf_op jit(solution)/shard_map/pallas_call | solution.py:292
  65.0 0.4 collective-permute-start.9
  65.4 2.3 %collective-permute-start.10 = (bf16[34,32,128]{2,1,0:T(8,128)(2,1)}, bf16[34,32,128]{2,1,0:T(8,128)(2,1)S(1)}, u32[]{:S(2)}, u32[]{:S(2)}) collective-permute-start(bf16[34,32,128]{2,1,0:T(8,128)(2,1)} %get-tuple-element.76), channel_id=1, source_target_pairs={{0,28},{4,0},{8,4},{12,8},{16,12},{20,16},{24,20},{28,24},{1,29},{... | collective-permute-start | bytes 835592 | tf_op jit(solution)/shard_map/ppermute | solution.py:433
  67.7 9.1 %shard_map.56 = (f32[4,4,112,128]{3,2,1,0:T(8,128)}, f32[4,4,112,128]{3,2,1,0:T(8,128)}) custom-call(s32[1]{0:T(128)} %bitcast.9.core_ref, bf16[36,128,128]{2,1,0:T(8,128)(2,1)} %get-tuple-element.77.x_ref, bf16[2,34,128,128]{3,2,1,0:T(8,128)(2,1)} %shard_map.54.sides_ref, bf16[34,128,128]{2,1,0:T(8,128)(2,1)} %get-tuple-element.74.grad_ref), custom_call_target="tpu_custom_call" | custom-call | tf_op jit(solution)/shard_map/pallas_call | solution.py:292
  76.9 0.6 copy-done.9
  77.6 5.5 %shard_map.57 = (bf16[16,32,128]{2,1,0:T(8,128)(2,1)}, bf16[16,32,128]{2,1,0:T(8,128)(2,1)}, bf16[16,32,128]{2,1,0:T(8,128)(2,1)}, bf16[16,32,128]{2,1,0:T(8,128)(2,1)}) custom-call(s32[3]{0:T(128)} %pad_add_fusion.z_ref._, bf16[34,128,128]{2,1,0:T(8,128)(2,1)} %get-tuple-element.74.grad_ref, bf16[34,32,128]{2,1,0:T(8,128)(2,1)} %copy-done.9, ...), custom_call_target="tpu_custom_call" | custom-call | flops 5435817984 | bytes 3080192 | tf_op jit(solution)/shard_map/pallas_call | solution.py:292
  83.0 4.8 %collective-permute-start.15 = (bf16[16,32,128]{2,1,0:T(8,128)(2,1)}, bf16[16,32,128]{2,1,0:T(8,128)(2,1)S(1)}, u32[]{:S(2)}, u32[]{:S(2)}) collective-permute-start(bf16[16,32,128]{2,1,0:T(8,128)(2,1)} %get-tuple-element.92), channel_id=1, source_target_pairs={{0,1},{1,2},{2,3},{3,0},{4,5},{5,6},{6,7},{7,4},{8,9},{9,10},{10,1... | collective-permute-start | bytes 393224 | tf_op jit(solution)/shard_map/ppermute | solution.py:462
  87.8 0.5 collective-permute-start.16
  88.4 0.1 fusion.5
  88.6 2.1 %collective-permute-start.13 = (bf16[4,112,128]{2,1,0:T(8,128)(2,1)S(1)}, bf16[4,112,128]{2,1,0:T(8,128)(2,1)S(1)}, u32[]{:S(2)}, u32[]{:S(2)}) collective-permute-start(bf16[4,112,128]{2,1,0:T(8,128)(2,1)S(1)} %get-tuple-element.119), channel_id=1, source_target_pairs={{0,16},{4,20},{8,24},{12,28},{16,0},{20,4},{24,8},{28,12},{1,17},{... | collective-permute-start | bytes 344072 | tf_op jit(solution)/shard_map/ppermute | solution.py:472
  90.7 1.4 %collective-permute-start.14 = (bf16[4,112,128]{2,1,0:T(8,128)(2,1)S(1)}, bf16[4,112,128]{2,1,0:T(8,128)(2,1)S(1)}, u32[]{:S(2)}, u32[]{:S(2)}) collective-permute-start(bf16[4,112,128]{2,1,0:T(8,128)(2,1)S(1)} %get-tuple-element.118), channel_id=1, source_target_pairs={{0,24},{4,28},{8,16},{12,20},{16,8},{20,12},{24,0},{28,4},{1,25},{... | collective-permute-start | bytes 344072 | tf_op jit(solution)/shard_map/ppermute | solution.py:472
  92.1 5.5 %shard_map.58 = (bf16[32,32,128]{2,1,0:T(8,128)(2,1)}, bf16[16,32,128]{2,1,0:T(8,128)(2,1)}, bf16[16,32,128]{2,1,0:T(8,128)(2,1)}, bf16[32,32,128]{2,1,0:T(8,128)(2,1)}) custom-call(s32[3]{0:T(128)} %pad_add_fusion.z_ref._, bf16[34,128,128]{2,1,0:T(8,128)(2,1)} %get-tuple-element.74.grad_ref, bf16[34,32,128]{2,1,0:T(8,128)(2,1)} %copy-done.9, ...), custom_call_target="tpu_custom_call" | custom-call | flops 5435817984 | bytes 3604480 | tf_op jit(solution)/shard_map/pallas_call | solution.py:292
  97.8 3.0 %collective-permute-start.19 = (f32[112,128]{1,0:T(8,128)S(1)}, f32[112,128]{1,0:T(8,128)S(1)}, u32[]{:S(2)}, u32[]{:S(2)}) collective-permute-start(f32[112,128]{1,0:T(8,128)S(1)} %get-tuple-element.122), channel_id=1, source_target_pairs={{0,3},{1,0},{2,1},{3,2},{4,7},{5,4},{6,5},{7,6},{8,11},{9,8},{10,9... | collective-permute-start | bytes 172040 | tf_op jit(solution)/shard_map/ppermute | solution.py:331
  100.7 1.5 %collective-permute-start.17 = (f32[112,128]{1,0:T(8,128)S(1)}, f32[112,128]{1,0:T(8,128)S(1)}, u32[]{:S(2)}, u32[]{:S(2)}) collective-permute-start(f32[112,128]{1,0:T(8,128)S(1)} %get-tuple-element.121), channel_id=1, source_target_pairs={{0,1},{1,2},{2,3},{3,0},{4,5},{5,6},{6,7},{7,4},{8,9},{9,10},{10,1... | collective-permute-start | bytes 172040 | tf_op jit(solution)/shard_map/ppermute | solution.py:331
  102.2 0.3 collective-permute-done.19
  102.6 3.2 %collective-permute-done.18 = f32[112,128]{1,0:T(8,128)S(1)} collective-permute-done((f32[112,128]{1,0:T(8,128)S(1)}, f32[112,128]{1,0:T(8,128)S(1)}, u32[]{:S(2)}, u32[]{:S(2)}) %collective-permute-start.18) | collective-permute-done | bytes 57376 | tf_op jit(solution)/shard_map/ppermute | solution.py:331
  105.8 1.0 collective-permute-done.17
  106.8 1.2 collective-permute-start.20
  108.0 1.9 %collective-permute-start.22 = (bf16[16,32,128]{2,1,0:T(8,128)(2,1)}, bf16[16,32,128]{2,1,0:T(8,128)(2,1)S(1)}, u32[]{:S(2)}, u32[]{:S(2)}) collective-permute-start(bf16[16,32,128]{2,1,0:T(8,128)(2,1)} %get-tuple-element.102), channel_id=1, source_target_pairs={{0,1},{1,2},{2,3},{3,0},{4,5},{5,6},{6,7},{7,4},{8,9},{9,10},{10,1... | collective-permute-start | bytes 393224 | tf_op jit(solution)/shard_map/ppermute | solution.py:331
  109.9 9.0 %all_gather.11 = f32[896,128]{1,0:T(8,128)S(1)} all-gather(f32[112,128]{1,0:T(8,128)S(1)} %broadcast_multiply_fusion), channel_id=1, replica_groups=mesh['space'=8,'chan'=4] {'space'}, dimensions={0}, use_global_device_ids=true | all-gather | bytes 516096 | tf_op jit(solution)/shard_map/all_gather | solution.py:498
  118.9 0.8 slice.4
  119.7 0.9 collective-permute-done.21
  121.1 1.7 %copy.10 = bf16[32,128,128]{2,1,0:T(8,128)(2,1)} copy(bf16[32,128,128]{1,0,2:T(8,128)(2,1)S(1)} %dynamic-slice_bitcast_fusion) | data formatting | bytes 2097152 | tf_op jit(solution)/shard_map/transpose | solution.py:509
  (57 shorter events, 0.8 us)
Async XLA Ops:
  1.6 8.3 %collective-permute-start = (bf16[432,128]{1,0:T(8,128)(2,1)S(1)}, bf16[432,128]{1,0:T(8,128)(2,1)S(1)}, u32[]{:S(2)}, u32[]{:S(2)}) collective-permute-start(bf16[432,128]{1,0:T(8,128)(2,1)S(1)} %pad_dynamic-slice_fusion.8), channel_id=1, source_target_pairs={{0,1},{1,2},{2,3},{3,0},{4,6},{5,7},{6,4},{7,5},{8,11},{9,8},{10,9... | collective-permute-start | bytes 331784 | tf_op jit(solution)/shard_map/ppermute | solution.py:350
  6.6 20.1 %copy-start.2 = (bf16[32,4,32,128]{3,2,1,0:T(8,128)(2,1)S(1)}, bf16[32,4,32,128]{3,2,1,0:T(8,128)(2,1)}, u32[]{:S(2)}) copy-start(bf16[32,4,32,128]{3,2,1,0:T(8,128)(2,1)} %param.5) | copy-start | bytes 3145732
  9.9 21.6 %collective-permute-start.1 = (bf16[36,32,128]{2,1,0:T(8,128)(2,1)S(1)}, bf16[36,32,128]{2,1,0:T(8,128)(2,1)S(1)}, u32[]{:S(2)}, u32[]{:S(2)}) collective-permute-start(bf16[36,32,128]{2,1,0:T(8,128)(2,1)S(1)} %get-tuple-element.54), channel_id=1, source_target_pairs={{0,2},{1,3},{2,0},{3,1},{4,6},{5,7},{6,4},{7,5},{8,10},{9,11},{10,... | collective-permute-start | bytes 884744 | tf_op jit(solution)/shard_map/ppermute | solution.py:322
  12.6 23.4 %collective-permute-start.5 = (bf16[36,32,128]{2,1,0:T(8,128)(2,1)S(1)}, bf16[36,32,128]{2,1,0:T(8,128)(2,1)}, u32[]{:S(2)}, u32[]{:S(2)}) collective-permute-start(bf16[36,32,128]{2,1,0:T(8,128)(2,1)S(1)} %get-tuple-element.61), channel_id=1, source_target_pairs={{0,1},{1,0},{2,3},{3,2},{4,5},{5,4},{6,7},{7,6},{8,9},{9,8},{10,11... | collective-permute-start | bytes 884744 | tf_op jit(solution)/shard_map/ppermute | solution.py:322
  12.6 23.4 %collective-permute-start.6 = (bf16[36,32,128]{2,1,0:T(8,128)(2,1)S(1)}, bf16[36,32,128]{2,1,0:T(8,128)(2,1)}, u32[]{:S(2)}, u32[]{:S(2)}) collective-permute-start(bf16[36,32,128]{2,1,0:T(8,128)(2,1)S(1)} %get-tuple-element.62), channel_id=1, source_target_pairs={{0,3},{1,2},{2,1},{3,0},{4,7},{5,6},{6,5},{7,4},{8,11},{9,10},{10,... | collective-permute-start | bytes 884744 | tf_op jit(solution)/shard_map/ppermute | solution.py:322
  31.5 4.4 %copy-start.8 = (bf16[36,32,128]{2,1,0:T(8,128)(2,1)}, bf16[36,32,128]{2,1,0:T(8,128)(2,1)S(1)}, u32[]{:S(2)}) copy-start(bf16[36,32,128]{2,1,0:T(8,128)(2,1)S(1)} %collective-permute-done.1.refs_2_) | copy-start | bytes 884740
  31.5 28.2 %collective-permute-start.2 = (bf16[37,32,128]{2,1,0:T(8,128)(2,1)S(1)}, bf16[37,32,128]{2,1,0:T(8,128)(2,1)S(1)}, u32[]{:S(2)}, u32[]{:S(2)}) collective-permute-start(bf16[37,32,128]{2,1,0:T(8,128)(2,1)S(1)} %get-tuple-element.57), channel_id=1, source_target_pairs={{0,1},{1,0},{2,3},{3,2},{4,5},{5,4},{6,7},{7,6},{8,9},{9,8},{10,11... | collective-permute-start | bytes 909320 | tf_op jit(solution)/shard_map/ppermute | solution.py:322
  32.1 27.7 %collective-permute-start.3 = (bf16[37,32,128]{2,1,0:T(8,128)(2,1)S(1)}, bf16[37,32,128]{2,1,0:T(8,128)(2,1)S(1)}, u32[]{:S(2)}, u32[]{:S(2)}) collective-permute-start(bf16[37,32,128]{2,1,0:T(8,128)(2,1)S(1)} %get-tuple-element.58), channel_id=1, source_target_pairs={{0,2},{1,3},{2,0},{3,1},{4,6},{5,7},{6,4},{7,5},{8,10},{9,11},{10,... | collective-permute-start | bytes 909320 | tf_op jit(solution)/shard_map/ppermute | solution.py:322
  35.9 23.9 %collective-permute-start.4 = (bf16[37,32,128]{2,1,0:T(8,128)(2,1)S(1)}, bf16[37,32,128]{2,1,0:T(8,128)(2,1)S(1)}, u32[]{:S(2)}, u32[]{:S(2)}) collective-permute-start(bf16[37,32,128]{2,1,0:T(8,128)(2,1)S(1)} %get-tuple-element.59), channel_id=1, source_target_pairs={{0,3},{1,2},{2,1},{3,0},{4,7},{5,6},{6,5},{7,4},{8,11},{9,10},{10,... | collective-permute-start | bytes 909320 | tf_op jit(solution)/shard_map/ppermute | solution.py:322
  39.2 9.6 %collective-permute-start.7 = (bf16[36,32,128]{2,1,0:T(8,128)(2,1)}, bf16[36,32,128]{2,1,0:T(8,128)(2,1)S(1)}, u32[]{:S(2)}, u32[]{:S(2)}) collective-permute-start(bf16[36,32,128]{2,1,0:T(8,128)(2,1)} %get-tuple-element.71), channel_id=1, source_target_pairs={{0,4},{4,8},{8,12},{12,16},{16,20},{20,24},{24,28},{28,0},{1,5},{5... | collective-permute-start | bytes 884744 | tf_op jit(solution)/shard_map/ppermute | solution.py:395
  39.2 9.6 %collective-permute-start.8 = (bf16[36,32,128]{2,1,0:T(8,128)(2,1)}, bf16[36,32,128]{2,1,0:T(8,128)(2,1)S(1)}, u32[]{:S(2)}, u32[]{:S(2)}) collective-permute-start(bf16[36,32,128]{2,1,0:T(8,128)(2,1)} %get-tuple-element.72), channel_id=1, source_target_pairs={{0,28},{4,0},{8,4},{12,8},{16,12},{20,16},{24,20},{28,24},{1,29},{... | collective-permute-start | bytes 884744 | tf_op jit(solution)/shard_map/ppermute | solution.py:396
  48.8 0.7 copy-start
  49.5 0.7 copy-start.1
  59.8 0.7 copy-start.5
  59.8 0.8 copy-start.6
  60.6 0.8 copy-start.7
  65.0 11.7 %collective-permute-start.9 = (bf16[34,32,128]{2,1,0:T(8,128)(2,1)}, bf16[34,32,128]{2,1,0:T(8,128)(2,1)S(1)}, u32[]{:S(2)}, u32[]{:S(2)}) collective-permute-start(bf16[34,32,128]{2,1,0:T(8,128)(2,1)} %get-tuple-element.75), channel_id=1, source_target_pairs={{0,4},{4,8},{8,12},{12,16},{16,20},{20,24},{24,28},{28,0},{1,5},{5... | collective-permute-start | bytes 835592 | tf_op jit(solution)/shard_map/ppermute | solution.py:432
  65.4 11.4 %collective-permute-start.10 = (bf16[34,32,128]{2,1,0:T(8,128)(2,1)}, bf16[34,32,128]{2,1,0:T(8,128)(2,1)S(1)}, u32[]{:S(2)}, u32[]{:S(2)}) collective-permute-start(bf16[34,32,128]{2,1,0:T(8,128)(2,1)} %get-tuple-element.76), channel_id=1, source_target_pairs={{0,28},{4,0},{8,4},{12,8},{16,12},{20,16},{24,20},{28,24},{1,29},{... | collective-permute-start | bytes 835592 | tf_op jit(solution)/shard_map/ppermute | solution.py:433
  76.8 0.7 copy-start.9
  76.8 0.8 copy-start.10
  76.8 11.6 %collective-permute-start.11 = (f32[4,4,112,128]{3,2,1,0:T(8,128)}, f32[4,4,112,128]{3,2,1,0:T(8,128)S(1)}, u32[]{:S(2)}, u32[]{:S(2)}) collective-permute-start(f32[4,4,112,128]{3,2,1,0:T(8,128)} %get-tuple-element.82), channel_id=1, source_target_pairs={{0,4},{4,0},{8,12},{12,8},{16,20},{20,16},{24,28},{28,24},{1,5},{5... | collective-permute-start | bytes 2752520 | tf_op jit(solution)/shard_map/ppermute | solution.py:450
  77.6 10.8 %copy-start.4 = (f32[4,4,112,128]{3,2,1,0:T(8,128)S(1)}, f32[4,4,112,128]{3,2,1,0:T(8,128)}, u32[]{:S(2)}) copy-start(f32[4,4,112,128]{3,2,1,0:T(8,128)} %get-tuple-element.81) | copy-start | bytes 2752516
  83.0 14.6 %collective-permute-start.15 = (bf16[16,32,128]{2,1,0:T(8,128)(2,1)}, bf16[16,32,128]{2,1,0:T(8,128)(2,1)S(1)}, u32[]{:S(2)}, u32[]{:S(2)}) collective-permute-start(bf16[16,32,128]{2,1,0:T(8,128)(2,1)} %get-tuple-element.92), channel_id=1, source_target_pairs={{0,1},{1,2},{2,3},{3,0},{4,5},{5,6},{6,7},{7,4},{8,9},{9,10},{10,1... | collective-permute-start | bytes 393224 | tf_op jit(solution)/shard_map/ppermute | solution.py:462
  87.8 9.8 %collective-permute-start.16 = (bf16[16,32,128]{2,1,0:T(8,128)(2,1)}, bf16[16,32,128]{2,1,0:T(8,128)(2,1)S(1)}, u32[]{:S(2)}, u32[]{:S(2)}) collective-permute-start(bf16[16,32,128]{2,1,0:T(8,128)(2,1)} %get-tuple-element.93), channel_id=1, source_target_pairs={{0,2},{1,3},{2,0},{3,1},{4,6},{5,7},{6,4},{7,5},{8,10},{9,11},{10,... | collective-permute-start | bytes 393224 | tf_op jit(solution)/shard_map/ppermute | solution.py:462
  88.5 9.1 %collective-permute-start.12 = (bf16[4,112,128]{2,1,0:T(8,128)(2,1)S(1)}, bf16[4,112,128]{2,1,0:T(8,128)(2,1)S(1)}, u32[]{:S(2)}, u32[]{:S(2)}) collective-permute-start(bf16[4,112,128]{2,1,0:T(8,128)(2,1)S(1)} %get-tuple-element.120), channel_id=1, source_target_pairs={{0,8},{4,12},{8,0},{12,4},{16,24},{20,28},{24,16},{28,20},{1,9},{5... | collective-permute-start | bytes 344072 | tf_op jit(solution)/shard_map/ppermute | solution.py:472
  88.6 9.0 %collective-permute-start.13 = (bf16[4,112,128]{2,1,0:T(8,128)(2,1)S(1)}, bf16[4,112,128]{2,1,0:T(8,128)(2,1)S(1)}, u32[]{:S(2)}, u32[]{:S(2)}) collective-permute-start(bf16[4,112,128]{2,1,0:T(8,128)(2,1)S(1)} %get-tuple-element.119), channel_id=1, source_target_pairs={{0,16},{4,20},{8,24},{12,28},{16,0},{20,4},{24,8},{28,12},{1,17},{... | collective-permute-start | bytes 344072 | tf_op jit(solution)/shard_map/ppermute | solution.py:472
  90.7 6.9 %collective-permute-start.14 = (bf16[4,112,128]{2,1,0:T(8,128)(2,1)S(1)}, bf16[4,112,128]{2,1,0:T(8,128)(2,1)S(1)}, u32[]{:S(2)}, u32[]{:S(2)}) collective-permute-start(bf16[4,112,128]{2,1,0:T(8,128)(2,1)S(1)} %get-tuple-element.118), channel_id=1, source_target_pairs={{0,24},{4,28},{8,16},{12,20},{16,8},{20,12},{24,0},{28,4},{1,25},{... | collective-permute-start | bytes 344072 | tf_op jit(solution)/shard_map/ppermute | solution.py:472
  97.7 23.1 %copy-start.3 = (bf16[32,32,128]{2,1,0:T(8,128)(2,1)S(1)}, bf16[32,32,128]{2,1,0:T(8,128)(2,1)}, u32[]{:S(2)}) copy-start(bf16[32,32,128]{2,1,0:T(8,128)(2,1)} %get-tuple-element.103) | copy-start | bytes 786436
  97.8 4.8 %collective-permute-start.19 = (f32[112,128]{1,0:T(8,128)S(1)}, f32[112,128]{1,0:T(8,128)S(1)}, u32[]{:S(2)}, u32[]{:S(2)}) collective-permute-start(f32[112,128]{1,0:T(8,128)S(1)} %get-tuple-element.122), channel_id=1, source_target_pairs={{0,3},{1,0},{2,1},{3,2},{4,7},{5,4},{6,5},{7,6},{8,11},{9,8},{10,9... | collective-permute-start | bytes 172040 | tf_op jit(solution)/shard_map/ppermute | solution.py:331
  100.7 5.1 %collective-permute-start.18 = (f32[112,128]{1,0:T(8,128)S(1)}, f32[112,128]{1,0:T(8,128)S(1)}, u32[]{:S(2)}, u32[]{:S(2)}) collective-permute-start(f32[112,128]{1,0:T(8,128)S(1)} %get-tuple-element.123), channel_id=1, source_target_pairs={{0,2},{1,3},{2,0},{3,1},{4,6},{5,7},{6,4},{7,5},{8,10},{9,11},{10,... | collective-permute-start | bytes 172040 | tf_op jit(solution)/shard_map/ppermute | solution.py:331
  100.7 6.1 %collective-permute-start.17 = (f32[112,128]{1,0:T(8,128)S(1)}, f32[112,128]{1,0:T(8,128)S(1)}, u32[]{:S(2)}, u32[]{:S(2)}) collective-permute-start(f32[112,128]{1,0:T(8,128)S(1)} %get-tuple-element.121), channel_id=1, source_target_pairs={{0,1},{1,2},{2,3},{3,0},{4,5},{5,6},{6,7},{7,4},{8,9},{9,10},{10,1... | collective-permute-start | bytes 172040 | tf_op jit(solution)/shard_map/ppermute | solution.py:331
  106.8 12.8 %collective-permute-start.20 = (bf16[32,32,128]{2,1,0:T(8,128)(2,1)}, bf16[32,32,128]{2,1,0:T(8,128)(2,1)S(1)}, u32[]{:S(2)}, u32[]{:S(2)}) collective-permute-start(bf16[32,32,128]{2,1,0:T(8,128)(2,1)} %get-tuple-element.100), channel_id=1, source_target_pairs={{0,3},{1,0},{2,1},{3,2},{4,7},{5,4},{6,5},{7,6},{8,11},{9,8},{10,9... | collective-permute-start | bytes 786440 | tf_op jit(solution)/shard_map/ppermute | solution.py:331
  108.0 12.7 %collective-permute-start.21 = (bf16[16,32,128]{2,1,0:T(8,128)(2,1)}, bf16[16,32,128]{2,1,0:T(8,128)(2,1)S(1)}, u32[]{:S(2)}, u32[]{:S(2)}) collective-permute-start(bf16[16,32,128]{2,1,0:T(8,128)(2,1)} %get-tuple-element.101), channel_id=1, source_target_pairs={{0,2},{1,3},{2,0},{3,1},{4,6},{5,7},{6,4},{7,5},{8,10},{9,11},{10,... | collective-permute-start | bytes 393224 | tf_op jit(solution)/shard_map/ppermute | solution.py:331
  108.0 12.7 %collective-permute-start.22 = (bf16[16,32,128]{2,1,0:T(8,128)(2,1)}, bf16[16,32,128]{2,1,0:T(8,128)(2,1)S(1)}, u32[]{:S(2)}, u32[]{:S(2)}) collective-permute-start(bf16[16,32,128]{2,1,0:T(8,128)(2,1)} %get-tuple-element.102), channel_id=1, source_target_pairs={{0,1},{1,2},{2,3},{3,0},{4,5},{5,6},{6,7},{7,4},{8,9},{9,10},{10,1... | collective-permute-start | bytes 393224 | tf_op jit(solution)/shard_map/ppermute | solution.py:331

commit v7 on v6

--- a/solution.py
+++ b/solution.py
@@ -62,7 +62,7 @@
 
 
 def block_step(rows):
-    return max(1, 2048 // rows)
+    return max(1, 4096 // rows)
 
 
 def over_columns(count, rows, visit):
@@ -491,8 +491,9 @@
         lax.dynamic_index_in_dim(chip_sum, lax.rem(z + j, chan_count), 0, keepdims=False)
         for j in range(chan_count)
     ]
-    shard_sum = sum(exchange(parts, "chan"))
-    returned = exchange(after(back, shard_sum), "chan")
+    summed = exchange(parts, "chan")
+    shard_sum = sum(summed)
+    returned = exchange(after(back, summed[2]), "chan")
     cell_total = planes * space_count * height * width
     shard_sum = shard_sum * (1.0 / math.sqrt(cell_total))
     whole = lax.all_gather(shard_sum, "space", axis=0, tiled=True)

time: 123 us -> 122 us (level)
  waiting for transfers between devices: 8.41 us -> 5.88 us
  starting transfers between devices: 33.7 us -> 35 us
    ppermute x6, waiting for transfers between devices: 5.51 us -> 3.09 us  [exchange(): lax.ppermute(blocks[j], axis, ring(count, j))]
  transfers between devices with their start and end apart: 23 -> 23, of which waited for: 6 -> 4; matrix products, arithmetic and copies ran while one was open for 5% -> 5% of each run, Pallas kernels for 34% -> 34%
where the time goes in v7:
time: 122 us; the launch traced here: 121 us
  Pallas kernels  44.5 us (36%)
  starting transfers between devices  35 us (29%)
  blocking collectives  21.6 us (18%)
  local copies, waits for them, and re-layouts  12.3 us (10%)
  waiting for transfers between devices  5.88 us (5%)
    pallas_call x9, Pallas kernels, call(): pl.pallas_call(kernel, out_shape=outs, in_specs=[pl.BlockSpec(memory_spac...  44.5 us
    all_gather x1, blocking collectives, body(): shares = lax.all_gather(share, 'space', axis=0, tiled=False)  12.4 us
    all_gather x1, blocking collectives, body(): whole = lax.all_gather(shard_sum, 'space', axis=0, tiled=True)  9.22 us
    ppermute x6, starting transfers between devices, exchange(): lax.ppermute(blocks[j], axis, ring(count, j))  8.78 us
    ppermute x6, starting transfers between devices, swap(): lax.ppermute(blocks[j], 'chan', [(i, i ^ j) for i in range(count)])  8.77 us
    ppermute x2, starting transfers between devices, body(): lax.ppermute(first[j], 'chan', ring(chan_count, j))  5.49 us
    unnamed x33, local copies, waits for them, and re-layouts  3.91 us
    ppermute x3, starting transfers between devices, body(): lax.ppermute(block, 'space', [(i, i ^ 2 * k) for i in range(space_count)])  3.55 us
  transfers between devices with their start and end apart: 23, of which 4 were waited for; matrix products, arithmetic and copies ran while one was open for 5% of the time, Pallas kernels for 34%

profile of v7, /device:TPU:0, one launch (start us, length us, event | category | flops | bytes accessed | tf_op | source)
XLA Modules:
  0.0 121.3 jit_solution(9103469598448462758)
XLA Ops:
  0.7 0.9 pad_dynamic-slice_fusion.8
  1.6 3.1 %collective-permute-start = (bf16[432,128]{1,0:T(8,128)(2,1)S(1)}, bf16[432,128]{1,0:T(8,128)(2,1)S(1)}, u32[]{:S(2)}, u32[]{:S(2)}) collective-permute-start(bf16[432,128]{1,0:T(8,128)(2,1)S(1)} %pad_dynamic-slice_fusion.8), channel_id=1, source_target_pairs={{0,1},{1,2},{2,3},{3,0},{4,6},{5,7},{6,4},{7,5},{8,11},{9,8},{10,9... | collective-permute-start | bytes 331784 | tf_op jit(solution)/shard_map/ppermute | solution.py:350
  4.7 1.9 %copy.9 = bf16[32,128,128]{1,0,2:T(8,128)(2,1)S(1)} copy(bf16[32,128,128]{2,1,0:T(8,128)(2,1)} %bitcast.43) | data formatting | bytes 2097152 | tf_op jit(solution)/shard_map/reshape | solution.py:308
  6.6 1.0 pad_dynamic-slice_fusion.4
  7.6 0.6 pad_add_fusion.z_ref._
  8.3 1.6 %collective-permute-done = bf16[432,128]{1,0:T(8,128)(2,1)S(1)} collective-permute-done((bf16[432,128]{1,0:T(8,128)(2,1)S(1)}, bf16[432,128]{1,0:T(8,128)(2,1)S(1)}, u32[]{:S(2)}, u32[]{:S(2)}) %collective-permute-start) | collective-permute-done | bytes 110624 | tf_op jit(solution)/shard_map/ppermute | solution.py:350
  9.9 2.7 %collective-permute-start.1 = (bf16[36,32,128]{2,1,0:T(8,128)(2,1)S(1)}, bf16[36,32,128]{2,1,0:T(8,128)(2,1)S(1)}, u32[]{:S(2)}, u32[]{:S(2)}) collective-permute-start(bf16[36,32,128]{2,1,0:T(8,128)(2,1)S(1)} %get-tuple-element.54), channel_id=1, source_target_pairs={{0,2},{1,3},{2,0},{3,1},{4,6},{5,7},{6,4},{7,5},{8,10},{9,11},{10,... | collective-permute-start | bytes 884744 | tf_op jit(solution)/shard_map/ppermute | solution.py:322
  12.6 1.7 %collective-permute-start.6 = (bf16[36,32,128]{2,1,0:T(8,128)(2,1)S(1)}, bf16[36,32,128]{2,1,0:T(8,128)(2,1)}, u32[]{:S(2)}, u32[]{:S(2)}) collective-permute-start(bf16[36,32,128]{2,1,0:T(8,128)(2,1)S(1)} %get-tuple-element.62), channel_id=1, source_target_pairs={{0,3},{1,2},{2,1},{3,0},{4,7},{5,6},{6,5},{7,4},{8,11},{9,10},{10,... | collective-permute-start | bytes 884744 | tf_op jit(solution)/shard_map/ppermute | solution.py:322
  14.3 12.4 %all-gather = bf16[3456,128]{1,0:T(8,128)(2,1)} all-gather(bf16[432,128]{1,0:T(8,128)(2,1)S(1)} %collective-permute-done), channel_id=2, replica_groups=mesh['space'=8,'chan'=4] {'space'}, dimensions={0}, use_global_device_ids=true | all-gather | bytes 995328 | tf_op jit(solution)/shard_map/all_gather | solution.py:370
  26.7 1.0 copy.8
  27.7 2.9 %shard_map.50 = (bf16[1152,384]{1,0:T(8,128)(2,1)}, bf16[1152,384]{1,0:T(8,128)(2,1)}) custom-call(s32[3]{0:T(128)} %pad_add_fusion.z_ref._, bf16[27,32,128]{2,1,0:T(8,128)(2,1)} %own_ref.1, bf16[8,432,128]{2,1,0:T(8,128)(2,1)} %bitcast.42), custom_call_target="tpu_custom_call" | custom-call | tf_op jit(solution)/shard_map/pallas_call | solution.py:292
  30.6 1.0 pad_dynamic-slice_fusion
  31.5 0.6 collective-permute-start.2
  32.1 3.8 %collective-permute-start.3 = (bf16[37,32,128]{2,1,0:T(8,128)(2,1)S(1)}, bf16[37,32,128]{2,1,0:T(8,128)(2,1)S(1)}, u32[]{:S(2)}, u32[]{:S(2)}) collective-permute-start(bf16[37,32,128]{2,1,0:T(8,128)(2,1)S(1)} %get-tuple-element.58), channel_id=1, source_target_pairs={{0,2},{1,3},{2,0},{3,1},{4,6},{5,7},{6,4},{7,5},{8,10},{9,11},{10,... | collective-permute-start | bytes 909320 | tf_op jit(solution)/shard_map/ppermute | solution.py:322
  36.0 3.1 %shard_map.51 = (bf16[36,128,128]{2,1,0:T(8,128)(2,1)}, bf16[36,128,128]{2,1,0:T(8,128)(2,1)}, bf16[36,32,128]{2,1,0:T(8,128)(2,1)}, bf16[36,32,128]{2,1,0:T(8,128)(2,1)}) custom-call(s32[3]{0:T(128)} %pad_add_fusion.z_ref._, bf16[36,32,128]{2,1,0:T(8,128)(2,1)} %get-tuple-element.64.refs_0_, bf16[36,32,128]{2,1,0:T(8,128)(2,1)} %collective-permute-done.5.refs_1_, ...), custom_call_target="tpu_custom_call" | custom-call | tf_op jit(solution)/shard_map/pallas_call | solution.py:292
  39.1 2.6 %collective-permute-start.8 = (bf16[36,32,128]{2,1,0:T(8,128)(2,1)}, bf16[36,32,128]{2,1,0:T(8,128)(2,1)S(1)}, u32[]{:S(2)}, u32[]{:S(2)}) collective-permute-start(bf16[36,32,128]{2,1,0:T(8,128)(2,1)} %get-tuple-element.72), channel_id=1, source_target_pairs={{0,28},{4,0},{8,4},{12,8},{16,12},{20,16},{24,20},{28,24},{1,29},{... | collective-permute-start | bytes 884744 | tf_op jit(solution)/shard_map/ppermute | solution.py:396
  41.7 5.8 %shard_map.52.refs_4_ = f32[34,64,128]{2,1,0:T(8,128)} custom-call(s32[3]{0:T(128)} %pad_add_fusion.z_ref._, bf16[36,128,128]{2,1,0:T(8,128)(2,1)} %get-tuple-element.70.x_ref, bf16[1152,384]{1,0:T(8,128)(2,1)} %get-tuple-element.69.weights_ref), custom_call_target="tpu_custom_call" | custom-call | tf_op jit(solution)/shard_map/pallas_call | solution.py:292
  47.5 1.1 collective-permute-done.7.low_ref
  48.6 0.7 copy-done
  49.4 0.7 copy-done.1
  50.1 3.4 %shard_map.54.sides_ref = bf16[2,34,128,128]{3,2,1,0:T(8,128)(2,1)} custom-call(s32[3]{0:T(128)} %pad_add_fusion.z_ref._, bf16[36,128,128]{2,1,0:T(8,128)(2,1)} %get-tuple-element.70.x_ref, bf16[36,32,128]{2,1,0:T(8,128)(2,1)} %copy-done, bf16[36,32,128]{2,1,0:T(8,128)(2,1)} %copy-done.1), custom_call_target="tpu_custom_call" | custom-call | tf_op jit(solution)/shard_map/pallas_call | solution.py:292
  53.5 6.1 %shard_map.53.refs_5_ = f32[34,64,128]{2,1,0:T(8,128)} custom-call(s32[3]{0:T(128)} %pad_add_fusion.z_ref._, bf16[36,128,128]{2,1,0:T(8,128)(2,1)} %get-tuple-element.70.x_ref, bf16[36,32,128]{2,1,0:T(8,128)(2,1)} %copy-done, bf16[36,32,128]{2,1,0:T(8,128)(2,1)} %copy-done.1, bf16[1152,384]{1,0:T(8,128)(2,1)} %get-tuple-element.69.weights_ref), custom_call_target="tpu_custom_call" | custom-call | tf_op jit(solution)/shard_map/pallas_call | solution.py:292
  59.6 0.7 copy-done.5
  60.3 0.1 copy-done.6
  60.4 0.8 copy-done.7
  61.2 3.5 %shard_map.55 = (bf16[34,128,128]{2,1,0:T(8,128)(2,1)}, bf16[34,32,128]{2,1,0:T(8,128)(2,1)}, bf16[34,32,128]{2,1,0:T(8,128)(2,1)}) custom-call(s32[3]{0:T(128)} %pad_add_fusion.z_ref._, bf16[37,32,128]{2,1,0:T(8,128)(2,1)} %get-tuple-element.111.refs_0_, bf16[37,32,128]{2,1,0:T(8,128)(2,1)} %copy-done.5, bf16[37,32,128]{2,1,0:T(8,128)(2,1)} %copy-done.6, ...), custom_call_target="tpu_custom_call" | custom-call | flops 5242880 | bytes 5111808 | tf_op jit(solution)/shard_map/pallas_call | solution.py:292
  64.7 0.4 collective-permute-start.9
  65.1 2.3 %collective-permute-start.10 = (bf16[34,32,128]{2,1,0:T(8,128)(2,1)}, bf16[34,32,128]{2,1,0:T(8,128)(2,1)S(1)}, u32[]{:S(2)}, u32[]{:S(2)}) collective-permute-start(bf16[34,32,128]{2,1,0:T(8,128)(2,1)} %get-tuple-element.76), channel_id=1, source_target_pairs={{0,28},{4,0},{8,4},{12,8},{16,12},{20,16},{24,20},{28,24},{1,29},{... | collective-permute-start | bytes 835592 | tf_op jit(solution)/shard_map/ppermute | solution.py:433
  67.4 8.6 %shard_map.56 = (f32[4,4,112,128]{3,2,1,0:T(8,128)}, f32[4,4,112,128]{3,2,1,0:T(8,128)}) custom-call(s32[1]{0:T(128)} %bitcast.9.core_ref, bf16[36,128,128]{2,1,0:T(8,128)(2,1)} %get-tuple-element.77.x_ref, bf16[2,34,128,128]{3,2,1,0:T(8,128)(2,1)} %shard_map.54.sides_ref, bf16[34,128,128]{2,1,0:T(8,128)(2,1)} %get-tuple-element.74.grad_ref), custom_call_target="tpu_custom_call" | custom-call | tf_op jit(solution)/shard_map/pallas_call | solution.py:292
  76.2 0.6 copy-done.9
  76.7 0.1 copy-done.10
  76.8 5.5 %shard_map.57 = (bf16[16,32,128]{2,1,0:T(8,128)(2,1)}, bf16[16,32,128]{2,1,0:T(8,128)(2,1)}, bf16[16,32,128]{2,1,0:T(8,128)(2,1)}, bf16[16,32,128]{2,1,0:T(8,128)(2,1)}) custom-call(s32[3]{0:T(128)} %pad_add_fusion.z_ref._, bf16[34,128,128]{2,1,0:T(8,128)(2,1)} %get-tuple-element.74.grad_ref, bf16[34,32,128]{2,1,0:T(8,128)(2,1)} %copy-done.9, ...), custom_call_target="tpu_custom_call" | custom-call | flops 5435817984 | bytes 3080192 | tf_op jit(solution)/shard_map/pallas_call | solution.py:292
  82.3 5.0 %collective-permute-start.15 = (bf16[16,32,128]{2,1,0:T(8,128)(2,1)}, bf16[16,32,128]{2,1,0:T(8,128)(2,1)S(1)}, u32[]{:S(2)}, u32[]{:S(2)}) collective-permute-start(bf16[16,32,128]{2,1,0:T(8,128)(2,1)} %get-tuple-element.92), channel_id=1, source_target_pairs={{0,1},{1,2},{2,3},{3,0},{4,5},{5,6},{6,7},{7,4},{8,9},{9,10},{10,1... | collective-permute-start | bytes 393224 | tf_op jit(solution)/shard_map/ppermute | solution.py:462
  87.2 0.5 collective-permute-start.16
  87.8 0.1 fusion.5
  88.0 2.1 %collective-permute-start.13 = (bf16[4,112,128]{2,1,0:T(8,128)(2,1)S(1)}, bf16[4,112,128]{2,1,0:T(8,128)(2,1)S(1)}, u32[]{:S(2)}, u32[]{:S(2)}) collective-permute-start(bf16[4,112,128]{2,1,0:T(8,128)(2,1)S(1)} %get-tuple-element.117), channel_id=1, source_target_pairs={{0,16},{4,20},{8,24},{12,28},{16,0},{20,4},{24,8},{28,12},{1,17},{... | collective-permute-start | bytes 344072 | tf_op jit(solution)/shard_map/ppermute | solution.py:472
  90.1 1.4 %collective-permute-start.14 = (bf16[4,112,128]{2,1,0:T(8,128)(2,1)S(1)}, bf16[4,112,128]{2,1,0:T(8,128)(2,1)S(1)}, u32[]{:S(2)}, u32[]{:S(2)}) collective-permute-start(bf16[4,112,128]{2,1,0:T(8,128)(2,1)S(1)} %get-tuple-element.116), channel_id=1, source_target_pairs={{0,24},{4,28},{8,16},{12,20},{16,8},{20,12},{24,0},{28,4},{1,25},{... | collective-permute-start | bytes 344072 | tf_op jit(solution)/shard_map/ppermute | solution.py:472
  91.5 5.5 %shard_map.58 = (bf16[32,32,128]{2,1,0:T(8,128)(2,1)}, bf16[16,32,128]{2,1,0:T(8,128)(2,1)}, bf16[16,32,128]{2,1,0:T(8,128)(2,1)}, bf16[32,32,128]{2,1,0:T(8,128)(2,1)}) custom-call(s32[3]{0:T(128)} %pad_add_fusion.z_ref._, bf16[34,128,128]{2,1,0:T(8,128)(2,1)} %get-tuple-element.74.grad_ref, bf16[34,32,128]{2,1,0:T(8,128)(2,1)} %copy-done.9, ...), custom_call_target="tpu_custom_call" | custom-call | flops 5435817984 | bytes 3604480 | tf_op jit(solution)/shard_map/pallas_call | solution.py:292
  97.2 2.5 %collective-permute-start.17 = (f32[112,128]{1,0:T(8,128)S(1)}, f32[112,128]{1,0:T(8,128)S(1)}, u32[]{:S(2)}, u32[]{:S(2)}) collective-permute-start(f32[112,128]{1,0:T(8,128)S(1)} %get-tuple-element.121), channel_id=1, source_target_pairs={{0,2},{1,3},{2,0},{3,1},{4,6},{5,7},{6,4},{7,5},{8,10},{9,11},{10,... | collective-permute-start | bytes 172040 | tf_op jit(solution)/shard_map/ppermute | solution.py:331
  99.6 0.6 collective-permute-start.22
  100.2 1.4 %collective-permute-start.21 = (f32[112,128]{1,0:T(8,128)S(1)}, f32[112,128]{1,0:T(8,128)S(1)}, u32[]{:S(2)}, u32[]{:S(2)}) collective-permute-start(f32[112,128]{1,0:T(8,128)S(1)} %get-tuple-element.119), channel_id=1, source_target_pairs={{0,1},{1,2},{2,3},{3,0},{4,5},{5,6},{6,7},{7,4},{8,9},{9,10},{10,1... | collective-permute-start | bytes 172040 | tf_op jit(solution)/shard_map/ppermute | solution.py:331
  101.7 1.3 %collective-permute-done.17 = f32[112,128]{1,0:T(8,128)S(1)} collective-permute-done((f32[112,128]{1,0:T(8,128)S(1)}, f32[112,128]{1,0:T(8,128)S(1)}, u32[]{:S(2)}, u32[]{:S(2)}) %collective-permute-start.17) | collective-permute-done | bytes 57376 | tf_op jit(solution)/shard_map/ppermute | solution.py:331
  103.0 3.7 %collective-permute-start.18 = (bf16[32,32,128]{2,1,0:T(8,128)(2,1)}, bf16[32,32,128]{2,1,0:T(8,128)(2,1)S(1)}, u32[]{:S(2)}, u32[]{:S(2)}) collective-permute-start(bf16[32,32,128]{2,1,0:T(8,128)(2,1)} %get-tuple-element.100), channel_id=1, source_target_pairs={{0,3},{1,0},{2,1},{3,2},{4,7},{5,4},{6,5},{7,6},{8,11},{9,8},{10,9... | collective-permute-start | bytes 786440 | tf_op jit(solution)/shard_map/ppermute | solution.py:331
  106.7 0.6 collective-permute-start.20
  107.3 9.2 %all_gather.11 = f32[896,128]{1,0:T(8,128)S(1)} all-gather(f32[112,128]{1,0:T(8,128)S(1)} %fusion.4), channel_id=1, replica_groups=mesh['space'=8,'chan'=4] {'space'}, dimensions={0}, use_global_device_ids=true | all-gather | bytes 516096 | tf_op jit(solution)/shard_map/all_gather | solution.py:499
  116.5 0.8 slice.4
  117.3 1.8 %collective-permute-done.19 = bf16[16,32,128]{2,1,0:T(8,128)(2,1)S(1)} collective-permute-done((bf16[16,32,128]{2,1,0:T(8,128)(2,1)}, bf16[16,32,128]{2,1,0:T(8,128)(2,1)S(1)}, u32[]{:S(2)}, u32[]{:S(2)}) %collective-permute-start.19) | collective-permute-done | bytes 131104 | tf_op jit(solution)/shard_map/ppermute | solution.py:331
  119.6 1.7 %copy.10 = bf16[32,128,128]{2,1,0:T(8,128)(2,1)} copy(bf16[32,128,128]{1,0,2:T(8,128)(2,1)S(1)} %dynamic-slice_bitcast_fusion) | data formatting | bytes 2097152 | tf_op jit(solution)/shard_map/transpose | solution.py:510
  (57 shorter events, 0.7 us)
Async XLA Ops:
  1.6 8.3 %collective-permute-start = (bf16[432,128]{1,0:T(8,128)(2,1)S(1)}, bf16[432,128]{1,0:T(8,128)(2,1)S(1)}, u32[]{:S(2)}, u32[]{:S(2)}) collective-permute-start(bf16[432,128]{1,0:T(8,128)(2,1)S(1)} %pad_dynamic-slice_fusion.8), channel_id=1, source_target_pairs={{0,1},{1,2},{2,3},{3,0},{4,6},{5,7},{6,4},{7,5},{8,11},{9,8},{10,9... | collective-permute-start | bytes 331784 | tf_op jit(solution)/shard_map/ppermute | solution.py:350
  6.6 20.1 %copy-start.2 = (bf16[32,4,32,128]{3,2,1,0:T(8,128)(2,1)S(1)}, bf16[32,4,32,128]{3,2,1,0:T(8,128)(2,1)}, u32[]{:S(2)}) copy-start(bf16[32,4,32,128]{3,2,1,0:T(8,128)(2,1)} %param.5) | copy-start | bytes 3145732
  9.9 21.6 %collective-permute-start.1 = (bf16[36,32,128]{2,1,0:T(8,128)(2,1)S(1)}, bf16[36,32,128]{2,1,0:T(8,128)(2,1)S(1)}, u32[]{:S(2)}, u32[]{:S(2)}) collective-permute-start(bf16[36,32,128]{2,1,0:T(8,128)(2,1)S(1)} %get-tuple-element.54), channel_id=1, source_target_pairs={{0,2},{1,3},{2,0},{3,1},{4,6},{5,7},{6,4},{7,5},{8,10},{9,11},{10,... | collective-permute-start | bytes 884744 | tf_op jit(solution)/shard_map/ppermute | solution.py:322
  12.6 23.4 %collective-permute-start.5 = (bf16[36,32,128]{2,1,0:T(8,128)(2,1)S(1)}, bf16[36,32,128]{2,1,0:T(8,128)(2,1)}, u32[]{:S(2)}, u32[]{:S(2)}) collective-permute-start(bf16[36,32,128]{2,1,0:T(8,128)(2,1)S(1)} %get-tuple-element.61), channel_id=1, source_target_pairs={{0,1},{1,0},{2,3},{3,2},{4,5},{5,4},{6,7},{7,6},{8,9},{9,8},{10,11... | collective-permute-start | bytes 884744 | tf_op jit(solution)/shard_map/ppermute | solution.py:322
  12.6 23.4 %collective-permute-start.6 = (bf16[36,32,128]{2,1,0:T(8,128)(2,1)S(1)}, bf16[36,32,128]{2,1,0:T(8,128)(2,1)}, u32[]{:S(2)}, u32[]{:S(2)}) collective-permute-start(bf16[36,32,128]{2,1,0:T(8,128)(2,1)S(1)} %get-tuple-element.62), channel_id=1, source_target_pairs={{0,3},{1,2},{2,1},{3,0},{4,7},{5,6},{6,5},{7,4},{8,11},{9,10},{10,... | collective-permute-start | bytes 884744 | tf_op jit(solution)/shard_map/ppermute | solution.py:322
  31.5 4.4 %copy-start.8 = (bf16[36,32,128]{2,1,0:T(8,128)(2,1)}, bf16[36,32,128]{2,1,0:T(8,128)(2,1)S(1)}, u32[]{:S(2)}) copy-start(bf16[36,32,128]{2,1,0:T(8,128)(2,1)S(1)} %collective-permute-done.1.refs_2_) | copy-start | bytes 884740
  31.5 28.1 %collective-permute-start.2 = (bf16[37,32,128]{2,1,0:T(8,128)(2,1)S(1)}, bf16[37,32,128]{2,1,0:T(8,128)(2,1)S(1)}, u32[]{:S(2)}, u32[]{:S(2)}) collective-permute-start(bf16[37,32,128]{2,1,0:T(8,128)(2,1)S(1)} %get-tuple-element.57), channel_id=1, source_target_pairs={{0,1},{1,0},{2,3},{3,2},{4,5},{5,4},{6,7},{7,6},{8,9},{9,8},{10,11... | collective-permute-start | bytes 909320 | tf_op jit(solution)/shard_map/ppermute | solution.py:322
  32.1 27.5 %collective-permute-start.3 = (bf16[37,32,128]{2,1,0:T(8,128)(2,1)S(1)}, bf16[37,32,128]{2,1,0:T(8,128)(2,1)S(1)}, u32[]{:S(2)}, u32[]{:S(2)}) collective-permute-start(bf16[37,32,128]{2,1,0:T(8,128)(2,1)S(1)} %get-tuple-element.58), channel_id=1, source_target_pairs={{0,2},{1,3},{2,0},{3,1},{4,6},{5,7},{6,4},{7,5},{8,10},{9,11},{10,... | collective-permute-start | bytes 909320 | tf_op jit(solution)/shard_map/ppermute | solution.py:322
  35.9 23.7 %collective-permute-start.4 = (bf16[37,32,128]{2,1,0:T(8,128)(2,1)S(1)}, bf16[37,32,128]{2,1,0:T(8,128)(2,1)S(1)}, u32[]{:S(2)}, u32[]{:S(2)}) collective-permute-start(bf16[37,32,128]{2,1,0:T(8,128)(2,1)S(1)} %get-tuple-element.59), channel_id=1, source_target_pairs={{0,3},{1,2},{2,1},{3,0},{4,7},{5,6},{6,5},{7,4},{8,11},{9,10},{10,... | collective-permute-start | bytes 909320 | tf_op jit(solution)/shard_map/ppermute | solution.py:322
  39.1 9.6 %collective-permute-start.7 = (bf16[36,32,128]{2,1,0:T(8,128)(2,1)}, bf16[36,32,128]{2,1,0:T(8,128)(2,1)S(1)}, u32[]{:S(2)}, u32[]{:S(2)}) collective-permute-start(bf16[36,32,128]{2,1,0:T(8,128)(2,1)} %get-tuple-element.71), channel_id=1, source_target_pairs={{0,4},{4,8},{8,12},{12,16},{16,20},{20,24},{24,28},{28,0},{1,5},{5... | collective-permute-start | bytes 884744 | tf_op jit(solution)/shard_map/ppermute | solution.py:395
  39.1 9.6 %collective-permute-start.8 = (bf16[36,32,128]{2,1,0:T(8,128)(2,1)}, bf16[36,32,128]{2,1,0:T(8,128)(2,1)S(1)}, u32[]{:S(2)}, u32[]{:S(2)}) collective-permute-start(bf16[36,32,128]{2,1,0:T(8,128)(2,1)} %get-tuple-element.72), channel_id=1, source_target_pairs={{0,28},{4,0},{8,4},{12,8},{16,12},{20,16},{24,20},{28,24},{1,29},{... | collective-permute-start | bytes 884744 | tf_op jit(solution)/shard_map/ppermute | solution.py:396
  48.6 0.7 copy-start
  49.4 0.7 copy-start.1
  59.6 0.7 copy-start.5
  59.6 0.8 copy-start.6
  60.4 0.8 copy-start.7
  64.7 11.3 %collective-permute-start.9 = (bf16[34,32,128]{2,1,0:T(8,128)(2,1)}, bf16[34,32,128]{2,1,0:T(8,128)(2,1)S(1)}, u32[]{:S(2)}, u32[]{:S(2)}) collective-permute-start(bf16[34,32,128]{2,1,0:T(8,128)(2,1)} %get-tuple-element.75), channel_id=1, source_target_pairs={{0,4},{4,8},{8,12},{12,16},{16,20},{20,24},{24,28},{28,0},{1,5},{5... | collective-permute-start | bytes 835592 | tf_op jit(solution)/shard_map/ppermute | solution.py:432
  65.1 10.9 %collective-permute-start.10 = (bf16[34,32,128]{2,1,0:T(8,128)(2,1)}, bf16[34,32,128]{2,1,0:T(8,128)(2,1)S(1)}, u32[]{:S(2)}, u32[]{:S(2)}) collective-permute-start(bf16[34,32,128]{2,1,0:T(8,128)(2,1)} %get-tuple-element.76), channel_id=1, source_target_pairs={{0,28},{4,0},{8,4},{12,8},{16,12},{20,16},{24,20},{28,24},{1,29},{... | collective-permute-start | bytes 835592 | tf_op jit(solution)/shard_map/ppermute | solution.py:433
  76.0 0.7 copy-start.9
  76.0 0.8 copy-start.10
  76.0 11.8 %collective-permute-start.11 = (f32[4,4,112,128]{3,2,1,0:T(8,128)}, f32[4,4,112,128]{3,2,1,0:T(8,128)S(1)}, u32[]{:S(2)}, u32[]{:S(2)}) collective-permute-start(f32[4,4,112,128]{3,2,1,0:T(8,128)} %get-tuple-element.82), channel_id=1, source_target_pairs={{0,4},{4,0},{8,12},{12,8},{16,20},{20,16},{24,28},{28,24},{1,5},{5... | collective-permute-start | bytes 2752520 | tf_op jit(solution)/shard_map/ppermute | solution.py:450
  76.8 11.0 %copy-start.4 = (f32[4,4,112,128]{3,2,1,0:T(8,128)S(1)}, f32[4,4,112,128]{3,2,1,0:T(8,128)}, u32[]{:S(2)}) copy-start(f32[4,4,112,128]{3,2,1,0:T(8,128)} %get-tuple-element.81) | copy-start | bytes 2752516
  82.3 14.7 %collective-permute-start.15 = (bf16[16,32,128]{2,1,0:T(8,128)(2,1)}, bf16[16,32,128]{2,1,0:T(8,128)(2,1)S(1)}, u32[]{:S(2)}, u32[]{:S(2)}) collective-permute-start(bf16[16,32,128]{2,1,0:T(8,128)(2,1)} %get-tuple-element.92), channel_id=1, source_target_pairs={{0,1},{1,2},{2,3},{3,0},{4,5},{5,6},{6,7},{7,4},{8,9},{9,10},{10,1... | collective-permute-start | bytes 393224 | tf_op jit(solution)/shard_map/ppermute | solution.py:462
  87.2 9.8 %collective-permute-start.16 = (bf16[16,32,128]{2,1,0:T(8,128)(2,1)}, bf16[16,32,128]{2,1,0:T(8,128)(2,1)S(1)}, u32[]{:S(2)}, u32[]{:S(2)}) collective-permute-start(bf16[16,32,128]{2,1,0:T(8,128)(2,1)} %get-tuple-element.93), channel_id=1, source_target_pairs={{0,2},{1,3},{2,0},{3,1},{4,6},{5,7},{6,4},{7,5},{8,10},{9,11},{10,... | collective-permute-start | bytes 393224 | tf_op jit(solution)/shard_map/ppermute | solution.py:462
  88.0 9.1 %collective-permute-start.12 = (bf16[4,112,128]{2,1,0:T(8,128)(2,1)S(1)}, bf16[4,112,128]{2,1,0:T(8,128)(2,1)S(1)}, u32[]{:S(2)}, u32[]{:S(2)}) collective-permute-start(bf16[4,112,128]{2,1,0:T(8,128)(2,1)S(1)} %get-tuple-element.118), channel_id=1, source_target_pairs={{0,8},{4,12},{8,0},{12,4},{16,24},{20,28},{24,16},{28,20},{1,9},{5... | collective-permute-start | bytes 344072 | tf_op jit(solution)/shard_map/ppermute | solution.py:472
  88.0 9.0 %collective-permute-start.13 = (bf16[4,112,128]{2,1,0:T(8,128)(2,1)S(1)}, bf16[4,112,128]{2,1,0:T(8,128)(2,1)S(1)}, u32[]{:S(2)}, u32[]{:S(2)}) collective-permute-start(bf16[4,112,128]{2,1,0:T(8,128)(2,1)S(1)} %get-tuple-element.117), channel_id=1, source_target_pairs={{0,16},{4,20},{8,24},{12,28},{16,0},{20,4},{24,8},{28,12},{1,17},{... | collective-permute-start | bytes 344072 | tf_op jit(solution)/shard_map/ppermute | solution.py:472
  90.1 6.9 %collective-permute-start.14 = (bf16[4,112,128]{2,1,0:T(8,128)(2,1)S(1)}, bf16[4,112,128]{2,1,0:T(8,128)(2,1)S(1)}, u32[]{:S(2)}, u32[]{:S(2)}) collective-permute-start(bf16[4,112,128]{2,1,0:T(8,128)(2,1)S(1)} %get-tuple-element.116), channel_id=1, source_target_pairs={{0,24},{4,28},{8,16},{12,20},{16,8},{20,12},{24,0},{28,4},{1,25},{... | collective-permute-start | bytes 344072 | tf_op jit(solution)/shard_map/ppermute | solution.py:472
  97.1 22.2 %copy-start.3 = (bf16[32,32,128]{2,1,0:T(8,128)(2,1)S(1)}, bf16[32,32,128]{2,1,0:T(8,128)(2,1)}, u32[]{:S(2)}) copy-start(bf16[32,32,128]{2,1,0:T(8,128)(2,1)} %get-tuple-element.103) | copy-start | bytes 786436
  97.2 5.8 %collective-permute-start.17 = (f32[112,128]{1,0:T(8,128)S(1)}, f32[112,128]{1,0:T(8,128)S(1)}, u32[]{:S(2)}, u32[]{:S(2)}) collective-permute-start(f32[112,128]{1,0:T(8,128)S(1)} %get-tuple-element.121), channel_id=1, source_target_pairs={{0,2},{1,3},{2,0},{3,1},{4,6},{5,7},{6,4},{7,5},{8,10},{9,11},{10,... | collective-permute-start | bytes 172040 | tf_op jit(solution)/shard_map/ppermute | solution.py:331
  99.6 7.6 %collective-permute-start.22 = (f32[112,128]{1,0:T(8,128)S(1)}, f32[112,128]{1,0:T(8,128)S(1)}, u32[]{:S(2)}, u32[]{:S(2)}) collective-permute-start(f32[112,128]{1,0:T(8,128)S(1)} %get-tuple-element.120), channel_id=1, source_target_pairs={{0,3},{1,0},{2,1},{3,2},{4,7},{5,4},{6,5},{7,6},{8,11},{9,8},{10,9... | collective-permute-start | bytes 172040 | tf_op jit(solution)/shard_map/ppermute | solution.py:331
  100.2 7.0 %collective-permute-start.21 = (f32[112,128]{1,0:T(8,128)S(1)}, f32[112,128]{1,0:T(8,128)S(1)}, u32[]{:S(2)}, u32[]{:S(2)}) collective-permute-start(f32[112,128]{1,0:T(8,128)S(1)} %get-tuple-element.119), channel_id=1, source_target_pairs={{0,1},{1,2},{2,3},{3,0},{4,5},{5,6},{6,7},{7,4},{8,9},{9,10},{10,1... | collective-permute-start | bytes 172040 | tf_op jit(solution)/shard_map/ppermute | solution.py:331
  103.0 14.3 %collective-permute-start.18 = (bf16[32,32,128]{2,1,0:T(8,128)(2,1)}, bf16[32,32,128]{2,1,0:T(8,128)(2,1)S(1)}, u32[]{:S(2)}, u32[]{:S(2)}) collective-permute-start(bf16[32,32,128]{2,1,0:T(8,128)(2,1)} %get-tuple-element.100), channel_id=1, source_target_pairs={{0,3},{1,0},{2,1},{3,2},{4,7},{5,4},{6,5},{7,6},{8,11},{9,8},{10,9... | collective-permute-start | bytes 786440 | tf_op jit(solution)/shard_map/ppermute | solution.py:331
  106.7 12.4 %collective-permute-start.19 = (bf16[16,32,128]{2,1,0:T(8,128)(2,1)}, bf16[16,32,128]{2,1,0:T(8,128)(2,1)S(1)}, u32[]{:S(2)}, u32[]{:S(2)}) collective-permute-start(bf16[16,32,128]{2,1,0:T(8,128)(2,1)} %get-tuple-element.101), channel_id=1, source_target_pairs={{0,2},{1,3},{2,0},{3,1},{4,6},{5,7},{6,4},{7,5},{8,10},{9,11},{10,... | collective-permute-start | bytes 393224 | tf_op jit(solution)/shard_map/ppermute | solution.py:331
  106.7 12.5 %collective-permute-start.20 = (bf16[16,32,128]{2,1,0:T(8,128)(2,1)}, bf16[16,32,128]{2,1,0:T(8,128)(2,1)S(1)}, u32[]{:S(2)}, u32[]{:S(2)}) collective-permute-start(bf16[16,32,128]{2,1,0:T(8,128)(2,1)} %get-tuple-element.102), channel_id=1, source_target_pairs={{0,1},{1,2},{2,3},{3,0},{4,5},{5,6},{6,7},{7,4},{8,9},{9,10},{10,1... | collective-permute-start | bytes 393224 | tf_op jit(solution)/shard_map/ppermute | solution.py:331

commit v8 on v7

--- a/solution.py
+++ b/solution.py
@@ -68,7 +68,9 @@
 def over_columns(count, rows, visit):
     step = block_step(rows)
     loops, rest = count // step, count % step
-    if loops:
+    if loops == 1:
+        visit(0, step)
+    elif loops:
         pl.loop(0, loops)(lambda i: visit(i * step, step))
     if rest:
         visit(loops * step, rest)
@@ -213,7 +215,9 @@
 ):
     columns, cells, channels = grad_ref.shape
     group = channels // chan_count
-    acc_ref[...] = jnp.zeros_like(acc_ref)
+    single = columns - 2 <= block_step(cells)
+    if not single:
+        acc_ref[...] = jnp.zeros_like(acc_ref)
 
     def visit(k, count):
         lhs = jnp.concatenate(
@@ -233,7 +237,8 @@
         grad = grad_ref[pl.ds(k + 1, count)].reshape(count * cells, channels).astype(F32)
         later, earlier = row_shifts(grad, height)
         rhs = jnp.concatenate([v.astype(BF16) for v in (later, grad, earlier)], axis=1)
-        acc_ref[...] += jnp.dot(lhs, rhs, preferred_element_type=F32)
+        product = jnp.dot(lhs, rhs, preferred_element_type=F32)
+        acc_ref[...] = product if single else acc_ref[...] + product
 
     over_columns(columns - 2, cells, visit)
     used = 27 * group
@@ -493,7 +498,8 @@
     ]
     summed = exchange(parts, "chan")
     shard_sum = sum(summed)
-    returned = exchange(after(back, summed[2]), "chan")
+    gated = [after(block, shard_sum if j in split else summed[2]) for j, block in enumerate(back)]
+    returned = exchange(gated, "chan")
     cell_total = planes * space_count * height * width
     shard_sum = shard_sum * (1.0 / math.sqrt(cell_total))
     whole = lax.all_gather(shard_sum, "space", axis=0, tiled=True)

time: 122 us -> 122 us (level)
  no operation moved by 1% of the time
where the time goes in v8:
time: 122 us; the launch traced here: 121 us
  Pallas kernels  44.5 us (36%)
  starting transfers between devices  35 us (29%)
  blocking collectives  21.7 us (18%)
  local copies, waits for them, and re-layouts  12.3 us (10%)
  waiting for transfers between devices  5.77 us (5%)
    pallas_call x9, Pallas kernels, call(): pl.pallas_call(kernel, out_shape=outs, in_specs=[pl.BlockSpec(memory_spac...  44.5 us
    all_gather x1, blocking collectives, body(): shares = lax.all_gather(share, 'space', axis=0, tiled=False)  12.4 us
    all_gather x1, blocking collectives, body(): whole = lax.all_gather(shard_sum, 'space', axis=0, tiled=True)  9.31 us
    ppermute x6, starting transfers between devices, exchange(): lax.ppermute(blocks[j], axis, ring(count, j))  8.8 us
    ppermute x6, starting transfers between devices, swap(): lax.ppermute(blocks[j], 'chan', [(i, i ^ j) for i in range(count)])  8.77 us
    ppermute x2, starting transfers between devices, body(): lax.ppermute(first[j], 'chan', ring(chan_count, j))  5.49 us
    unnamed x33, local copies, waits for them, and re-layouts  3.91 us
    ppermute x3, starting transfers between devices, body(): lax.ppermute(block, 'space', [(i, i ^ 2 * k) for i in range(space_count)])  3.55 us
  transfers between devices with their start and end apart: 23, of which 4 were waited for; matrix products, arithmetic and copies ran while one was open for 5% of the time, Pallas kernels for 34%

profile of v8, /device:TPU:0, one launch (start us, length us, event | category | flops | bytes accessed | tf_op | source)
XLA Modules:
  0.0 121.3 jit_solution(9500440043896380309)
XLA Ops:
  0.7 0.9 pad_dynamic-slice_fusion.8
  1.6 3.1 %collective-permute-start = (bf16[432,128]{1,0:T(8,128)(2,1)S(1)}, bf16[432,128]{1,0:T(8,128)(2,1)S(1)}, u32[]{:S(2)}, u32[]{:S(2)}) collective-permute-start(bf16[432,128]{1,0:T(8,128)(2,1)S(1)} %pad_dynamic-slice_fusion.8), channel_id=1, source_target_pairs={{0,1},{1,2},{2,3},{3,0},{4,6},{5,7},{6,4},{7,5},{8,11},{9,8},{10,9... | collective-permute-start | bytes 331784 | tf_op jit(solution)/shard_map/ppermute | solution.py:355
  4.7 1.9 %copy.9 = bf16[32,128,128]{1,0,2:T(8,128)(2,1)S(1)} copy(bf16[32,128,128]{2,1,0:T(8,128)(2,1)} %bitcast.42) | data formatting | bytes 2097152 | tf_op jit(solution)/shard_map/reshape | solution.py:313
  6.6 1.0 pad_dynamic-slice_fusion.4
  7.6 0.6 pad_add_fusion.z_ref._
  8.3 1.6 %collective-permute-done = bf16[432,128]{1,0:T(8,128)(2,1)S(1)} collective-permute-done((bf16[432,128]{1,0:T(8,128)(2,1)S(1)}, bf16[432,128]{1,0:T(8,128)(2,1)S(1)}, u32[]{:S(2)}, u32[]{:S(2)}) %collective-permute-start) | collective-permute-done | bytes 110624 | tf_op jit(solution)/shard_map/ppermute | solution.py:355
  9.9 2.7 %collective-permute-start.1 = (bf16[36,32,128]{2,1,0:T(8,128)(2,1)S(1)}, bf16[36,32,128]{2,1,0:T(8,128)(2,1)S(1)}, u32[]{:S(2)}, u32[]{:S(2)}) collective-permute-start(bf16[36,32,128]{2,1,0:T(8,128)(2,1)S(1)} %get-tuple-element.54), channel_id=1, source_target_pairs={{0,2},{1,3},{2,0},{3,1},{4,6},{5,7},{6,4},{7,5},{8,10},{9,11},{10,... | collective-permute-start | bytes 884744 | tf_op jit(solution)/shard_map/ppermute | solution.py:327
  12.6 1.7 %collective-permute-start.6 = (bf16[36,32,128]{2,1,0:T(8,128)(2,1)S(1)}, bf16[36,32,128]{2,1,0:T(8,128)(2,1)}, u32[]{:S(2)}, u32[]{:S(2)}) collective-permute-start(bf16[36,32,128]{2,1,0:T(8,128)(2,1)S(1)} %get-tuple-element.62), channel_id=1, source_target_pairs={{0,3},{1,2},{2,1},{3,0},{4,7},{5,6},{6,5},{7,4},{8,11},{9,10},{10,... | collective-permute-start | bytes 884744 | tf_op jit(solution)/shard_map/ppermute | solution.py:327
  14.3 12.4 %all-gather = bf16[3456,128]{1,0:T(8,128)(2,1)} all-gather(bf16[432,128]{1,0:T(8,128)(2,1)S(1)} %collective-permute-done), channel_id=2, replica_groups=mesh['space'=8,'chan'=4] {'space'}, dimensions={0}, use_global_device_ids=true | all-gather | bytes 995328 | tf_op jit(solution)/shard_map/all_gather | solution.py:375
  26.7 1.0 copy.8
  27.7 2.9 %shard_map.50 = (bf16[1152,384]{1,0:T(8,128)(2,1)}, bf16[1152,384]{1,0:T(8,128)(2,1)}) custom-call(s32[3]{0:T(128)} %pad_add_fusion.z_ref._, bf16[27,32,128]{2,1,0:T(8,128)(2,1)} %own_ref.1, bf16[8,432,128]{2,1,0:T(8,128)(2,1)} %bitcast.41), custom_call_target="tpu_custom_call" | custom-call | tf_op jit(solution)/shard_map/pallas_call | solution.py:297
  30.6 1.0 pad_dynamic-slice_fusion
  31.5 0.6 collective-permute-start.2
  32.1 3.8 %collective-permute-start.3 = (bf16[37,32,128]{2,1,0:T(8,128)(2,1)S(1)}, bf16[37,32,128]{2,1,0:T(8,128)(2,1)S(1)}, u32[]{:S(2)}, u32[]{:S(2)}) collective-permute-start(bf16[37,32,128]{2,1,0:T(8,128)(2,1)S(1)} %get-tuple-element.58), channel_id=1, source_target_pairs={{0,2},{1,3},{2,0},{3,1},{4,6},{5,7},{6,4},{7,5},{8,10},{9,11},{10,... | collective-permute-start | bytes 909320 | tf_op jit(solution)/shard_map/ppermute | solution.py:327
  36.0 3.1 %shard_map.51 = (bf16[36,128,128]{2,1,0:T(8,128)(2,1)}, bf16[36,128,128]{2,1,0:T(8,128)(2,1)}, bf16[36,32,128]{2,1,0:T(8,128)(2,1)}, bf16[36,32,128]{2,1,0:T(8,128)(2,1)}) custom-call(s32[3]{0:T(128)} %pad_add_fusion.z_ref._, bf16[36,32,128]{2,1,0:T(8,128)(2,1)} %get-tuple-element.64.refs_0_, bf16[36,32,128]{2,1,0:T(8,128)(2,1)} %collective-permute-done.5.refs_1_, ...), custom_call_target="tpu_custom_call" | custom-call | tf_op jit(solution)/shard_map/pallas_call | solution.py:297
  39.1 2.6 %collective-permute-start.8 = (bf16[36,32,128]{2,1,0:T(8,128)(2,1)}, bf16[36,32,128]{2,1,0:T(8,128)(2,1)S(1)}, u32[]{:S(2)}, u32[]{:S(2)}) collective-permute-start(bf16[36,32,128]{2,1,0:T(8,128)(2,1)} %get-tuple-element.72), channel_id=1, source_target_pairs={{0,28},{4,0},{8,4},{12,8},{16,12},{20,16},{24,20},{28,24},{1,29},{... | collective-permute-start | bytes 884744 | tf_op jit(solution)/shard_map/ppermute | solution.py:401
  41.7 5.8 %shard_map.52.refs_4_ = f32[34,64,128]{2,1,0:T(8,128)} custom-call(s32[3]{0:T(128)} %pad_add_fusion.z_ref._, bf16[36,128,128]{2,1,0:T(8,128)(2,1)} %get-tuple-element.70.x_ref, bf16[1152,384]{1,0:T(8,128)(2,1)} %get-tuple-element.69.weights_ref), custom_call_target="tpu_custom_call" | custom-call | tf_op jit(solution)/shard_map/pallas_call | solution.py:297
  47.5 1.1 collective-permute-done.7.low_ref
  48.6 0.7 copy-done
  49.4 0.7 copy-done.1
  50.1 3.4 %shard_map.54.sides_ref = bf16[2,34,128,128]{3,2,1,0:T(8,128)(2,1)} custom-call(s32[3]{0:T(128)} %pad_add_fusion.z_ref._, bf16[36,128,128]{2,1,0:T(8,128)(2,1)} %get-tuple-element.70.x_ref, bf16[36,32,128]{2,1,0:T(8,128)(2,1)} %copy-done, bf16[36,32,128]{2,1,0:T(8,128)(2,1)} %copy-done.1), custom_call_target="tpu_custom_call" | custom-call | tf_op jit(solution)/shard_map/pallas_call | solution.py:297
  53.5 6.1 %shard_map.53.refs_5_ = f32[34,64,128]{2,1,0:T(8,128)} custom-call(s32[3]{0:T(128)} %pad_add_fusion.z_ref._, bf16[36,128,128]{2,1,0:T(8,128)(2,1)} %get-tuple-element.70.x_ref, bf16[36,32,128]{2,1,0:T(8,128)(2,1)} %copy-done, bf16[36,32,128]{2,1,0:T(8,128)(2,1)} %copy-done.1, bf16[1152,384]{1,0:T(8,128)(2,1)} %get-tuple-element.69.weights_ref), custom_call_target="tpu_custom_call" | custom-call | tf_op jit(solution)/shard_map/pallas_call | solution.py:297
  59.6 0.7 copy-done.5
  60.3 0.1 copy-done.6
  60.4 0.8 copy-done.7
  61.2 3.5 %shard_map.55 = (bf16[34,128,128]{2,1,0:T(8,128)(2,1)}, bf16[34,32,128]{2,1,0:T(8,128)(2,1)}, bf16[34,32,128]{2,1,0:T(8,128)(2,1)}) custom-call(s32[3]{0:T(128)} %pad_add_fusion.z_ref._, bf16[37,32,128]{2,1,0:T(8,128)(2,1)} %get-tuple-element.113.refs_0_, bf16[37,32,128]{2,1,0:T(8,128)(2,1)} %copy-done.5, bf16[37,32,128]{2,1,0:T(8,128)(2,1)} %copy-done.6, ...), custom_call_target="tpu_custom_call" | custom-call | flops 5242880 | bytes 5111808 | tf_op jit(solution)/shard_map/pallas_call | solution.py:297
  64.7 0.4 collective-permute-start.9
  65.1 2.3 %collective-permute-start.10 = (bf16[34,32,128]{2,1,0:T(8,128)(2,1)}, bf16[34,32,128]{2,1,0:T(8,128)(2,1)S(1)}, u32[]{:S(2)}, u32[]{:S(2)}) collective-permute-start(bf16[34,32,128]{2,1,0:T(8,128)(2,1)} %get-tuple-element.76), channel_id=1, source_target_pairs={{0,28},{4,0},{8,4},{12,8},{16,12},{20,16},{24,20},{28,24},{1,29},{... | collective-permute-start | bytes 835592 | tf_op jit(solution)/shard_map/ppermute | solution.py:438
  67.4 8.6 %shard_map.56 = (f32[4,4,112,128]{3,2,1,0:T(8,128)}, f32[4,4,112,128]{3,2,1,0:T(8,128)}) custom-call(s32[1]{0:T(128)} %bitcast.9.core_ref, bf16[36,128,128]{2,1,0:T(8,128)(2,1)} %get-tuple-element.77.x_ref, bf16[2,34,128,128]{3,2,1,0:T(8,128)(2,1)} %shard_map.54.sides_ref, bf16[34,128,128]{2,1,0:T(8,128)(2,1)} %get-tuple-element.74.grad_ref), custom_call_target="tpu_custom_call" | custom-call | tf_op jit(solution)/shard_map/pallas_call | solution.py:297
  76.2 0.6 copy-done.9
  76.7 0.1 copy-done.10
  76.8 5.5 %shard_map.57 = (bf16[16,32,128]{2,1,0:T(8,128)(2,1)}, bf16[16,32,128]{2,1,0:T(8,128)(2,1)}, bf16[16,32,128]{2,1,0:T(8,128)(2,1)}, bf16[16,32,128]{2,1,0:T(8,128)(2,1)}) custom-call(s32[3]{0:T(128)} %pad_add_fusion.z_ref._, bf16[34,128,128]{2,1,0:T(8,128)(2,1)} %get-tuple-element.74.grad_ref, bf16[34,32,128]{2,1,0:T(8,128)(2,1)} %copy-done.9, ...), custom_call_target="tpu_custom_call" | custom-call | flops 5435817984 | bytes 3080192 | tf_op jit(solution)/shard_map/pallas_call | solution.py:297
  82.3 5.0 %collective-permute-start.15 = (bf16[16,32,128]{2,1,0:T(8,128)(2,1)}, bf16[16,32,128]{2,1,0:T(8,128)(2,1)S(1)}, u32[]{:S(2)}, u32[]{:S(2)}) collective-permute-start(bf16[16,32,128]{2,1,0:T(8,128)(2,1)} %get-tuple-element.89), channel_id=1, source_target_pairs={{0,1},{1,2},{2,3},{3,0},{4,5},{5,6},{6,7},{7,4},{8,9},{9,10},{10,1... | collective-permute-start | bytes 393224 | tf_op jit(solution)/shard_map/ppermute | solution.py:467
  87.2 0.5 collective-permute-start.16
  87.8 0.1 fusion.5
  88.0 2.1 %collective-permute-start.13 = (bf16[4,112,128]{2,1,0:T(8,128)(2,1)S(1)}, bf16[4,112,128]{2,1,0:T(8,128)(2,1)S(1)}, u32[]{:S(2)}, u32[]{:S(2)}) collective-permute-start(bf16[4,112,128]{2,1,0:T(8,128)(2,1)S(1)} %get-tuple-element.119), channel_id=1, source_target_pairs={{0,16},{4,20},{8,24},{12,28},{16,0},{20,4},{24,8},{28,12},{1,17},{... | collective-permute-start | bytes 344072 | tf_op jit(solution)/shard_map/ppermute | solution.py:477
  90.1 1.4 %collective-permute-start.14 = (bf16[4,112,128]{2,1,0:T(8,128)(2,1)S(1)}, bf16[4,112,128]{2,1,0:T(8,128)(2,1)S(1)}, u32[]{:S(2)}, u32[]{:S(2)}) collective-permute-start(bf16[4,112,128]{2,1,0:T(8,128)(2,1)S(1)} %get-tuple-element.118), channel_id=1, source_target_pairs={{0,24},{4,28},{8,16},{12,20},{16,8},{20,12},{24,0},{28,4},{1,25},{... | collective-permute-start | bytes 344072 | tf_op jit(solution)/shard_map/ppermute | solution.py:477
  91.5 5.5 %shard_map.58 = (bf16[32,32,128]{2,1,0:T(8,128)(2,1)}, bf16[16,32,128]{2,1,0:T(8,128)(2,1)}, bf16[16,32,128]{2,1,0:T(8,128)(2,1)}, bf16[32,32,128]{2,1,0:T(8,128)(2,1)}) custom-call(s32[3]{0:T(128)} %pad_add_fusion.z_ref._, bf16[34,128,128]{2,1,0:T(8,128)(2,1)} %get-tuple-element.74.grad_ref, bf16[34,32,128]{2,1,0:T(8,128)(2,1)} %copy-done.9, ...), custom_call_target="tpu_custom_call" | custom-call | flops 5435817984 | bytes 3604480 | tf_op jit(solution)/shard_map/pallas_call | solution.py:297
  97.2 2.5 %collective-permute-start.17 = (f32[112,128]{1,0:T(8,128)S(1)}, f32[112,128]{1,0:T(8,128)S(1)}, u32[]{:S(2)}, u32[]{:S(2)}) collective-permute-start(f32[112,128]{1,0:T(8,128)S(1)} %get-tuple-element.123), channel_id=1, source_target_pairs={{0,2},{1,3},{2,0},{3,1},{4,6},{5,7},{6,4},{7,5},{8,10},{9,11},{10,... | collective-permute-start | bytes 172040 | tf_op jit(solution)/shard_map/ppermute | solution.py:336
  99.6 0.6 collective-permute-start.20
  100.2 1.4 %collective-permute-start.19 = (f32[112,128]{1,0:T(8,128)S(1)}, f32[112,128]{1,0:T(8,128)S(1)}, u32[]{:S(2)}, u32[]{:S(2)}) collective-permute-start(f32[112,128]{1,0:T(8,128)S(1)} %get-tuple-element.121), channel_id=1, source_target_pairs={{0,1},{1,2},{2,3},{3,0},{4,5},{5,6},{6,7},{7,4},{8,9},{9,10},{10,1... | collective-permute-start | bytes 172040 | tf_op jit(solution)/shard_map/ppermute | solution.py:336
  101.7 1.3 %collective-permute-done.17 = f32[112,128]{1,0:T(8,128)S(1)} collective-permute-done((f32[112,128]{1,0:T(8,128)S(1)}, f32[112,128]{1,0:T(8,128)S(1)}, u32[]{:S(2)}, u32[]{:S(2)}) %collective-permute-start.17) | collective-permute-done | bytes 57376 | tf_op jit(solution)/shard_map/ppermute | solution.py:336
  103.0 3.7 %collective-permute-start.18 = (bf16[32,32,128]{2,1,0:T(8,128)(2,1)}, bf16[32,32,128]{2,1,0:T(8,128)(2,1)S(1)}, u32[]{:S(2)}, u32[]{:S(2)}) collective-permute-start(bf16[32,32,128]{2,1,0:T(8,128)(2,1)} %get-tuple-element.98), channel_id=1, source_target_pairs={{0,3},{1,0},{2,1},{3,2},{4,7},{5,4},{6,5},{7,6},{8,11},{9,8},{10,9... | collective-permute-start | bytes 786440 | tf_op jit(solution)/shard_map/ppermute | solution.py:336
  106.8 0.5 collective-permute-start.22
  107.4 9.3 %all_gather.11 = f32[896,128]{1,0:T(8,128)S(1)} all-gather(f32[112,128]{1,0:T(8,128)S(1)} %broadcast_multiply_fusion), channel_id=1, replica_groups=mesh['space'=8,'chan'=4] {'space'}, dimensions={0}, use_global_device_ids=true | all-gather | bytes 516096 | tf_op jit(solution)/shard_map/all_gather | solution.py:505
  116.7 0.8 slice.4
  117.5 1.6 %collective-permute-done.21 = bf16[16,32,128]{2,1,0:T(8,128)(2,1)S(1)} collective-permute-done((bf16[16,32,128]{2,1,0:T(8,128)(2,1)}, bf16[16,32,128]{2,1,0:T(8,128)(2,1)S(1)}, u32[]{:S(2)}, u32[]{:S(2)}) %collective-permute-start.21) | collective-permute-done | bytes 131104 | tf_op jit(solution)/shard_map/ppermute | solution.py:336
  119.6 1.7 %copy.10 = bf16[32,128,128]{2,1,0:T(8,128)(2,1)} copy(bf16[32,128,128]{1,0,2:T(8,128)(2,1)S(1)} %dynamic-slice_bitcast_fusion) | data formatting | bytes 2097152 | tf_op jit(solution)/shard_map/transpose | solution.py:516
  (57 shorter events, 0.8 us)
Async XLA Ops:
  1.6 8.3 %collective-permute-start = (bf16[432,128]{1,0:T(8,128)(2,1)S(1)}, bf16[432,128]{1,0:T(8,128)(2,1)S(1)}, u32[]{:S(2)}, u32[]{:S(2)}) collective-permute-start(bf16[432,128]{1,0:T(8,128)(2,1)S(1)} %pad_dynamic-slice_fusion.8), channel_id=1, source_target_pairs={{0,1},{1,2},{2,3},{3,0},{4,6},{5,7},{6,4},{7,5},{8,11},{9,8},{10,9... | collective-permute-start | bytes 331784 | tf_op jit(solution)/shard_map/ppermute | solution.py:355
  6.6 20.1 %copy-start.2 = (bf16[32,4,32,128]{3,2,1,0:T(8,128)(2,1)S(1)}, bf16[32,4,32,128]{3,2,1,0:T(8,128)(2,1)}, u32[]{:S(2)}) copy-start(bf16[32,4,32,128]{3,2,1,0:T(8,128)(2,1)} %param.5) | copy-start | bytes 3145732
  9.9 21.6 %collective-permute-start.1 = (bf16[36,32,128]{2,1,0:T(8,128)(2,1)S(1)}, bf16[36,32,128]{2,1,0:T(8,128)(2,1)S(1)}, u32[]{:S(2)}, u32[]{:S(2)}) collective-permute-start(bf16[36,32,128]{2,1,0:T(8,128)(2,1)S(1)} %get-tuple-element.54), channel_id=1, source_target_pairs={{0,2},{1,3},{2,0},{3,1},{4,6},{5,7},{6,4},{7,5},{8,10},{9,11},{10,... | collective-permute-start | bytes 884744 | tf_op jit(solution)/shard_map/ppermute | solution.py:327
  12.6 23.4 %collective-permute-start.5 = (bf16[36,32,128]{2,1,0:T(8,128)(2,1)S(1)}, bf16[36,32,128]{2,1,0:T(8,128)(2,1)}, u32[]{:S(2)}, u32[]{:S(2)}) collective-permute-start(bf16[36,32,128]{2,1,0:T(8,128)(2,1)S(1)} %get-tuple-element.61), channel_id=1, source_target_pairs={{0,1},{1,0},{2,3},{3,2},{4,5},{5,4},{6,7},{7,6},{8,9},{9,8},{10,11... | collective-permute-start | bytes 884744 | tf_op jit(solution)/shard_map/ppermute | solution.py:327
  12.6 23.4 %collective-permute-start.6 = (bf16[36,32,128]{2,1,0:T(8,128)(2,1)S(1)}, bf16[36,32,128]{2,1,0:T(8,128)(2,1)}, u32[]{:S(2)}, u32[]{:S(2)}) collective-permute-start(bf16[36,32,128]{2,1,0:T(8,128)(2,1)S(1)} %get-tuple-element.62), channel_id=1, source_target_pairs={{0,3},{1,2},{2,1},{3,0},{4,7},{5,6},{6,5},{7,4},{8,11},{9,10},{10,... | collective-permute-start | bytes 884744 | tf_op jit(solution)/shard_map/ppermute | solution.py:327
  31.5 4.4 %copy-start.8 = (bf16[36,32,128]{2,1,0:T(8,128)(2,1)}, bf16[36,32,128]{2,1,0:T(8,128)(2,1)S(1)}, u32[]{:S(2)}) copy-start(bf16[36,32,128]{2,1,0:T(8,128)(2,1)S(1)} %collective-permute-done.1.refs_2_) | copy-start | bytes 884740
  31.5 28.1 %collective-permute-start.2 = (bf16[37,32,128]{2,1,0:T(8,128)(2,1)S(1)}, bf16[37,32,128]{2,1,0:T(8,128)(2,1)S(1)}, u32[]{:S(2)}, u32[]{:S(2)}) collective-permute-start(bf16[37,32,128]{2,1,0:T(8,128)(2,1)S(1)} %get-tuple-element.57), channel_id=1, source_target_pairs={{0,1},{1,0},{2,3},{3,2},{4,5},{5,4},{6,7},{7,6},{8,9},{9,8},{10,11... | collective-permute-start | bytes 909320 | tf_op jit(solution)/shard_map/ppermute | solution.py:327
  32.1 27.5 %collective-permute-start.3 = (bf16[37,32,128]{2,1,0:T(8,128)(2,1)S(1)}, bf16[37,32,128]{2,1,0:T(8,128)(2,1)S(1)}, u32[]{:S(2)}, u32[]{:S(2)}) collective-permute-start(bf16[37,32,128]{2,1,0:T(8,128)(2,1)S(1)} %get-tuple-element.58), channel_id=1, source_target_pairs={{0,2},{1,3},{2,0},{3,1},{4,6},{5,7},{6,4},{7,5},{8,10},{9,11},{10,... | collective-permute-start | bytes 909320 | tf_op jit(solution)/shard_map/ppermute | solution.py:327
  35.9 23.7 %collective-permute-start.4 = (bf16[37,32,128]{2,1,0:T(8,128)(2,1)S(1)}, bf16[37,32,128]{2,1,0:T(8,128)(2,1)S(1)}, u32[]{:S(2)}, u32[]{:S(2)}) collective-permute-start(bf16[37,32,128]{2,1,0:T(8,128)(2,1)S(1)} %get-tuple-element.59), channel_id=1, source_target_pairs={{0,3},{1,2},{2,1},{3,0},{4,7},{5,6},{6,5},{7,4},{8,11},{9,10},{10,... | collective-permute-start | bytes 909320 | tf_op jit(solution)/shard_map/ppermute | solution.py:327
  39.1 9.6 %collective-permute-start.7 = (bf16[36,32,128]{2,1,0:T(8,128)(2,1)}, bf16[36,32,128]{2,1,0:T(8,128)(2,1)S(1)}, u32[]{:S(2)}, u32[]{:S(2)}) collective-permute-start(bf16[36,32,128]{2,1,0:T(8,128)(2,1)} %get-tuple-element.71), channel_id=1, source_target_pairs={{0,4},{4,8},{8,12},{12,16},{16,20},{20,24},{24,28},{28,0},{1,5},{5... | collective-permute-start | bytes 884744 | tf_op jit(solution)/shard_map/ppermute | solution.py:400
  39.1 9.6 %collective-permute-start.8 = (bf16[36,32,128]{2,1,0:T(8,128)(2,1)}, bf16[36,32,128]{2,1,0:T(8,128)(2,1)S(1)}, u32[]{:S(2)}, u32[]{:S(2)}) collective-permute-start(bf16[36,32,128]{2,1,0:T(8,128)(2,1)} %get-tuple-element.72), channel_id=1, source_target_pairs={{0,28},{4,0},{8,4},{12,8},{16,12},{20,16},{24,20},{28,24},{1,29},{... | collective-permute-start | bytes 884744 | tf_op jit(solution)/shard_map/ppermute | solution.py:401
  48.6 0.7 copy-start
  49.4 0.7 copy-start.1
  59.6 0.7 copy-start.5
  59.6 0.8 copy-start.6
  60.4 0.8 copy-start.7
  64.7 11.3 %collective-permute-start.9 = (bf16[34,32,128]{2,1,0:T(8,128)(2,1)}, bf16[34,32,128]{2,1,0:T(8,128)(2,1)S(1)}, u32[]{:S(2)}, u32[]{:S(2)}) collective-permute-start(bf16[34,32,128]{2,1,0:T(8,128)(2,1)} %get-tuple-element.75), channel_id=1, source_target_pairs={{0,4},{4,8},{8,12},{12,16},{16,20},{20,24},{24,28},{28,0},{1,5},{5... | collective-permute-start | bytes 835592 | tf_op jit(solution)/shard_map/ppermute | solution.py:437
  65.1 10.9 %collective-permute-start.10 = (bf16[34,32,128]{2,1,0:T(8,128)(2,1)}, bf16[34,32,128]{2,1,0:T(8,128)(2,1)S(1)}, u32[]{:S(2)}, u32[]{:S(2)}) collective-permute-start(bf16[34,32,128]{2,1,0:T(8,128)(2,1)} %get-tuple-element.76), channel_id=1, source_target_pairs={{0,28},{4,0},{8,4},{12,8},{16,12},{20,16},{24,20},{28,24},{1,29},{... | collective-permute-start | bytes 835592 | tf_op jit(solution)/shard_map/ppermute | solution.py:438
  76.0 0.7 copy-start.9
  76.0 0.8 copy-start.10
  76.0 11.8 %collective-permute-start.11 = (f32[4,4,112,128]{3,2,1,0:T(8,128)}, f32[4,4,112,128]{3,2,1,0:T(8,128)S(1)}, u32[]{:S(2)}, u32[]{:S(2)}) collective-permute-start(f32[4,4,112,128]{3,2,1,0:T(8,128)} %get-tuple-element.82), channel_id=1, source_target_pairs={{0,4},{4,0},{8,12},{12,8},{16,20},{20,16},{24,28},{28,24},{1,5},{5... | collective-permute-start | bytes 2752520 | tf_op jit(solution)/shard_map/ppermute | solution.py:455
  76.8 11.0 %copy-start.4 = (f32[4,4,112,128]{3,2,1,0:T(8,128)S(1)}, f32[4,4,112,128]{3,2,1,0:T(8,128)}, u32[]{:S(2)}) copy-start(f32[4,4,112,128]{3,2,1,0:T(8,128)} %get-tuple-element.81) | copy-start | bytes 2752516
  82.3 14.7 %collective-permute-start.15 = (bf16[16,32,128]{2,1,0:T(8,128)(2,1)}, bf16[16,32,128]{2,1,0:T(8,128)(2,1)S(1)}, u32[]{:S(2)}, u32[]{:S(2)}) collective-permute-start(bf16[16,32,128]{2,1,0:T(8,128)(2,1)} %get-tuple-element.89), channel_id=1, source_target_pairs={{0,1},{1,2},{2,3},{3,0},{4,5},{5,6},{6,7},{7,4},{8,9},{9,10},{10,1... | collective-permute-start | bytes 393224 | tf_op jit(solution)/shard_map/ppermute | solution.py:467
  87.2 9.8 %collective-permute-start.16 = (bf16[16,32,128]{2,1,0:T(8,128)(2,1)}, bf16[16,32,128]{2,1,0:T(8,128)(2,1)S(1)}, u32[]{:S(2)}, u32[]{:S(2)}) collective-permute-start(bf16[16,32,128]{2,1,0:T(8,128)(2,1)} %get-tuple-element.90), channel_id=1, source_target_pairs={{0,2},{1,3},{2,0},{3,1},{4,6},{5,7},{6,4},{7,5},{8,10},{9,11},{10,... | collective-permute-start | bytes 393224 | tf_op jit(solution)/shard_map/ppermute | solution.py:467
  88.0 9.1 %collective-permute-start.12 = (bf16[4,112,128]{2,1,0:T(8,128)(2,1)S(1)}, bf16[4,112,128]{2,1,0:T(8,128)(2,1)S(1)}, u32[]{:S(2)}, u32[]{:S(2)}) collective-permute-start(bf16[4,112,128]{2,1,0:T(8,128)(2,1)S(1)} %get-tuple-element.120), channel_id=1, source_target_pairs={{0,8},{4,12},{8,0},{12,4},{16,24},{20,28},{24,16},{28,20},{1,9},{5... | collective-permute-start | bytes 344072 | tf_op jit(solution)/shard_map/ppermute | solution.py:477
  88.0 9.0 %collective-permute-start.13 = (bf16[4,112,128]{2,1,0:T(8,128)(2,1)S(1)}, bf16[4,112,128]{2,1,0:T(8,128)(2,1)S(1)}, u32[]{:S(2)}, u32[]{:S(2)}) collective-permute-start(bf16[4,112,128]{2,1,0:T(8,128)(2,1)S(1)} %get-tuple-element.119), channel_id=1, source_target_pairs={{0,16},{4,20},{8,24},{12,28},{16,0},{20,4},{24,8},{28,12},{1,17},{... | collective-permute-start | bytes 344072 | tf_op jit(solution)/shard_map/ppermute | solution.py:477
  90.1 6.9 %collective-permute-start.14 = (bf16[4,112,128]{2,1,0:T(8,128)(2,1)S(1)}, bf16[4,112,128]{2,1,0:T(8,128)(2,1)S(1)}, u32[]{:S(2)}, u32[]{:S(2)}) collective-permute-start(bf16[4,112,128]{2,1,0:T(8,128)(2,1)S(1)} %get-tuple-element.118), channel_id=1, source_target_pairs={{0,24},{4,28},{8,16},{12,20},{16,8},{20,12},{24,0},{28,4},{1,25},{... | collective-permute-start | bytes 344072 | tf_op jit(solution)/shard_map/ppermute | solution.py:477
  97.1 22.2 %copy-start.3 = (bf16[32,32,128]{2,1,0:T(8,128)(2,1)S(1)}, bf16[32,32,128]{2,1,0:T(8,128)(2,1)}, u32[]{:S(2)}) copy-start(bf16[32,32,128]{2,1,0:T(8,128)(2,1)} %get-tuple-element.103) | copy-start | bytes 786436
  97.2 5.8 %collective-permute-start.17 = (f32[112,128]{1,0:T(8,128)S(1)}, f32[112,128]{1,0:T(8,128)S(1)}, u32[]{:S(2)}, u32[]{:S(2)}) collective-permute-start(f32[112,128]{1,0:T(8,128)S(1)} %get-tuple-element.123), channel_id=1, source_target_pairs={{0,2},{1,3},{2,0},{3,1},{4,6},{5,7},{6,4},{7,5},{8,10},{9,11},{10,... | collective-permute-start | bytes 172040 | tf_op jit(solution)/shard_map/ppermute | solution.py:336
  99.6 7.1 %collective-permute-start.20 = (f32[112,128]{1,0:T(8,128)S(1)}, f32[112,128]{1,0:T(8,128)S(1)}, u32[]{:S(2)}, u32[]{:S(2)}) collective-permute-start(f32[112,128]{1,0:T(8,128)S(1)} %get-tuple-element.122), channel_id=1, source_target_pairs={{0,3},{1,0},{2,1},{3,2},{4,7},{5,4},{6,5},{7,6},{8,11},{9,8},{10,9... | collective-permute-start | bytes 172040 | tf_op jit(solution)/shard_map/ppermute | solution.py:336
  100.2 6.5 %collective-permute-start.19 = (f32[112,128]{1,0:T(8,128)S(1)}, f32[112,128]{1,0:T(8,128)S(1)}, u32[]{:S(2)}, u32[]{:S(2)}) collective-permute-start(f32[112,128]{1,0:T(8,128)S(1)} %get-tuple-element.121), channel_id=1, source_target_pairs={{0,1},{1,2},{2,3},{3,0},{4,5},{5,6},{6,7},{7,4},{8,9},{9,10},{10,1... | collective-permute-start | bytes 172040 | tf_op jit(solution)/shard_map/ppermute | solution.py:336
  103.0 14.5 %collective-permute-start.18 = (bf16[32,32,128]{2,1,0:T(8,128)(2,1)}, bf16[32,32,128]{2,1,0:T(8,128)(2,1)S(1)}, u32[]{:S(2)}, u32[]{:S(2)}) collective-permute-start(bf16[32,32,128]{2,1,0:T(8,128)(2,1)} %get-tuple-element.98), channel_id=1, source_target_pairs={{0,3},{1,0},{2,1},{3,2},{4,7},{5,4},{6,5},{7,6},{8,11},{9,8},{10,9... | collective-permute-start | bytes 786440 | tf_op jit(solution)/shard_map/ppermute | solution.py:336
  106.8 12.4 %collective-permute-start.21 = (bf16[16,32,128]{2,1,0:T(8,128)(2,1)}, bf16[16,32,128]{2,1,0:T(8,128)(2,1)S(1)}, u32[]{:S(2)}, u32[]{:S(2)}) collective-permute-start(bf16[16,32,128]{2,1,0:T(8,128)(2,1)} %get-tuple-element.100), channel_id=1, source_target_pairs={{0,2},{1,3},{2,0},{3,1},{4,6},{5,7},{6,4},{7,5},{8,10},{9,11},{10,... | collective-permute-start | bytes 393224 | tf_op jit(solution)/shard_map/ppermute | solution.py:336
  106.8 12.3 %collective-permute-start.22 = (bf16[16,32,128]{2,1,0:T(8,128)(2,1)}, bf16[16,32,128]{2,1,0:T(8,128)(2,1)S(1)}, u32[]{:S(2)}, u32[]{:S(2)}) collective-permute-start(bf16[16,32,128]{2,1,0:T(8,128)(2,1)} %get-tuple-element.102), channel_id=1, source_target_pairs={{0,1},{1,2},{2,3},{3,0},{4,5},{5,6},{6,7},{7,4},{8,9},{9,10},{10,1... | collective-permute-start | bytes 393224 | tf_op jit(solution)/shard_map/ppermute | solution.py:336
